TPU v7x, 256 devices: a whole 4x4x8 slice. The times are simulated.
256 devices in a mesh: tile: 128 (over z, y, x_hi, core), chan: 2 (over x_lo).
Axes of the slice: x: 4 (x_hi: 2, x_lo: 2; x = x_hi * 2 + x_lo), y: 4, z: 8, core: 2. Of those that a mesh axis runs over, the one named last changes fastest.
Arguments:
- activation: float32 [64, 128, 4, 4, 128], P('chan', 'tile'), may hold values from -6 to 6
- out_grad: float32 [64, 128, 4, 4, 128], P('chan', 'tile'), may hold values from -6 to 6
- kernel: float32 [27, 64, 64], P(None, 'chan'), may hold values from -0.15625 to 0.15625
Outputs:
- input_grad: float32 [64, 128, 4, 4, 128], P('chan', 'tile')
- kernel_grad: float32 [27, 64, 64], P(None, 'chan')
All inputs are finite; a program needn't handle non-finite values.
Results may differ from a plain program's by a relative error of at most 0.0003.
Values sent between devices are 32-bit elements; how exact they have to be, the bound alone decides.
No kernel may reach another device: no remote copies, remote signals or barrier semaphores. Data moves between devices by JAX's collectives and lax.ppermute only.
A program may use at most 128 MiB of HBM per device.

v0:
```python
import math

import jax
import jax.numpy as jnp
from jax import lax
from jax.sharding import PartitionSpec as P

TY = 4


def passed_along(value, axis, steps):
    count = lax.axis_size(axis)
    leading, last = (max(0, -steps), min(count, count - steps))
    return lax.ppermute(value, axis, [(source, source + steps) for source in range(leading, last)])


def rim_cells(field):
    column = lax.axis_index("tile") % TY
    below = passed_along(field[:, -1:], "tile", TY)
    above = passed_along(field[:, :1], "tile", -TY)
    extended = jnp.concatenate([below, field, above], axis=1)
    left_keep = jnp.where(column > 0, 1.0, 0.0).astype(jnp.float32)
    right_keep = jnp.where(column < TY - 1, 1.0, 0.0).astype(jnp.float32)
    left_side = passed_along(extended[..., -1:], "tile", 1) * left_keep
    right_side = passed_along(extended[..., :1], "tile", -1) * right_keep
    widened = jnp.concatenate([left_side, extended, right_side], axis=3)
    return jnp.pad(widened, ((0, 0), (0, 0), (1, 1), (0, 0)))


def window(padded, start_x, start_z, start_y, row_count, depth, width):
    piece = padded[
        :, start_x : start_x + row_count, start_z : start_z + depth, start_y : start_y + width
    ]
    return piece.reshape(piece.shape[0], -1)


def filter_terms(grad_flat, act_padded, row_count, depth, width):
    result = []
    for shift_x in range(3):
        for shift_z in range(3):
            for shift_y in range(3):
                act_piece = window(act_padded, shift_x, shift_z, shift_y, row_count, depth, width)
                result.append(
                    lax.dot_general(
                        grad_flat,
                        act_piece,
                        (((1,), (1,)), ((), ())),
                        precision=lax.Precision.HIGHEST,
                        preferred_element_type=jnp.float32,
                    )
                )
    return jnp.stack(result)


def data_terms(weights, grad_padded, row_count, depth, width):
    total = jnp.zeros((weights.shape[2], row_count * depth * width), jnp.float32)
    for shift_x in range(3):
        for shift_z in range(3):
            for shift_y in range(3):
                index_tap = 9 * shift_x + 3 * shift_z + shift_y
                grad_piece = window(
                    grad_padded, 2 - shift_x, 2 - shift_z, 2 - shift_y, row_count, depth, width
                )
                total = total + lax.dot_general(
                    weights[index_tap],
                    grad_piece,
                    (((0,), (0,)), ((), ())),
                    precision=lax.Precision.HIGHEST,
                    preferred_element_type=jnp.float32,
                )
    return total


def body(activation, out_grad, kernel):
    act_local = activation[:, 0]
    grad_local = out_grad[:, 0]
    row_count, depth, width = (act_local.shape[1], act_local.shape[2], act_local.shape[3])
    cin_local = act_local.shape[0]
    voxels = row_count * lax.axis_size("tile") * depth * width
    act_full = lax.all_gather(act_local, "chan", axis=0, tiled=True)
    act_padded = rim_cells(act_full)
    grad_flat = grad_local.reshape(grad_local.shape[0], -1)
    local_filter = filter_terms(grad_flat, act_padded, row_count, depth, width) * (
        1.0 / math.sqrt(voxels)
    )
    kernel_grad = lax.psum(local_filter, "tile")
    grad_padded = rim_cells(grad_local)
    input_flat = lax.psum_scatter(
        data_terms(kernel, grad_padded, row_count, depth, width),
        "chan",
        scatter_dimension=0,
        tiled=True,
    )
    input_grad = input_flat.reshape(cin_local, 1, row_count, depth, width)
    return (input_grad, kernel_grad)


def solution(mesh):
    in_specs = (
        P("chan", "tile", None, None, None),
        P("chan", "tile", None, None, None),
        P(None, "chan", None),
    )
    out_specs = (P("chan", "tile", None, None, None), P(None, "chan", None))
    return jax.shard_map(body, mesh=mesh, in_specs=in_specs, out_specs=out_specs, check_vma=False)
```

profile of v0, /device:TPU:1, one launch (start us, length us, event | category | flops | bytes accessed | tf_op | source)
XLA Modules:
  0.0 1393.2 jit_solution(16760934835487114839)
XLA Ops:
  9.0 4.0 collective-permute-start
  14.3 7.7 all-gather
  22.8 3.7 collective-permute-start.4
  29.3 4.3 collective-permute-start.3
  33.6 4.6 collective-permute-start.2
  39.2 2.8 collective-permute-done.3
  43.1 4.0 collective-permute-done.2
  49.0 3.6 fusion.103
  71.5 1.8 reshape.180
  78.6 2.4 convolution_bitcast_fusion.10
  82.7 2.4 convolution_bitcast_fusion.11
  86.8 2.4 convolution_bitcast_fusion.6
  91.0 2.4 convolution_bitcast_fusion.7
  93.3 1.8 reshape.188
  95.1 2.4 convolution_bitcast_fusion.8
  99.2 2.4 convolution_bitcast_fusion.9
  103.3 2.4 convolution_bitcast_fusion.12
  107.5 2.4 convolution_bitcast_fusion.5
  114.1 1.8 convolution_add_fusion.11
  129.8 1.9 collective-permute-start.7
  132.0 6.0 collective-permute-start.6
  141.2 2.1 select_maximum_fusion
  143.3 5.8 fusion.100
  149.1 2.1 reshape.198
  151.2 2.2 fusion.43
  153.4 2.1 reshape.199
  155.5 2.1 reshape.200
  157.5 1.8 pad_maximum_fusion
  159.4 2.0 fusion.101
  209.3 1.8 reshape.197
  211.1 1172.4 %all-reduce.4.cloned.1.call-done = f32[27,32,64]{2,1,0:T(8,128)} async-done(((f32[27,32,64]{2,1,0:T(8,128)}), f32[27,32,64]{2,1,0:T(8,128)}) %all-reduce.4.cloned.1.call-update) | async-done | bytes 221200 | tf_op jit(solution)/shard_map/psum | solution.py:86
  1383.5 1.8 copy.38
  (254 shorter events, 113.2 us)
Async XLA Ops:
  8.0 19.8 %copy-start = (f32[32,1,4,4,128]{4,3,2,1,0:T(4,128)S(1)}, f32[32,1,4,4,128]{4,3,2,1,0:T(4,128)}, u32[]{:S(2)}) copy-start(f32[32,1,4,4,128]{4,3,2,1,0:T(4,128)} %param.4) | copy-start | bytes 786436
  8.0 201.3 %reduce-scatter.2.cloned.1.call-start = ((), (), s32[]{:S(2)}) async-start(), calls=%async_computation.1 | async-start | bytes 786432 | tf_op jit(solution)/shard_map/reduce_scatter | solution.py:88
  9.0 19.9 %collective-permute-start = (f32[32,1,4,128]{3,2,1,0:T(4,128)S(1)}, f32[32,1,4,128]{3,2,1,0:T(4,128)S(1)}, u32[]{:S(2)}, u32[]{:S(2)}) collective-permute-start(f32[32,1,4,128]{3,2,1,0:T(4,128)S(1)} %get-tuple-element.68), channel_id=1, source_target_pairs={{0,8},{2,10},{4,12},{6,14},{8,16},{10,18},{12,20},{14,22},{16,24},... | collective-permute-start | bytes 196616 | tf_op jit(solution)/shard_map/ppermute | solution.py:14
  13.0 15.9 %collective-permute-start.1 = (f32[32,1,4,128]{3,2,1,0:T(4,128)S(1)}, f32[32,1,4,128]{3,2,1,0:T(4,128)S(1)}, u32[]{:S(2)}, u32[]{:S(2)}) collective-permute-start(f32[32,1,4,128]{3,2,1,0:T(4,128)S(1)} %get-tuple-element.69), channel_id=1, source_target_pairs={{8,0},{10,2},{12,4},{14,6},{16,8},{18,10},{20,12},{22,14},{24,16},... | collective-permute-start | bytes 196616 | tf_op jit(solution)/shard_map/ppermute | solution.py:14
  22.8 106.0 %collective-permute-start.4 = (f32[64,1,4,128]{3,2,1,0:T(4,128)}, f32[64,1,4,128]{3,2,1,0:T(4,128)S(1)}, u32[]{:S(2)}, u32[]{:S(2)}) collective-permute-start(f32[64,1,4,128]{3,2,1,0:T(4,128)} %get-tuple-element.60), channel_id=1, source_target_pairs={{0,8},{2,10},{4,12},{6,14},{8,16},{10,18},{12,20},{14,22},{16,24},... | collective-permute-start | bytes 393224 | tf_op jit(solution)/shard_map/ppermute | solution.py:14
  26.5 102.3 %collective-permute-start.5 = (f32[64,1,4,128]{3,2,1,0:T(4,128)S(1)}, f32[64,1,4,128]{3,2,1,0:T(4,128)S(1)}, u32[]{:S(2)}, u32[]{:S(2)}) collective-permute-start(f32[64,1,4,128]{3,2,1,0:T(4,128)S(1)} %get-tuple-element.61), channel_id=1, source_target_pairs={{8,0},{10,2},{12,4},{14,6},{16,8},{18,10},{20,12},{22,14},{24,16},... | collective-permute-start | bytes 393224 | tf_op jit(solution)/shard_map/ppermute | solution.py:14
  29.3 12.8 collective-permute-start.3
  33.6 13.5 collective-permute-start.2
  128.7 1254.8 %all-reduce.4.cloned.1.call-start = ((), (), s32[]{:S(2)}) async-start(), calls=%async_computation.2 | async-start | bytes 884736 | tf_op jit(solution)/shard_map/psum | solution.py:86
  129.8 10.5 collective-permute-start.7
  132.0 8.7 collective-permute-start.6
  178.9 3.7 copy-start.20
  179.1 4.6 copy-start.38
  180.3 4.6 copy-start.37
  181.4 4.6 copy-start.36
  182.6 4.6 copy-start.35
  183.7 4.6 copy-start.34
  184.9 4.6 copy-start.33
  186.0 4.6 copy-start.32
  187.2 4.6 copy-start.31
  188.3 4.6 copy-start.18
  189.5 4.6 copy-start.30
  190.6 4.6 copy-start.29
  191.8 4.6 copy-start.28
  192.9 4.9 copy-start.25
  194.1 4.8 copy-start.24
  195.2 4.8 copy-start.23
  196.4 4.8 copy-start.22
  197.8 4.6 copy-start.21
  198.9 4.6 copy-start.19
  201.2 4.6 copy-start.2
  202.4 3.7 copy-start.1
  (42 other events, 92.4 us)
Sparse Core Ops, SparseCore 0:
  128.8 26.9 reduce-scatter.1
Sparse Core Ops, SparseCore 1:
  209.3 1174.1 all-reduce.3
where the time goes:
time: 1400 us; the launch traced here: 1390 us
  waiting for transfers between devices  1180 us (84%)
  local copies, waits for them, and re-layouts  87.5 us (6%)
  matrix products  65.8 us (5%)
  starting transfers between devices  27.2 us (2%)
  between operations  16.7 us (1%)
    psum x1, waiting for transfers between devices, body(): kernel_grad = lax.psum(local_filter, 'tile')  1170 us
    reshape x54, local copies, waits for them, and re-layouts, window(): return piece.reshape(piece.shape[0], -1)  66.1 us
    dot_general x27, matrix products, data_terms(): lax.dot_general(weights[index_tap], grad_piece, (((0,), (0,)), ((), ())),...  35.4 us
    dot_general x27, matrix products, filter_terms(): lax.dot_general(grad_flat, act_piece, (((1,), (1,)), ((), ())), precision...  30.4 us
  transfers between devices with their start and end apart: 10, of which 3 were waited for; matrix products, arithmetic and copies ran while one was open for 11% of the time, Pallas kernels for 0%

commit v1 on v0

v1 whole, which is shorter than its diff:
```python
import jax
import jax.numpy as jnp
from jax import lax
from jax.experimental import pallas as pl
from jax.experimental.pallas import tpu as pltpu
from jax.sharding import Mesh, PartitionSpec as P

F32, BF16 = jnp.float32, jnp.bfloat16
ALONG_X = ("z", "y")
ALONG_Y = ("xh", "c")
TILE = ALONG_X + ALONG_Y
NEAR = ("y", "xh", "c")
FAR = "z"
CI = 32
NT = (((1,), (1,)), ((), ()))


def passed_along(value, axis, steps):
    count = lax.axis_size(axis)
    first, last = max(0, -steps), min(count, count - steps)
    return lax.ppermute(value, axis, [(s, s + steps) for s in range(first, last)])


def traded(value):
    return lax.ppermute(value, "chan", [(0, 1), (1, 0)])


def split(value):
    high = value.astype(BF16)
    return high, (value - high.astype(F32)).astype(BF16)


def edges_kernel(grad, first, last):
    lane = lax.broadcasted_iota(jnp.int32, (CI, 128), 1)
    heads = jnp.zeros((CI, 128), F32)
    tails = jnp.zeros((CI, 128), F32)
    for cell in range(16):
        tile = grad[pl.ds(cell, CI, stride=16), :]
        place = 4 + cell
        heads = jnp.where(lane == place, pltpu.roll(tile, place, 1), heads)
        tails = jnp.where(lane == place, pltpu.roll(tile, place + 1, 1), tails)
    first[...] = heads
    last[...] = tails


def rim(own, below, above, at):
    lane = lax.broadcasted_iota(jnp.int32, (CI, 128), 1)
    low = pltpu.roll(below, (128 - 16 - at) % 128, 1)
    high = pltpu.roll(above, (16 - at) % 128, 1)
    return jnp.where(lane < 4, low, jnp.where(lane >= 20, high, own))


def spread(grad, below, above, left, right, high, low):
    lane = lax.broadcasted_iota(jnp.int32, (CI, 128), 1)
    zero = jnp.zeros((CI, 128), BF16)
    for xp in range(6):
        for d in range(3):
            for ref in (high, low):
                ref[d, xp, :, 0:128] = zero
                ref[d, xp, :, 640:768] = zero
        for z in range(4):
            if xp == 0:
                tile = below[pl.ds(z, CI, stride=4), :]
            elif xp == 5:
                tile = above[pl.ds(z, CI, stride=4), :]
            else:
                tile = grad[pl.ds((xp - 1) * 4 + z, CI, stride=16), :]
            at = xp * 4 + z
            before = jnp.where(
                lane == 0, pltpu.roll(left, (128 - at) % 128, 1), pltpu.roll(tile, 1, 1)
            )
            after = jnp.where(
                lane == 127, pltpu.roll(right, 127 - at, 1), pltpu.roll(tile, 127, 1)
            )
            for d, value in ((0, after), (1, tile), (2, before)):
                high[d, xp, :, (z + 1) * 128 : (z + 2) * 128], low[
                    d, xp, :, (z + 1) * 128 : (z + 2) * 128
                ] = split(value)


def taps(ref, x):
    return jnp.concatenate(
        [
            ref[d, x + 2 - a, :, (2 - b) * 128 : (2 - b) * 128 + 512]
            for a in range(3)
            for b in range(3)
            for d in range(3)
        ],
        axis=0,
    )


def x_row(ref, x):
    return jnp.concatenate([ref[pl.ds(x * 4 + z, CI, stride=16), :] for z in range(4)], axis=1)


def filter_kernel(
    chan, own, other, grad, below, above, left, right, rims_below, rims_above, out, high, low
):
    spread(
        grad,
        below,
        above,
        rim(left[...], rims_below[...], rims_above[...], 0),
        rim(right[...], rims_below[...], rims_above[...], 64),
        high,
        low,
    )
    is_first = chan[0] == 0
    total = None
    for x in range(4):
        mine, theirs = x_row(own, x), x_row(other, x)
        act = jnp.concatenate(
            [jnp.where(is_first, mine, theirs), jnp.where(is_first, theirs, mine)], axis=0
        )
        act_high, act_low = split(act)
        both = jnp.concatenate([act_high, act_low], axis=0)
        p = lax.dot_general(taps(high, x), both, NT, preferred_element_type=F32)
        q = lax.dot_general(taps(low, x), act_high, NT, preferred_element_type=F32)
        part = p[:, :64] + p[:, 64:] + q
        total = part if total is None else total + part
    total = total * (1.0 / 512.0)
    for j in range(16):
        if j < 13:
            pair = [total[64 * j : 64 * j + 32], total[64 * j + 32 : 64 * j + 64]]
        elif j == 13:
            pair = [total[64 * j : 64 * j + 32], jnp.zeros((32, 64), F32)]
        else:
            pair = [jnp.zeros((32, 64), F32)] * 2
        out[32 * j : 32 * j + 32, :] = jnp.concatenate(pair, axis=1)


def data_kernel(chan, weights, high, low, kept, sent):
    w = weights[...].reshape(864, 64)
    w = jnp.where(chan[0] == 0, w, jnp.concatenate([w[:, 32:], w[:, :32]], axis=1))
    w_high = w.astype(BF16).astype(F32)
    both = jnp.concatenate([w_high, w - w_high], axis=1)
    both = jnp.concatenate([both, jnp.zeros((32, 128), F32)], axis=0)
    both = both.T.astype(BF16)[:, :864]
    for x in range(4):
        p = jnp.dot(both, taps(high, x), preferred_element_type=F32)
        q = jnp.dot(both[:64], taps(low, x), preferred_element_type=F32)
        result = p[:64] + p[64:] + q
        for z in range(4):
            tile = result[:, z * 128 : (z + 1) * 128]
            kept[pl.ds(x * 4 + z, CI, stride=16), :] = tile[:32]
            sent[pl.ds(x * 4 + z, CI, stride=16), :] = tile[32:]


def sum_kernel(copies, pieces, out):
    def run(values, result):
        total = values[0:32, :]
        for j in range(1, pieces):
            total = total + values[32 * j : 32 * j + 32, :]
        for j in range(copies):
            result[32 * j : 32 * j + 32, :] = total

    return run


def unpack_kernel(packed, out):
    for tap in range(27):
        half = 64 * (tap % 2)
        out[tap, :, :] = packed[32 * (tap // 2) : 32 * (tap // 2) + 32, half : half + 64]


VMEM = pl.BlockSpec(memory_space=pltpu.VMEM)
SMEM = pl.BlockSpec(memory_space=pltpu.SMEM)
PARAMS = pltpu.CompilerParams(vmem_limit_bytes=40 * 2**20)


def shape(*dims, dtype=F32):
    return jax.ShapeDtypeStruct(dims, dtype)


def call(kernel, outs, in_specs, flops=0, moved=0):
    return pl.pallas_call(
        kernel,
        out_shape=outs,
        in_specs=in_specs,
        out_specs=jax.tree.map(lambda _: VMEM, outs),
        compiler_params=PARAMS,
        cost_estimate=pl.CostEstimate(flops=flops, bytes_accessed=moved, transcendentals=0),
    )


def summed(values, copies):
    rows = values.shape[0]
    return call(sum_kernel(copies, rows // 32, None), shape(32 * copies, 128), [VMEM])(values)


def summed_over_tiles(partial):
    near, far = lax.axis_size(NEAR), lax.axis_size(FAR)
    pieces = lax.all_to_all(partial, NEAR, 0, 0, tiled=True)
    copies = lax.all_to_all(summed(pieces, far), FAR, 0, 0, tiled=True)
    return lax.all_to_all(summed(copies, near), NEAR, 0, 0, tiled=True)


def body(activation, out_grad, kernel):
    act = activation.reshape(512, 128)
    grad = out_grad.reshape(512, 128)
    chan = lax.axis_index("chan").astype(jnp.int32).reshape(1)
    other = traded(act)
    first, last = call(edges_kernel, (shape(CI, 128),) * 2, [VMEM])(grad)
    left = passed_along(last, ALONG_Y, 1)
    right = passed_along(first, ALONG_Y, -1)
    rows = grad.reshape(CI, 4, 4, 128)
    below = passed_along(rows[:, 3], ALONG_X, 1).reshape(128, 128)
    above = passed_along(rows[:, 0], ALONG_X, -1).reshape(128, 128)
    rims = jnp.concatenate([left[:, :64], right[:, :64]], axis=1)
    rims_below = passed_along(rims, ALONG_X, 1)
    rims_above = passed_along(rims, ALONG_X, -1)
    halves = shape(3, 6, CI, 768, dtype=BF16)
    partial, high, low = call(
        filter_kernel, (shape(512, 128), halves, halves), [SMEM] + [VMEM] * 9, 700_000_000, 1 << 22
    )(chan, act, other, grad, below, above, left, right, rims_below, rims_above)
    kept, sent = call(
        data_kernel, (shape(512, 128),) * 2, [SMEM] + [VMEM] * 3, 700_000_000, 1 << 22
    )(chan, kernel, high, low)
    input_grad = (kept + traded(sent)).reshape(activation.shape)
    packed = summed_over_tiles(partial)
    kernel_grad = call(unpack_kernel, shape(27, 32, 64), [VMEM])(packed)
    return (input_grad, kernel_grad)


def solution(mesh):
    mesh = Mesh(mesh.devices.reshape(8, 4, 2, 2, 2), TILE + ("chan",))
    field = P("chan", TILE, None, None, None)
    weights = P(None, "chan", None)
    return jax.shard_map(
        body,
        mesh=mesh,
        in_specs=(field, field, weights),
        out_specs=(field, weights),
        check_vma=False,
    )
```

time: 1400 us -> 82.9 us (0.06)
  waiting for transfers between devices: 1180 us -> 15 us
  local copies, waits for them, and re-layouts: 87.5 us -> 0.98 us
  matrix products: 65.8 us -> 0 us
  between operations: 16.7 us -> 0.77 us
  blocking collectives: 7.74 us -> 22.6 us
    psum x1 -> x0, waiting for transfers between devices: 1170 us -> none  [body(): kernel_grad = lax.psum(local_filter, 'tile')]
    reshape x55 -> x0, local copies, waits for them, and re-layouts: 67.9 us -> none  [the longest x54 66.1 us: window(): return piece.reshape(piece.shape[0], -1)]
    dot_general x54 -> x0, matrix products: 65.8 us -> none  [the longest x27 35.4 us: data_terms(): lax.dot_general(weights[index_tap], grad_piece, (((0,), (0,)), ((), ())),...]
    all_to_all x0 -> x1, blocking collectives: none -> 22.6 us  [summed_over_tiles(): pieces = lax.all_to_all(partial, NEAR, 0, 0, tiled=True)]
    all_to_all x0 -> x2, starting transfers between devices: none -> 16.6 us  [the longest x1 11 us: summed_over_tiles(): copies = lax.all_to_all(summed(pieces, far), FAR, 0, 0, tiled=True)]
    slice x10 -> x0, local copies, waits for them, and re-layouts: 15.9 us -> none  [the longest x4 12.9 us: window(): padded[:, start_x:start_x + row_count, start_z:start_z + depth, start_y:s...]
    all_to_all x0 -> x2, waiting for transfers between devices: none -> 14.1 us  [the longest x1 7.99 us: summed_over_tiles(): return lax.all_to_all(summed(copies, near), NEAR, 0, 0, tiled=True)]
  transfers between devices with their start and end apart: 10 -> 10, of which waited for: 3 -> 3; matrix products, arithmetic and copies ran while one was open for 11% -> 1% of each run, Pallas kernels for 0% -> 3%
where the time goes in v1:
time: 82.9 us; the launch traced here: 82.4 us
  starting transfers between devices  35.6 us (43%)
  blocking collectives  22.6 us (27%)
  waiting for transfers between devices  15 us (18%)
  Pallas kernels  6.6 us (8%)
  local copies, waits for them, and re-layouts  0.98 us (1%)
    all_to_all x1, blocking collectives, summed_over_tiles(): pieces = lax.all_to_all(partial, NEAR, 0, 0, tiled=True)  22.6 us
    ppermute x6, starting transfers between devices, passed_along(): lax.ppermute(value, axis, [(s, s + steps) for s in range(first, last)])  18.5 us
    all_to_all x1, starting transfers between devices, summed_over_tiles(): copies = lax.all_to_all(summed(pieces, far), FAR, 0, 0, tiled=True)  11 us
    all_to_all x1, waiting for transfers between devices, summed_over_tiles(): return lax.all_to_all(summed(copies, near), NEAR, 0, 0, tiled=True)  7.99 us
    all_to_all x1, waiting for transfers between devices, summed_over_tiles(): copies = lax.all_to_all(summed(pieces, far), FAR, 0, 0, tiled=True)  6.1 us
    all_to_all x1, starting transfers between devices, summed_over_tiles(): return lax.all_to_all(summed(copies, near), NEAR, 0, 0, tiled=True)  5.63 us
    pallas_call x1, Pallas kernels, body(): call(filter_kernel, (shape(512, 128), halves, halves), [SMEM] + [VMEM] *...  2.27 us
    pallas_call x1, Pallas kernels, body(): call(data_kernel, (shape(512, 128),) * 2, [SMEM] + [VMEM] * 3, 700000000,...  1.82 us
  transfers between devices with their start and end apart: 10, of which 3 were waited for; matrix products, arithmetic and copies ran while one was open for 1% of the time, Pallas kernels for 3%

profile of v1, /device:TPU:1, one launch (start us, length us, event | category | flops | bytes accessed | tf_op | source)
XLA Modules:
  0.0 82.4 jit_solution(3296590725685350527)
XLA Ops:
  0.6 0.0 copy-start
  0.6 0.9 %copy-done = f32[32,1,4,4,128]{4,3,2,1,0:T(4,128)S(1)} copy-done((f32[32,1,4,4,128]{4,3,2,1,0:T(4,128)S(1)}, f32[32,1,4,4,128]{4,3,2,1,0:T(4,128)}, u32[]{:S(2)}) %copy-start) | copy-done | bytes 262168
  1.6 0.2 shard_map.50
  1.8 6.0 %collective-permute-start.3 = (f32[32,128]{1,0:T(8,128)S(1)}, f32[32,128]{1,0:T(8,128)S(1)}, u32[]{:S(2)}, u32[]{:S(2)}) collective-permute-start(f32[32,128]{1,0:T(8,128)S(1)} %get-tuple-element.9), channel_id=1, source_target_pairs={{0,2},{2,4},{4,6},{1,3},{3,5},{5,7},{8,10},{10,12},{12,14},{9,11},... | collective-permute-start | bytes 49160 | tf_op jit(solution)/shard_map/ppermute | solution.py:21
  7.8 1.9 %collective-permute-start.4 = (f32[32,128]{1,0:T(8,128)S(1)}, f32[32,128]{1,0:T(8,128)S(1)}, u32[]{:S(2)}, u32[]{:S(2)}) collective-permute-start(f32[32,128]{1,0:T(8,128)S(1)} %get-tuple-element.10), channel_id=1, source_target_pairs={{2,0},{4,2},{6,4},{3,1},{5,3},{7,5},{10,8},{12,10},{14,12},{11,9},... | collective-permute-start | bytes 49160 | tf_op jit(solution)/shard_map/ppermute | solution.py:21
  9.8 0.4 collective-permute-start
  10.2 1.3 %collective-permute-start.2 = (f32[32,4,128]{2,1,0:T(4,128)S(1)}, f32[32,4,128]{2,1,0:T(4,128)S(1)}, u32[]{:S(2)}, u32[]{:S(2)}) collective-permute-start(f32[32,4,128]{2,1,0:T(4,128)S(1)} %get-tuple-element.18), channel_id=1, source_target_pairs={{8,0},{16,8},{24,16},{32,24},{40,32},{48,40},{56,48},{64,56},{72,6... | collective-permute-start | bytes 196616 | tf_op jit(solution)/shard_map/ppermute | solution.py:21
  11.5 4.0 %collective-permute-start.1 = (f32[32,4,128]{2,1,0:T(4,128)S(1)}, f32[32,4,128]{2,1,0:T(4,128)S(1)}, u32[]{:S(2)}, u32[]{:S(2)}) collective-permute-start(f32[32,4,128]{2,1,0:T(4,128)S(1)} %get-tuple-element.19), channel_id=1, source_target_pairs={{0,8},{8,16},{16,24},{24,32},{32,40},{40,48},{48,56},{56,64},{64,7... | collective-permute-start | bytes 196616 | tf_op jit(solution)/shard_map/ppermute | solution.py:21
  15.5 0.0 collective-permute-done.3.left
  15.5 0.0 collective-permute-done.4.right
  15.5 0.1 pad_maximum_fusion
  15.6 1.3 %collective-permute-start.6 = (f32[32,128]{1,0:T(8,128)S(1)}, f32[32,128]{1,0:T(8,128)S(1)}, u32[]{:S(2)}, u32[]{:S(2)}) collective-permute-start(f32[32,128]{1,0:T(8,128)S(1)} %pad_maximum_fusion), channel_id=1, source_target_pairs={{8,0},{16,8},{24,16},{32,24},{40,32},{48,40},{56,48},{64,56},{72,6... | collective-permute-start | bytes 49160 | tf_op jit(solution)/shard_map/ppermute | solution.py:21
  16.9 4.0 %collective-permute-start.5 = (f32[32,128]{1,0:T(8,128)S(1)}, f32[32,128]{1,0:T(8,128)S(1)}, u32[]{:S(2)}, u32[]{:S(2)}) collective-permute-start(f32[32,128]{1,0:T(8,128)S(1)} %pad_maximum_fusion), channel_id=1, source_target_pairs={{0,8},{8,16},{16,24},{24,32},{32,40},{40,48},{48,56},{56,64},{64,7... | collective-permute-start | bytes 49160 | tf_op jit(solution)/shard_map/ppermute | solution.py:21
  20.9 0.0 collective-permute-done.6.rims_above
  20.9 0.8 %collective-permute-done.5.rims_below = f32[32,128]{1,0:T(8,128)S(1)} collective-permute-done((f32[32,128]{1,0:T(8,128)S(1)}, f32[32,128]{1,0:T(8,128)S(1)}, u32[]{:S(2)}, u32[]{:S(2)}) %collective-permute-start.5) | collective-permute-done | bytes 16416 | tf_op jit(solution)/shard_map/ppermute | solution.py:21
  21.7 0.0 collective-permute-done.2
  21.7 0.0 collective-permute-done.1
  21.7 0.0 collective-permute-done.other
  21.7 0.0 copy-done.1
  21.8 2.3 %shard_map.51 = (f32[512,128]{1,0:T(8,128)S(1)}, bf16[3,6,32,768]{3,2,1,0:T(8,128)(2,1)S(1)}, bf16[3,6,32,768]{3,2,1,0:T(8,128)(2,1)S(1)}) custom-call(s32[1]{0:T(128)} %bitcast.chan, f32[512,128]{1,0:T(8,128)S(1)} %bitcast.31, f32[512,128]{1,0:T(8,128)S(1)} %collective-permute-done.other, f32[512,128]{1,0:T(8,128)S(1)} %bitcast.25, ...), custom_call_target="tpu_custom_call" | custom-call | flops 700000000 | bytes 4194304 | tf_op jit(solution)/shard_map/pallas_call | solution.py:214
  24.0 22.6 %all_to_all.33 = f32[16,32,128]{2,1,0:T(8,128)S(1)} all-to-all(f32[16,32,128]{2,1,0:T(8,128)S(1)} %bitcast.27), channel_id=1, replica_groups=mesh['z'=8,'y'=4,'xh'=2,'c'=2,'chan'=2] {'y','xh','c'}, dimensions={0} | all-to-all | bytes 524288 | tf_op jit(solution)/shard_map/all_to_all | solution.py:194
  46.7 0.7 shard_map.53
  47.4 11.0 %all-to-all-start.1 = ((f32[8,32,128]{2,1,0:T(8,128)}), f32[8,32,128]{2,1,0:T(8,128)S(1)}, u32[]{:S(2)}, u32[]{:S(2)}) async-start(f32[8,32,128]{2,1,0:T(8,128)} %bitcast.12), calls=%async_computation.1 | async-start | bytes 262144 | tf_op jit(solution)/shard_map/all_to_all | solution.py:195
  58.3 1.8 %shard_map.52 = (f32[512,128]{1,0:T(8,128)S(1)}, f32[512,128]{1,0:T(8,128)S(1)}) custom-call(s32[1]{0:T(128)} %bitcast.chan, f32[27,32,64]{2,1,0:T(8,128)S(1)} %copy-done.2, bf16[3,6,32,768]{3,2,1,0:T(8,128)(2,1)S(1)} %get-tuple-element.11.high, bf16[3,6,32,768]{3,2,1,0:T(8,128)(2,1)S(1)} %get-tuple-element.12.low), custom_call_target="tpu_custom_call" | custom-call | flops 700000000 | bytes 4194304 | tf_op jit(solution)/shard_map/pallas_call | solution.py:217
  60.2 0.1 collective-permute-start.7
  60.3 6.1 %all-to-all-done.1 = f32[8,32,128]{2,1,0:T(8,128)S(1)} async-done(((f32[8,32,128]{2,1,0:T(8,128)}), f32[8,32,128]{2,1,0:T(8,128)S(1)}, u32[]{:S(2)}, u32[]{:S(2)}) %all-to-all-start.1) | async-done | bytes 131104 | tf_op jit(solution)/shard_map/all_to_all | solution.py:195
  66.4 0.7 shard_map.54
  67.1 5.6 %all-to-all-start.2 = ((f32[16,32,128]{2,1,0:T(8,128)}), f32[16,32,128]{2,1,0:T(8,128)S(1)}, u32[]{:S(2)}, u32[]{:S(2)}) async-start(f32[16,32,128]{2,1,0:T(8,128)} %bitcast.14), calls=%async_computation.2 | async-start | bytes 524288 | tf_op jit(solution)/shard_map/all_to_all | solution.py:196
  72.7 0.0 collective-permute-done.7
  72.7 0.7 add.3
  73.5 8.0 %all-to-all-done.2 = f32[16,32,128]{2,1,0:T(8,128)S(1)} async-done(((f32[16,32,128]{2,1,0:T(8,128)}), f32[16,32,128]{2,1,0:T(8,128)S(1)}, u32[]{:S(2)}, u32[]{:S(2)}) %all-to-all-start.2) | async-done | bytes 262176 | tf_op jit(solution)/shard_map/all_to_all | solution.py:196
  81.5 0.9 %shard_map.55 = f32[27,32,64]{2,1,0:T(8,128)} custom-call(f32[512,128]{1,0:T(8,128)S(1)} %bitcast.22), custom_call_target="tpu_custom_call" | custom-call | tf_op jit(solution)/shard_map/pallas_call | solution.py:222
  (6 shorter events, 0.0 us)
Async XLA Ops:
  0.6 1.0 %copy-start = (f32[32,1,4,4,128]{4,3,2,1,0:T(4,128)S(1)}, f32[32,1,4,4,128]{4,3,2,1,0:T(4,128)}, u32[]{:S(2)}) copy-start(f32[32,1,4,4,128]{4,3,2,1,0:T(4,128)} %param.4) | copy-start | bytes 786436
  1.6 20.2 %copy-start.1 = (f32[32,1,4,4,128]{4,3,2,1,0:T(4,128)S(1)}, f32[32,1,4,4,128]{4,3,2,1,0:T(4,128)}, u32[]{:S(2)}) copy-start(f32[32,1,4,4,128]{4,3,2,1,0:T(4,128)} %param.4) | copy-start | bytes 786436
  1.6 20.2 %copy-start.3 = (f32[32,1,4,4,128]{4,3,2,1,0:T(4,128)S(1)}, f32[32,1,4,4,128]{4,3,2,1,0:T(4,128)}, u32[]{:S(2)}) copy-start(f32[32,1,4,4,128]{4,3,2,1,0:T(4,128)} %param.3) | copy-start | bytes 786436
  1.8 13.7 %collective-permute-start.3 = (f32[32,128]{1,0:T(8,128)S(1)}, f32[32,128]{1,0:T(8,128)S(1)}, u32[]{:S(2)}, u32[]{:S(2)}) collective-permute-start(f32[32,128]{1,0:T(8,128)S(1)} %get-tuple-element.9), channel_id=1, source_target_pairs={{0,2},{2,4},{4,6},{1,3},{3,5},{5,7},{8,10},{10,12},{12,14},{9,11},... | collective-permute-start | bytes 49160 | tf_op jit(solution)/shard_map/ppermute | solution.py:21
  7.8 7.7 %collective-permute-start.4 = (f32[32,128]{1,0:T(8,128)S(1)}, f32[32,128]{1,0:T(8,128)S(1)}, u32[]{:S(2)}, u32[]{:S(2)}) collective-permute-start(f32[32,128]{1,0:T(8,128)S(1)} %get-tuple-element.10), channel_id=1, source_target_pairs={{2,0},{4,2},{6,4},{3,1},{5,3},{7,5},{10,8},{12,10},{14,12},{11,9},... | collective-permute-start | bytes 49160 | tf_op jit(solution)/shard_map/ppermute | solution.py:21
  9.8 12.0 %collective-permute-start = (f32[512,128]{1,0:T(8,128)}, f32[512,128]{1,0:T(8,128)S(1)}, u32[]{:S(2)}, u32[]{:S(2)}) collective-permute-start(f32[512,128]{1,0:T(8,128)} %bitcast.30), channel_id=1, source_target_pairs={{0,1},{1,0},{2,3},{3,2},{4,5},{5,4},{6,7},{7,6},{8,9},{9,8},{10,11... | collective-permute-start | bytes 786440 | tf_op jit(solution)/shard_map/ppermute | solution.py:25
  10.2 11.5 %collective-permute-start.2 = (f32[32,4,128]{2,1,0:T(4,128)S(1)}, f32[32,4,128]{2,1,0:T(4,128)S(1)}, u32[]{:S(2)}, u32[]{:S(2)}) collective-permute-start(f32[32,4,128]{2,1,0:T(4,128)S(1)} %get-tuple-element.18), channel_id=1, source_target_pairs={{8,0},{16,8},{24,16},{32,24},{40,32},{48,40},{56,48},{64,56},{72,6... | collective-permute-start | bytes 196616 | tf_op jit(solution)/shard_map/ppermute | solution.py:21
  11.5 10.2 %collective-permute-start.1 = (f32[32,4,128]{2,1,0:T(4,128)S(1)}, f32[32,4,128]{2,1,0:T(4,128)S(1)}, u32[]{:S(2)}, u32[]{:S(2)}) collective-permute-start(f32[32,4,128]{2,1,0:T(4,128)S(1)} %get-tuple-element.19), channel_id=1, source_target_pairs={{0,8},{8,16},{16,24},{24,32},{32,40},{40,48},{48,56},{56,64},{64,7... | collective-permute-start | bytes 196616 | tf_op jit(solution)/shard_map/ppermute | solution.py:21
  15.6 5.3 %collective-permute-start.6 = (f32[32,128]{1,0:T(8,128)S(1)}, f32[32,128]{1,0:T(8,128)S(1)}, u32[]{:S(2)}, u32[]{:S(2)}) collective-permute-start(f32[32,128]{1,0:T(8,128)S(1)} %pad_maximum_fusion), channel_id=1, source_target_pairs={{8,0},{16,8},{24,16},{32,24},{40,32},{48,40},{56,48},{64,56},{72,6... | collective-permute-start | bytes 49160 | tf_op jit(solution)/shard_map/ppermute | solution.py:21
  16.9 4.8 %collective-permute-start.5 = (f32[32,128]{1,0:T(8,128)S(1)}, f32[32,128]{1,0:T(8,128)S(1)}, u32[]{:S(2)}, u32[]{:S(2)}) collective-permute-start(f32[32,128]{1,0:T(8,128)S(1)} %pad_maximum_fusion), channel_id=1, source_target_pairs={{0,8},{8,16},{16,24},{24,32},{32,40},{40,48},{48,56},{56,64},{64,7... | collective-permute-start | bytes 49160 | tf_op jit(solution)/shard_map/ppermute | solution.py:21
  46.7 11.7 %copy-start.2 = (f32[27,32,64]{2,1,0:T(8,128)S(1)}, f32[27,32,64]{2,1,0:T(8,128)}, u32[]{:S(2)}) copy-start(f32[27,32,64]{2,1,0:T(8,128)} %weights.1) | copy-start | bytes 663556
  47.4 19.0 %all-to-all-start.1 = ((f32[8,32,128]{2,1,0:T(8,128)}), f32[8,32,128]{2,1,0:T(8,128)S(1)}, u32[]{:S(2)}, u32[]{:S(2)}) async-start(f32[8,32,128]{2,1,0:T(8,128)} %bitcast.12), calls=%async_computation.1 | async-start | bytes 262144 | tf_op jit(solution)/shard_map/all_to_all | solution.py:195
  60.2 12.6 %collective-permute-start.7 = (f32[512,128]{1,0:T(8,128)S(1)}, f32[512,128]{1,0:T(8,128)S(1)}, u32[]{:S(2)}, u32[]{:S(2)}) collective-permute-start(f32[512,128]{1,0:T(8,128)S(1)} %get-tuple-element.14), channel_id=1, source_target_pairs={{0,1},{1,0},{2,3},{3,2},{4,5},{5,4},{6,7},{7,6},{8,9},{9,8},{10,11... | collective-permute-start | bytes 786440 | tf_op jit(solution)/shard_map/ppermute | solution.py:25
  67.1 14.4 %all-to-all-start.2 = ((f32[16,32,128]{2,1,0:T(8,128)}), f32[16,32,128]{2,1,0:T(8,128)S(1)}, u32[]{:S(2)}, u32[]{:S(2)}) async-start(f32[16,32,128]{2,1,0:T(8,128)} %bitcast.14), calls=%async_computation.2 | async-start | bytes 524288 | tf_op jit(solution)/shard_map/all_to_all | solution.py:196

commit v2 on v1

--- a/solution.py
+++ b/solution.py
@@ -15,14 +15,10 @@
 NT = (((1,), (1,)), ((), ()))
 
 
-def passed_along(value, axis, steps):
+def swapped(value, axis, first):
     count = lax.axis_size(axis)
-    first, last = max(0, -steps), min(count, count - steps)
-    return lax.ppermute(value, axis, [(s, s + steps) for s in range(first, last)])
-
-
-def traded(value):
-    return lax.ppermute(value, "chan", [(0, 1), (1, 0)])
+    pairs = [(s, s + 1) for s in range(first, count - 1, 2)]
+    return lax.ppermute(value, axis, pairs + [(t, s) for s, t in pairs])
 
 
 def split(value):
@@ -30,27 +26,30 @@
     return high, (value - high.astype(F32)).astype(BF16)
 
 
-def edges_kernel(grad, first, last):
+def edges_kernel(odd, core, grad, near_row, far_row, to_core, to_chip):
     lane = lax.broadcasted_iota(jnp.int32, (CI, 128), 1)
     heads = jnp.zeros((CI, 128), F32)
     tails = jnp.zeros((CI, 128), F32)
-    for cell in range(16):
-        tile = grad[pl.ds(cell, CI, stride=16), :]
-        place = 4 + cell
-        heads = jnp.where(lane == place, pltpu.roll(tile, place, 1), heads)
-        tails = jnp.where(lane == place, pltpu.roll(tile, place + 1, 1), tails)
-    first[...] = heads
-    last[...] = tails
-
-
-def rim(own, below, above, at):
-    lane = lax.broadcasted_iota(jnp.int32, (CI, 128), 1)
-    low = pltpu.roll(below, (128 - 16 - at) % 128, 1)
-    high = pltpu.roll(above, (16 - at) % 128, 1)
-    return jnp.where(lane < 4, low, jnp.where(lane >= 20, high, own))
-
-
-def spread(grad, below, above, left, right, high, low):
+    for xp in range(6):
+        for z in range(4):
+            tile = extended(odd, grad, near_row, far_row, xp, z)
+            at = 4 * xp + z
+            heads = jnp.where(lane == at, pltpu.roll(tile, at, 1), heads)
+            tails = jnp.where(lane == at, pltpu.roll(tile, at + 1, 1), tails)
+    is_first = core[0] == 0
+    to_core[...] = jnp.where(is_first, tails, heads)
+    to_chip[...] = jnp.where(is_first, heads, tails)
+
+
+def extended(odd, grad, near_row, far_row, xp, z):
+    if 0 < xp < 5:
+        return grad[pl.ds((xp - 1) * 4 + z, CI, stride=16), :]
+    near = near_row[pl.ds(z, CI, stride=4), :]
+    far = far_row[pl.ds(z, CI, stride=4), :]
+    return jnp.where((odd[0] == 1) == (xp == 0), near, far)
+
+
+def spread(odd, grad, near_row, far_row, left, right, high, low):
     lane = lax.broadcasted_iota(jnp.int32, (CI, 128), 1)
     zero = jnp.zeros((CI, 128), BF16)
     for xp in range(6):
@@ -59,12 +58,7 @@
                 ref[d, xp, :, 0:128] = zero
                 ref[d, xp, :, 640:768] = zero
         for z in range(4):
-            if xp == 0:
-                tile = below[pl.ds(z, CI, stride=4), :]
-            elif xp == 5:
-                tile = above[pl.ds(z, CI, stride=4), :]
-            else:
-                tile = grad[pl.ds((xp - 1) * 4 + z, CI, stride=16), :]
+            tile = extended(odd, grad, near_row, far_row, xp, z)
             at = xp * 4 + z
             before = jnp.where(
                 lane == 0, pltpu.roll(left, (128 - at) % 128, 1), pltpu.roll(tile, 1, 1)
@@ -95,17 +89,12 @@
 
 
 def filter_kernel(
-    chan, own, other, grad, below, above, left, right, rims_below, rims_above, out, high, low
+    chan, odd, core, own, other, grad, near_row, far_row, from_core, from_chip, out, high, low
 ):
-    spread(
-        grad,
-        below,
-        above,
-        rim(left[...], rims_below[...], rims_above[...], 0),
-        rim(right[...], rims_below[...], rims_above[...], 64),
-        high,
-        low,
-    )
+    at_left = core[0] == 0
+    left = jnp.where(at_left, from_chip[...], from_core[...])
+    right = jnp.where(at_left, from_core[...], from_chip[...])
+    spread(odd, grad, near_row, far_row, left, right, high, low)
     is_first = chan[0] == 0
     total = None
     for x in range(4):
@@ -196,28 +185,33 @@
     return lax.all_to_all(summed(copies, near), NEAR, 0, 0, tiled=True)
 
 
+def place(axis):
+    return lax.axis_index(axis).astype(jnp.int32).reshape(1)
+
+
 def body(activation, out_grad, kernel):
     act = activation.reshape(512, 128)
     grad = out_grad.reshape(512, 128)
-    chan = lax.axis_index("chan").astype(jnp.int32).reshape(1)
-    other = traded(act)
-    first, last = call(edges_kernel, (shape(CI, 128),) * 2, [VMEM])(grad)
-    left = passed_along(last, ALONG_Y, 1)
-    right = passed_along(first, ALONG_Y, -1)
+    chan, odd, core = place("chan"), lax.rem(place("y"), 2), place("c")
     rows = grad.reshape(CI, 4, 4, 128)
-    below = passed_along(rows[:, 3], ALONG_X, 1).reshape(128, 128)
-    above = passed_along(rows[:, 0], ALONG_X, -1).reshape(128, 128)
-    rims = jnp.concatenate([left[:, :64], right[:, :64]], axis=1)
-    rims_below = passed_along(rims, ALONG_X, 1)
-    rims_above = passed_along(rims, ALONG_X, -1)
+    top, bottom = rows[:, 3].reshape(128, 128), rows[:, 0].reshape(128, 128)
+    is_odd = odd[0] == 1
+    near_row = swapped(jnp.where(is_odd, bottom, top), ALONG_X, 0)
+    far_row = swapped(jnp.where(is_odd, top, bottom), ALONG_X, 1)
+    other = swapped(act, "chan", 0)
+    to_core, to_chip = call(edges_kernel, (shape(CI, 128),) * 2, [SMEM] * 2 + [VMEM] * 3)(
+        odd, core, grad, near_row, far_row
+    )
+    from_core = swapped(to_core, "c", 0)
+    from_chip = swapped(to_chip, ALONG_Y, 1)
     halves = shape(3, 6, CI, 768, dtype=BF16)
     partial, high, low = call(
-        filter_kernel, (shape(512, 128), halves, halves), [SMEM] + [VMEM] * 9, 700_000_000, 1 << 22
-    )(chan, act, other, grad, below, above, left, right, rims_below, rims_above)
+        filter_kernel, (shape(512, 128), halves, halves), [SMEM] * 3 + [VMEM] * 7, 700_000_000, 1 << 22
+    )(chan, odd, core, act, other, grad, near_row, far_row, from_core, from_chip)
     kept, sent = call(
         data_kernel, (shape(512, 128),) * 2, [SMEM] + [VMEM] * 3, 700_000_000, 1 << 22
     )(chan, kernel, high, low)
-    input_grad = (kept + traded(sent)).reshape(activation.shape)
+    input_grad = (kept + swapped(sent, "chan", 0)).reshape(activation.shape)
     packed = summed_over_tiles(partial)
     kernel_grad = call(unpack_kernel, shape(27, 32, 64), [VMEM])(packed)
     return (input_grad, kernel_grad)

time: 82.9 us -> 71.2 us (0.86)
  starting transfers between devices: 35.6 us -> 24.5 us
  blocking collectives: 22.6 us -> 19.4 us
  waiting for transfers between devices: 15 us -> 17.8 us
  local copies, waits for them, and re-layouts: 0.98 us -> 0.01 us
    ppermute x8 -> x6, starting transfers between devices: 19 us -> 10.7 us  [swapped(): return lax.ppermute(value, axis, pairs + [(t, s) for s, t in pairs])]
    all_to_all x1, blocking collectives: 22.6 us -> 19.4 us  [summed_over_tiles(): pieces = lax.all_to_all(partial, NEAR, 0, 0, tiled=True)]
    ppermute x8 -> x6, waiting for transfers between devices: 0.86 us -> 3.71 us  [swapped(): return lax.ppermute(value, axis, pairs + [(t, s) for s, t in pairs])]
    all_to_all x1, starting transfers between devices: 11 us -> 8.18 us  [summed_over_tiles(): copies = lax.all_to_all(summed(pieces, far), FAR, 0, 0, tiled=True)]
    unnamed x8 -> x6, local copies, waits for them, and re-layouts: 0.95 us -> 0.01 us
    select_n x0 -> x1, other arithmetic: none -> 0.9 us  [body(): far_row = swapped(jnp.where(is_odd, top, bottom), ALONG_X, 1)]
  transfers between devices with their start and end apart: 10 -> 8, of which waited for: 3 -> 4; matrix products, arithmetic and copies ran while one was open for 1% -> 2% of each run, Pallas kernels for 3% -> 4%
where the time goes in v2:
time: 71.2 us; the launch traced here: 70.8 us
  starting transfers between devices  24.5 us (34%)
  blocking collectives  19.4 us (27%)
  waiting for transfers between devices  17.8 us (25%)
  Pallas kernels  6.66 us (9%)
  other arithmetic  1.63 us (2%)
    all_to_all x1, blocking collectives, summed_over_tiles(): pieces = lax.all_to_all(partial, NEAR, 0, 0, tiled=True)  19.4 us
    ppermute x6, starting transfers between devices, swapped(): return lax.ppermute(value, axis, pairs + [(t, s) for s, t in pairs])  10.7 us
    all_to_all x1, starting transfers between devices, summed_over_tiles(): copies = lax.all_to_all(summed(pieces, far), FAR, 0, 0, tiled=True)  8.18 us
    all_to_all x1, waiting for transfers between devices, summed_over_tiles(): return lax.all_to_all(summed(copies, near), NEAR, 0, 0, tiled=True)  7.99 us
    all_to_all x1, waiting for transfers between devices, summed_over_tiles(): copies = lax.all_to_all(summed(pieces, far), FAR, 0, 0, tiled=True)  6.1 us
    all_to_all x1, starting transfers between devices, summed_over_tiles(): return lax.all_to_all(summed(copies, near), NEAR, 0, 0, tiled=True)  5.63 us
    ppermute x6, waiting for transfers between devices, swapped(): return lax.ppermute(value, axis, pairs + [(t, s) for s, t in pairs])  3.71 us
    pallas_call x1, Pallas kernels, body(): call(filter_kernel, (shape(512, 128), halves, halves), [SMEM] * 3 + [VMEM...  2.27 us
  transfers between devices with their start and end apart: 8, of which 4 were waited for; matrix products, arithmetic and copies ran while one was open for 2% of the time, Pallas kernels for 4%

profile of v2, /device:TPU:1, one launch (start us, length us, event | category | flops | bytes accessed | tf_op | source)
XLA Modules:
  0.0 70.8 jit_solution(14248909896498445229)
XLA Ops:
  0.6 0.0 copy-start
  0.6 2.1 %collective-permute-start = (f32[512,128]{1,0:T(8,128)}, f32[512,128]{1,0:T(8,128)S(1)}, u32[]{:S(2)}, u32[]{:S(2)}) collective-permute-start(f32[512,128]{1,0:T(8,128)} %bitcast.25), channel_id=1, source_target_pairs={{0,1},{1,0},{2,3},{3,2},{4,5},{5,4},{6,7},{7,6},{8,9},{9,8},{10,11... | collective-permute-start | bytes 786440 | tf_op jit(solution)/shard_map/ppermute | solution.py:21
  2.8 0.9 %slice_select_fusion = (f32[32,1,4,128]{3,2,1,0:T(4,128)S(1)}, f32[32,1,4,128]{3,2,1,0:T(4,128)S(1)}) fusion(f32[32,4,4,128]{3,2,1,0:T(4,128)} %bitcast.20, pred[]{:T(512)} %bitcast.5), kind=kLoop, calls=%fused_computation | loop fusion | flops 32768 | bytes 262145 | tf_op jit(solution)/shard_map/jit(_where)/select_n | solution.py:200
  3.7 0.0 copy-start.2
  3.7 1.4 %collective-permute-start.1 = (f32[128,128]{1,0:T(8,128)S(1)}, f32[128,128]{1,0:T(8,128)S(1)}, u32[]{:S(2)}, u32[]{:S(2)}) collective-permute-start(f32[128,128]{1,0:T(8,128)S(1)} %bitcast.29), channel_id=1, source_target_pairs={{0,8},{16,24},{32,40},{48,56},{64,72},{80,88},{96,104},{112,120},{... | collective-permute-start | bytes 196616 | tf_op jit(solution)/shard_map/ppermute | solution.py:21
  5.1 0.7 collective-permute-start.2
  5.7 1.2 %collective-permute-done.1.near_row = f32[128,128]{1,0:T(8,128)S(1)} collective-permute-done((f32[128,128]{1,0:T(8,128)S(1)}, f32[128,128]{1,0:T(8,128)S(1)}, u32[]{:S(2)}, u32[]{:S(2)}) %collective-permute-start.1) | collective-permute-done | bytes 65568 | tf_op jit(solution)/shard_map/ppermute | solution.py:21
  6.9 0.0 collective-permute-done.2.far_row
  6.9 0.0 copy-done
  6.9 0.3 shard_map.50
  7.2 2.5 %collective-permute-start.3 = (f32[32,128]{1,0:T(8,128)S(1)}, f32[32,128]{1,0:T(8,128)S(1)}, u32[]{:S(2)}, u32[]{:S(2)}) collective-permute-start(f32[32,128]{1,0:T(8,128)S(1)} %get-tuple-element.9), channel_id=1, source_target_pairs={{0,2},{2,0},{1,3},{3,1},{4,6},{6,4},{5,7},{7,5},{8,10},{10,8},{9,1... | collective-permute-start | bytes 49160 | tf_op jit(solution)/shard_map/ppermute | solution.py:21
  9.6 4.0 %collective-permute-start.4 = (f32[32,128]{1,0:T(8,128)S(1)}, f32[32,128]{1,0:T(8,128)S(1)}, u32[]{:S(2)}, u32[]{:S(2)}) collective-permute-start(f32[32,128]{1,0:T(8,128)S(1)} %get-tuple-element.10), channel_id=1, source_target_pairs={{2,4},{4,2},{3,5},{5,3},{10,12},{12,10},{11,13},{13,11},{18,20},{2... | collective-permute-start | bytes 49160 | tf_op jit(solution)/shard_map/ppermute | solution.py:21
  13.6 0.0 collective-permute-done.3.from_core
  13.6 2.5 %collective-permute-done.4.from_chip = f32[32,128]{1,0:T(8,128)S(1)} collective-permute-done((f32[32,128]{1,0:T(8,128)S(1)}, f32[32,128]{1,0:T(8,128)S(1)}, u32[]{:S(2)}, u32[]{:S(2)}) %collective-permute-start.4) | collective-permute-done | bytes 16416 | tf_op jit(solution)/shard_map/ppermute | solution.py:21
  16.2 0.0 collective-permute-done.other
  16.2 0.0 copy-done.2
  16.2 2.3 %shard_map.51 = (f32[512,128]{1,0:T(8,128)S(1)}, bf16[3,6,32,768]{3,2,1,0:T(8,128)(2,1)S(1)}, bf16[3,6,32,768]{3,2,1,0:T(8,128)(2,1)S(1)}) custom-call(s32[1]{0:T(128)} %bitcast.chan, s32[1]{0:T(128)S(6)} %rem.18.odd, s32[1]{0:T(128)} %bitcast.2.core, f32[512,128]{1,0:T(8,128)S(1)} %bitcast.26, f32[512,128]{1,0:T(8,128)S(1)} %collective-permute-done.other, ...), custom_call_target="tpu_custom_call" | custom-call | flops 700000000 | bytes 4194304 | tf_op jit(solution)/shard_map/pallas_call | solution.py:208
  18.4 19.4 %all_to_all.33 = f32[16,32,128]{2,1,0:T(8,128)S(1)} all-to-all(f32[16,32,128]{2,1,0:T(8,128)S(1)} %bitcast.24), channel_id=1, replica_groups=mesh['z'=8,'y'=4,'xh'=2,'c'=2,'chan'=2] {'y','xh','c'}, dimensions={0} | all-to-all | bytes 524288 | tf_op jit(solution)/shard_map/all_to_all | solution.py:183
  37.9 0.0 copy-start.1
  37.9 0.7 shard_map.53
  38.6 8.2 %all-to-all-start.1 = ((f32[8,32,128]{2,1,0:T(8,128)}), f32[8,32,128]{2,1,0:T(8,128)S(1)}, u32[]{:S(2)}, u32[]{:S(2)}) async-start(f32[8,32,128]{2,1,0:T(8,128)} %bitcast.13), calls=%async_computation.1 | async-start | bytes 262144 | tf_op jit(solution)/shard_map/all_to_all | solution.py:184
  46.7 0.0 copy-done.1
  46.7 1.8 %shard_map.52 = (f32[512,128]{1,0:T(8,128)S(1)}, f32[512,128]{1,0:T(8,128)S(1)}) custom-call(s32[1]{0:T(128)} %bitcast.chan, f32[27,32,64]{2,1,0:T(8,128)S(1)} %copy-done.1, bf16[3,6,32,768]{3,2,1,0:T(8,128)(2,1)S(1)} %get-tuple-element.11.high, bf16[3,6,32,768]{3,2,1,0:T(8,128)(2,1)S(1)} %get-tuple-element.12.low), custom_call_target="tpu_custom_call" | custom-call | flops 700000000 | bytes 4194304 | tf_op jit(solution)/shard_map/pallas_call | solution.py:211
  48.6 0.1 collective-permute-start.5
  48.7 6.1 %all-to-all-done.1 = f32[8,32,128]{2,1,0:T(8,128)S(1)} async-done(((f32[8,32,128]{2,1,0:T(8,128)}), f32[8,32,128]{2,1,0:T(8,128)S(1)}, u32[]{:S(2)}, u32[]{:S(2)}) %all-to-all-start.1) | async-done | bytes 131104 | tf_op jit(solution)/shard_map/all_to_all | solution.py:184
  54.8 0.7 %shard_map.54 = f32[512,128]{1,0:T(8,128)} custom-call(f32[256,128]{1,0:T(8,128)S(1)} %bitcast.23), custom_call_target="tpu_custom_call" | custom-call | tf_op jit(solution)/shard_map/pallas_call | solution.py:178
  55.5 5.6 %all-to-all-start.2 = ((f32[16,32,128]{2,1,0:T(8,128)}), f32[16,32,128]{2,1,0:T(8,128)S(1)}, u32[]{:S(2)}, u32[]{:S(2)}) async-start(f32[16,32,128]{2,1,0:T(8,128)} %bitcast.15), calls=%async_computation.2 | async-start | bytes 524288 | tf_op jit(solution)/shard_map/all_to_all | solution.py:185
  61.1 0.0 collective-permute-done.5
  61.1 0.7 %add.3 = f32[512,128]{1,0:T(8,128)} add(f32[512,128]{1,0:T(8,128)S(1)} %get-tuple-element.13, f32[512,128]{1,0:T(8,128)S(1)} %collective-permute-done.5) | non-fusion elementwise | flops 65536 | bytes 786432 | tf_op jit(solution)/shard_map/add | solution.py:214
  61.9 8.0 %all-to-all-done.2 = f32[16,32,128]{2,1,0:T(8,128)S(1)} async-done(((f32[16,32,128]{2,1,0:T(8,128)}), f32[16,32,128]{2,1,0:T(8,128)S(1)}, u32[]{:S(2)}, u32[]{:S(2)}) %all-to-all-start.2) | async-done | bytes 262176 | tf_op jit(solution)/shard_map/all_to_all | solution.py:185
  69.9 0.9 %shard_map.55 = f32[27,32,64]{2,1,0:T(8,128)} custom-call(f32[512,128]{1,0:T(8,128)S(1)} %bitcast.19), custom_call_target="tpu_custom_call" | custom-call | tf_op jit(solution)/shard_map/pallas_call | solution.py:216
Async XLA Ops:
  0.6 6.3 %copy-start = (f32[32,1,4,4,128]{4,3,2,1,0:T(4,128)S(1)}, f32[32,1,4,4,128]{4,3,2,1,0:T(4,128)}, u32[]{:S(2)}) copy-start(f32[32,1,4,4,128]{4,3,2,1,0:T(4,128)} %param.4) | copy-start | bytes 786436
  0.6 15.5 %collective-permute-start = (f32[512,128]{1,0:T(8,128)}, f32[512,128]{1,0:T(8,128)S(1)}, u32[]{:S(2)}, u32[]{:S(2)}) collective-permute-start(f32[512,128]{1,0:T(8,128)} %bitcast.25), channel_id=1, source_target_pairs={{0,1},{1,0},{2,3},{3,2},{4,5},{5,4},{6,7},{7,6},{8,9},{9,8},{10,11... | collective-permute-start | bytes 786440 | tf_op jit(solution)/shard_map/ppermute | solution.py:21
  3.7 12.5 %copy-start.2 = (f32[32,1,4,4,128]{4,3,2,1,0:T(4,128)S(1)}, f32[32,1,4,4,128]{4,3,2,1,0:T(4,128)}, u32[]{:S(2)}) copy-start(f32[32,1,4,4,128]{4,3,2,1,0:T(4,128)} %param.3) | copy-start | bytes 786436
  3.7 3.2 %collective-permute-start.1 = (f32[128,128]{1,0:T(8,128)S(1)}, f32[128,128]{1,0:T(8,128)S(1)}, u32[]{:S(2)}, u32[]{:S(2)}) collective-permute-start(f32[128,128]{1,0:T(8,128)S(1)} %bitcast.29), channel_id=1, source_target_pairs={{0,8},{16,24},{32,40},{48,56},{64,72},{80,88},{96,104},{112,120},{... | collective-permute-start | bytes 196616 | tf_op jit(solution)/shard_map/ppermute | solution.py:21
  5.1 1.8 %collective-permute-start.2 = (f32[128,128]{1,0:T(8,128)S(1)}, f32[128,128]{1,0:T(8,128)S(1)}, u32[]{:S(2)}, u32[]{:S(2)}) collective-permute-start(f32[128,128]{1,0:T(8,128)S(1)} %bitcast.28), channel_id=1, source_target_pairs={{8,16},{24,32},{40,48},{56,64},{72,80},{88,96},{104,112},{120,128}... | collective-permute-start | bytes 196616 | tf_op jit(solution)/shard_map/ppermute | solution.py:21
  7.2 6.5 %collective-permute-start.3 = (f32[32,128]{1,0:T(8,128)S(1)}, f32[32,128]{1,0:T(8,128)S(1)}, u32[]{:S(2)}, u32[]{:S(2)}) collective-permute-start(f32[32,128]{1,0:T(8,128)S(1)} %get-tuple-element.9), channel_id=1, source_target_pairs={{0,2},{2,0},{1,3},{3,1},{4,6},{6,4},{5,7},{7,5},{8,10},{10,8},{9,1... | collective-permute-start | bytes 49160 | tf_op jit(solution)/shard_map/ppermute | solution.py:21
  9.6 6.5 %collective-permute-start.4 = (f32[32,128]{1,0:T(8,128)S(1)}, f32[32,128]{1,0:T(8,128)S(1)}, u32[]{:S(2)}, u32[]{:S(2)}) collective-permute-start(f32[32,128]{1,0:T(8,128)S(1)} %get-tuple-element.10), channel_id=1, source_target_pairs={{2,4},{4,2},{3,5},{5,3},{10,12},{12,10},{11,13},{13,11},{18,20},{2... | collective-permute-start | bytes 49160 | tf_op jit(solution)/shard_map/ppermute | solution.py:21
  37.9 8.9 %copy-start.1 = (f32[27,32,64]{2,1,0:T(8,128)S(1)}, f32[27,32,64]{2,1,0:T(8,128)}, u32[]{:S(2)}) copy-start(f32[27,32,64]{2,1,0:T(8,128)} %weights.1) | copy-start | bytes 663556
  38.6 16.2 %all-to-all-start.1 = ((f32[8,32,128]{2,1,0:T(8,128)}), f32[8,32,128]{2,1,0:T(8,128)S(1)}, u32[]{:S(2)}, u32[]{:S(2)}) async-start(f32[8,32,128]{2,1,0:T(8,128)} %bitcast.13), calls=%async_computation.1 | async-start | bytes 262144 | tf_op jit(solution)/shard_map/all_to_all | solution.py:184
  48.6 12.6 %collective-permute-start.5 = (f32[512,128]{1,0:T(8,128)S(1)}, f32[512,128]{1,0:T(8,128)S(1)}, u32[]{:S(2)}, u32[]{:S(2)}) collective-permute-start(f32[512,128]{1,0:T(8,128)S(1)} %get-tuple-element.14), channel_id=1, source_target_pairs={{0,1},{1,0},{2,3},{3,2},{4,5},{5,4},{6,7},{7,6},{8,9},{9,8},{10,11... | collective-permute-start | bytes 786440 | tf_op jit(solution)/shard_map/ppermute | solution.py:21
  55.5 14.4 %all-to-all-start.2 = ((f32[16,32,128]{2,1,0:T(8,128)}), f32[16,32,128]{2,1,0:T(8,128)S(1)}, u32[]{:S(2)}, u32[]{:S(2)}) async-start(f32[16,32,128]{2,1,0:T(8,128)} %bitcast.15), calls=%async_computation.2 | async-start | bytes 524288 | tf_op jit(solution)/shard_map/all_to_all | solution.py:185

commit v3 on v2

v3 whole, which is shorter than its diff:
```python
import jax
import jax.numpy as jnp
from jax import lax
from jax.experimental import pallas as pl
from jax.experimental.pallas import tpu as pltpu
from jax.sharding import Mesh, PartitionSpec as P

F32, BF16 = jnp.float32, jnp.bfloat16
ALONG_X = ("z", "y")
ALONG_Y = ("xh", "c")
TILE = ALONG_X + ALONG_Y
CI = 32
NT = (((1,), (1,)), ((), ()))


def swapped(value, axis, first):
    count = lax.axis_size(axis)
    pairs = [(s, (s + 1) % count) for s in range(first, count, 2)]
    return lax.ppermute(value, axis, pairs + [(t, s) for s, t in pairs])


def split(value):
    high = value.astype(BF16)
    return high, (value - high.astype(F32)).astype(BF16)


def rows_kernel(along, grad, near, far):
    odd = is_odd(along)
    for z in range(4):
        top = grad[pl.ds(12 + z, CI, stride=16), :]
        bottom = grad[pl.ds(z, CI, stride=16), :]
        near[pl.ds(z, CI, stride=4), :] = jnp.where(odd, bottom, top)
        far[pl.ds(z, CI, stride=4), :] = jnp.where(odd, top, bottom)


def edges_kernel(along, across, grad, near_row, far_row, to_core, to_chip):
    lane = lax.broadcasted_iota(jnp.int32, (CI, 128), 1)
    heads = jnp.zeros((CI, 128), F32)
    tails = jnp.zeros((CI, 128), F32)
    for xp in range(6):
        for z in range(4):
            tile = extended(along, grad, near_row, far_row, xp, z)
            at = 6 * xp + z + 1
            heads = jnp.where(lane == at, pltpu.roll(tile, at, 1), heads)
            tails = jnp.where(lane == at, pltpu.roll(tile, at + 1, 1), tails)
    odd = is_odd(across)
    to_core[...] = jnp.where(odd, heads, tails)
    to_chip[...] = jnp.where(odd, tails, heads)


def extended(along, grad, near_row, far_row, xp, z):
    if 0 < xp < 5:
        return grad[pl.ds((xp - 1) * 4 + z, CI, stride=16), :]
    near = near_row[pl.ds(z, CI, stride=4), :]
    far = far_row[pl.ds(z, CI, stride=4), :]
    row = jnp.where(is_odd(along) == (xp == 0), near, far)
    return jnp.where(along[0] == (0 if xp == 0 else 31), 0.0, row)


def is_odd(place):
    return (place[0] & 1) == 1


def spread(along, grad, near_row, far_row, left, right, high, low):
    lane = lax.broadcasted_iota(jnp.int32, (CI, 128), 1)
    zero = jnp.zeros((CI, 128), BF16)
    for xp in range(6):
        for d in range(3):
            for ref in (high, low):
                ref[d, xp, :, 0:128] = zero
                ref[d, xp, :, 640:768] = zero
        for z in range(4):
            tile = extended(along, grad, near_row, far_row, xp, z)
            before, after = pltpu.roll(tile, 1, 1), pltpu.roll(tile, 127, 1)
            if left is None:
                before = jnp.where(lane == 0, 0.0, before)
                after = jnp.where(lane == 127, 0.0, after)
            else:
                at = 6 * xp + z + 1
                before = jnp.where(lane == 0, pltpu.roll(left, 128 - at, 1), before)
                after = jnp.where(lane == 127, pltpu.roll(right, 127 - at, 1), after)
            for d, value in ((0, after), (1, tile), (2, before)):
                high[d, xp, :, (z + 1) * 128 : (z + 2) * 128], low[
                    d, xp, :, (z + 1) * 128 : (z + 2) * 128
                ] = split(value)


def taps(ref, x):
    return jnp.concatenate(
        [
            ref[d, x + 2 - a, :, (2 - b) * 128 : (2 - b) * 128 + 512]
            for a in range(3)
            for b in range(3)
            for d in range(3)
        ],
        axis=0,
    )


def x_row(ref, x):
    return jnp.concatenate([ref[pl.ds(x * 4 + z, CI, stride=16), :] for z in range(4)], axis=1)


def filter_kernel(
    chan, along, own, other, grad, near_row, far_row, total_out, first_out, last_out, high, low
):
    spread(along, grad, near_row, far_row, None, None, high, low)
    is_first = chan[0] == 0
    lane = lax.broadcasted_iota(jnp.int32, (64, 128), 1)
    heads = jnp.zeros((64, 128), F32)
    tails = jnp.zeros((64, 128), F32)
    total = None
    for x in range(4):
        mine, theirs = x_row(own, x), x_row(other, x)
        act = jnp.concatenate(
            [jnp.where(is_first, mine, theirs), jnp.where(is_first, theirs, mine)], axis=0
        )
        for z in range(4):
            at, tile = 6 * x + z, act[:, 128 * z : 128 * z + 128]
            heads = jnp.where(lane == at, pltpu.roll(tile, at, 1) if at else tile, heads)
            tails = jnp.where(lane == at, pltpu.roll(tile, at + 1, 1), tails)
        act_high, act_low = split(act)
        both = jnp.concatenate([act_high, act_low], axis=0)
        p = lax.dot_general(taps(high, x), both, NT, preferred_element_type=F32)
        q = lax.dot_general(taps(low, x), act_high, NT, preferred_element_type=F32)
        part = p[:, :64] + p[:, 64:] + q
        total = part if total is None else total + part
    total_out[...] = total
    first_out[...] = heads
    last_out[...] = tails


def rims(across, from_core, from_chip):
    odd = is_odd(across)
    left = jnp.where(odd, from_core[...], from_chip[...])
    right = jnp.where(odd, from_chip[...], from_core[...])
    return jnp.where(across[0] == 0, 0.0, left), jnp.where(across[0] == 3, 0.0, right)


def rim_taps(rim, column):
    shifted = jnp.concatenate(
        [
            pltpu.roll(rim, 128 - (6 * (2 - a) + 2 - b), 1) if a + b < 4 else rim
            for a in range(3)
            for b in range(3)
        ],
        axis=0,
    )
    high, low = split(shifted)
    col_high, col_low = split(column)
    both = jnp.concatenate([col_high, col_low], axis=0)
    p = lax.dot_general(high, both, NT, preferred_element_type=F32)
    q = lax.dot_general(low, col_high, NT, preferred_element_type=F32)
    return p[:, :64] + p[:, 64:] + q


def rim_kernel(across, total, first, last, from_core, from_chip, keep, give):
    left, right = rims(across, from_core, from_chip)
    extra = {2: rim_taps(left, first[...]), 0: rim_taps(right, last[...])}

    def of_tap(tap):
        if tap > 26:
            return jnp.zeros((CI, 64), F32)
        value = total[CI * tap : CI * tap + CI, :]
        group, d = divmod(tap, 3)
        if d in extra:
            value = value + extra[d][CI * group : CI * group + CI]
        return value * (1.0 / 512.0)

    odd = is_odd(across)
    for j in range(8):
        pairs = [
            jnp.concatenate([of_tap(2 * pair), of_tap(2 * pair + 1)], axis=1)
            for pair in (j, j + 8)
        ]
        keep[32 * j : 32 * j + 32, :] = jnp.where(odd, pairs[1], pairs[0])
        give[32 * j : 32 * j + 32, :] = jnp.where(odd, pairs[0], pairs[1])


def data_kernel(
    chan, along, across, weights, grad, near_row, far_row, from_core, from_chip, kept, sent, high, low
):
    left, right = rims(across, from_core, from_chip)
    spread(along, grad, near_row, far_row, left, right, high, low)
    w = weights[...].reshape(864, 64)
    w = jnp.where(chan[0] == 0, w, jnp.concatenate([w[:, 32:], w[:, :32]], axis=1))
    w_high = w.astype(BF16).astype(F32)
    both = jnp.concatenate([w_high, w - w_high], axis=1)
    both = jnp.concatenate([both, jnp.zeros((32, 128), F32)], axis=0)
    both = both.T.astype(BF16)[:, :864]
    for x in range(4):
        p = jnp.dot(both, taps(high, x), preferred_element_type=F32)
        q = jnp.dot(both[:64], taps(low, x), preferred_element_type=F32)
        result = p[:64] + p[64:] + q
        for z in range(4):
            tile = result[:, z * 128 : (z + 1) * 128]
            kept[pl.ds(x * 4 + z, CI, stride=16), :] = tile[:32]
            sent[pl.ds(x * 4 + z, CI, stride=16), :] = tile[32:]


def quarter(ref, index):
    return ref[pl.ds(pl.multiple_of(index * 64, 64), 64), :]


def quarters_kernel(row, kept, received, own, one, two, three, both):
    both[...] = kept[...] + received[...]
    for bits, out in enumerate((own, one, two, three)):
        out[...] = quarter(both, row[0] ^ bits)


def sum_kernel(own, one, two, three, out):
    out[...] = (own[...] + one[...]) + (two[...] + three[...])


def copies_kernel(own, other, out):
    total = own[...] + other[...]
    for j in range(8):
        out[64 * j : 64 * j + 64, :] = total


def fold_kernel(pieces, out):
    total = pieces[0:64, :]
    for j in range(1, 8):
        total = total + pieces[64 * j : 64 * j + 64, :]
    out[...] = total


def join_kernel(core, own, other, out):
    at_left = core[0] == 0
    out[0:64, :] = jnp.where(at_left, own[...], other[...])
    out[64:128, :] = jnp.where(at_left, other[...], own[...])


def unpack_kernel(row, own, one, two, three, out):
    low_bit, high_bit = (row[0] & 1) == 0, (row[0] & 2) == 0
    refs = (own, one, two, three)
    for part in range(4):
        a, b, c, d = (refs[part ^ bits][...] for bits in range(4))
        value = jnp.where(high_bit, jnp.where(low_bit, a, b), jnp.where(low_bit, c, d))
        for half in range(2):
            for j in range(2):
                pair = 8 * half + 2 * part + j
                rows = value[64 * half + 32 * j : 64 * half + 32 * j + 32]
                for k in range(2):
                    if 2 * pair + k < 27:
                        out[2 * pair + k, :, :] = rows[:, 64 * k : 64 * k + 64]


VMEM = pl.BlockSpec(memory_space=pltpu.VMEM)
SMEM = pl.BlockSpec(memory_space=pltpu.SMEM)
PARAMS = pltpu.CompilerParams(vmem_limit_bytes=40 * 2**20)


def shape(*dims, dtype=F32):
    return jax.ShapeDtypeStruct(dims, dtype)


def call(kernel, outs, in_specs, scratch=(), flops=0, moved=0):
    return pl.pallas_call(
        kernel,
        out_shape=outs,
        in_specs=in_specs,
        out_specs=jax.tree.map(lambda _: VMEM, outs),
        scratch_shapes=scratch,
        compiler_params=PARAMS,
        cost_estimate=pl.CostEstimate(flops=flops, bytes_accessed=moved, transcendentals=0),
    )


def crossed(value, bits):
    return lax.ppermute(value, "y", [(s, s ^ bits) for s in range(4)])


def summed_over_tiles(keep, give):
    row, core = place("y"), place("c")
    small = shape(64, 128)
    own, one, two, three = call(
        quarters_kernel, (small,) * 4, [SMEM, VMEM, VMEM], [pltpu.VMEM((256, 128), F32)]
    )(row, keep, swapped(give, "c", 0))
    two, one, three = crossed(two, 2), crossed(one, 1), crossed(three, 3)
    part = call(sum_kernel, small, [VMEM] * 4)(own, one, two, three)
    copies = call(copies_kernel, shape(512, 128), [VMEM] * 2)(part, swapped(part, "xh", 0))
    copies = lax.all_to_all(copies, "z", 0, 0, tiled=True)
    part = call(fold_kernel, small, [VMEM])(copies)
    part = call(join_kernel, shape(128, 128), [SMEM, VMEM, VMEM])(core, part, swapped(part, "c", 0))
    two, one, three = crossed(part, 2), crossed(part, 1), crossed(part, 3)
    return call(unpack_kernel, shape(27, 32, 64), [SMEM] + [VMEM] * 4)(row, part, one, two, three)


def place(axis):
    return lax.axis_index(axis).astype(jnp.int32).reshape(1)


def body(activation, out_grad, kernel):
    act = activation.reshape(512, 128)
    grad = out_grad.reshape(512, 128)
    chan, along, across = place("chan"), place(ALONG_X), place(ALONG_Y)
    other = swapped(act, "chan", 0)
    to_near, to_far = call(rows_kernel, (shape(128, 128),) * 2, [SMEM, VMEM])(along, grad)
    far_row = swapped(to_far, ALONG_X, 1)
    near_row = swapped(to_near, ALONG_X, 0)
    to_core, to_chip = call(edges_kernel, (shape(CI, 128),) * 2, [SMEM] * 2 + [VMEM] * 3)(
        along, across, grad, near_row, far_row
    )
    from_core = swapped(to_core, "c", 0)
    from_chip = swapped(to_chip, ALONG_Y, 1)
    halves = [pltpu.VMEM((3, 6, CI, 768), BF16)] * 2
    column = shape(64, 128)
    total, first, last = call(
        filter_kernel, (shape(864, 64), column, column), [SMEM] * 2 + [VMEM] * 5, halves, 700_000_000, 1 << 22
    )(chan, along, act, other, grad, near_row, far_row)
    keep, give = call(rim_kernel, (shape(256, 128),) * 2, [SMEM] + [VMEM] * 5)(
        across, total, first, last, from_core, from_chip
    )
    kept, sent = call(
        data_kernel, (shape(512, 128),) * 2, [SMEM] * 3 + [VMEM] * 6, halves, 700_000_000, 1 << 22
    )(chan, along, across, kernel, grad, near_row, far_row, from_core, from_chip)
    input_grad = (kept + swapped(sent, "chan", 0)).reshape(activation.shape)
    kernel_grad = summed_over_tiles(keep, give)
    return (input_grad, kernel_grad)


def solution(mesh):
    mesh = Mesh(mesh.devices.reshape(8, 4, 2, 2, 2), TILE + ("chan",))
    field = P("chan", TILE, None, None, None)
    weights = P(None, "chan", None)
    return jax.shard_map(
        body,
        mesh=mesh,
        in_specs=(field, field, weights),
        out_specs=(field, weights),
        check_vma=False,
    )
```

time: 71.2 us -> 64 us (0.90)
  blocking collectives: 19.4 us -> 0 us
  starting transfers between devices: 24.5 us -> 37.3 us
  local copies, waits for them, and re-layouts: 0.01 us -> 0.97 us
  other arithmetic: 1.63 us -> 0.73 us
    all_to_all x1 -> x0, blocking collectives: 19.4 us -> none  [summed_over_tiles(): pieces = lax.all_to_all(partial, NEAR, 0, 0, tiled=True)]
    ppermute x6 -> x9, starting transfers between devices: 10.7 us -> 23.1 us  [swapped(): return lax.ppermute(value, axis, pairs + [(t, s) for s, t in pairs])]
    ppermute x0 -> x6, starting transfers between devices: none -> 7.87 us  [crossed(): return lax.ppermute(value, 'y', [(s, s ^ bits) for s in range(4)])]
    all_to_all x2 -> x1, starting transfers between devices: 13.8 us -> 6.4 us  [summed_over_tiles(): copies = lax.all_to_all(copies, 'z', 0, 0, tiled=True)]
    all_to_all x2 -> x1, waiting for transfers between devices: 14.1 us -> 7.12 us  [summed_over_tiles(): copies = lax.all_to_all(copies, 'z', 0, 0, tiled=True)]
    ppermute x0 -> x6, waiting for transfers between devices: none -> 4.68 us  [crossed(): return lax.ppermute(value, 'y', [(s, s ^ bits) for s in range(4)])]
    ppermute x6 -> x9, waiting for transfers between devices: 3.71 us -> 5.58 us  [swapped(): return lax.ppermute(value, axis, pairs + [(t, s) for s, t in pairs])]
    unnamed x6 -> x8, local copies, waits for them, and re-layouts: 0.01 us -> 0.97 us
  transfers between devices with their start and end apart: 8 -> 16, of which waited for: 4 -> 9; matrix products, arithmetic and copies ran while one was open for 2% -> 1% of each run, Pallas kernels for 4% -> 7%
where the time goes in v3:
time: 64 us; the launch traced here: 63.8 us
  starting transfers between devices  37.3 us (58%)
  waiting for transfers between devices  17.4 us (27%)
  Pallas kernels  6.68 us (10%)
  local copies, waits for them, and re-layouts  0.97 us (2%)
  other arithmetic  0.73 us (1%)
  between operations  0.73 us (1%)
    ppermute x9, starting transfers between devices, swapped(): return lax.ppermute(value, axis, pairs + [(t, s) for s, t in pairs])  23.1 us
    ppermute x6, starting transfers between devices, crossed(): return lax.ppermute(value, 'y', [(s, s ^ bits) for s in range(4)])  7.87 us
    all_to_all x1, waiting for transfers between devices, summed_over_tiles(): copies = lax.all_to_all(copies, 'z', 0, 0, tiled=True)  7.12 us
    all_to_all x1, starting transfers between devices, summed_over_tiles(): copies = lax.all_to_all(copies, 'z', 0, 0, tiled=True)  6.4 us
    ppermute x9, waiting for transfers between devices, swapped(): return lax.ppermute(value, axis, pairs + [(t, s) for s, t in pairs])  5.58 us
    ppermute x6, waiting for transfers between devices, crossed(): return lax.ppermute(value, 'y', [(s, s ^ bits) for s in range(4)])  4.68 us
    pallas_call x1, Pallas kernels, body(): call(filter_kernel, (shape(864, 64), column, column), [SMEM] * 2 + [VMEM]...  2.21 us
    pallas_call x1, Pallas kernels, body(): call(data_kernel, (shape(512, 128),) * 2, [SMEM] * 3 + [VMEM] * 6, halves...  2.03 us
  transfers between devices with their start and end apart: 16, of which 9 were waited for; matrix products, arithmetic and copies ran while one was open for 1% of the time, Pallas kernels for 7%

profile of v3, /device:TPU:1, one launch (start us, length us, event | category | flops | bytes accessed | tf_op | source)
XLA Modules:
  0.0 63.8 jit_solution(1810909866627144094)
XLA Ops:
  0.6 2.1 %collective-permute-start.5 = (f32[512,128]{1,0:T(8,128)}, f32[512,128]{1,0:T(8,128)S(1)}, u32[]{:S(2)}, u32[]{:S(2)}) collective-permute-start(f32[512,128]{1,0:T(8,128)} %bitcast.17), channel_id=1, source_target_pairs={{0,1},{1,0},{2,3},{3,2},{4,5},{5,4},{6,7},{7,6},{8,9},{9,8},{10,11... | collective-permute-start | bytes 786440 | tf_op jit(solution)/shard_map/ppermute | solution.py:19
  2.8 0.9 %copy-done = f32[32,1,4,4,128]{4,3,2,1,0:T(4,128)S(1)} copy-done((f32[32,1,4,4,128]{4,3,2,1,0:T(4,128)S(1)}, f32[32,1,4,4,128]{4,3,2,1,0:T(4,128)}, u32[]{:S(2)}) %copy-start) | copy-done | bytes 262168
  3.8 1.4 %collective-permute-start = (f32[128,128]{1,0:T(8,128)S(1)}, f32[128,128]{1,0:T(8,128)S(1)}, u32[]{:S(2)}, u32[]{:S(2)}) collective-permute-start(f32[128,128]{1,0:T(8,128)S(1)} %get-tuple-element.17), channel_id=1, source_target_pairs={{0,8},{16,24},{32,40},{48,56},{64,72},{80,88},{96,104},{112,120},{... | collective-permute-start | bytes 196616 | tf_op jit(solution)/shard_map/ppermute | solution.py:19
  5.2 7.2 %collective-permute-start.1 = (f32[128,128]{1,0:T(8,128)S(1)}, f32[128,128]{1,0:T(8,128)S(1)}, u32[]{:S(2)}, u32[]{:S(2)}) collective-permute-start(f32[128,128]{1,0:T(8,128)S(1)} %get-tuple-element.18), channel_id=1, source_target_pairs={{8,16},{24,32},{40,48},{56,64},{72,80},{88,96},{104,112},{120,128}... | collective-permute-start | bytes 196616 | tf_op jit(solution)/shard_map/ppermute | solution.py:19
  12.3 1.6 %collective-permute-done.1.far_row = f32[128,128]{1,0:T(8,128)S(1)} collective-permute-done((f32[128,128]{1,0:T(8,128)S(1)}, f32[128,128]{1,0:T(8,128)S(1)}, u32[]{:S(2)}, u32[]{:S(2)}) %collective-permute-start.1) | collective-permute-done | bytes 65568 | tf_op jit(solution)/shard_map/ppermute | solution.py:19
  14.0 0.3 shard_map.51
  14.3 2.2 %collective-permute-start.2 = (f32[32,128]{1,0:T(8,128)S(1)}, f32[32,128]{1,0:T(8,128)S(1)}, u32[]{:S(2)}, u32[]{:S(2)}) collective-permute-start(f32[32,128]{1,0:T(8,128)S(1)} %get-tuple-element.19), channel_id=1, source_target_pairs={{0,2},{2,0},{1,3},{3,1},{4,6},{6,4},{5,7},{7,5},{8,10},{10,8},{9,1... | collective-permute-start | bytes 49160 | tf_op jit(solution)/shard_map/ppermute | solution.py:19
  16.5 2.4 %collective-permute-start.3 = (f32[32,128]{1,0:T(8,128)S(1)}, f32[32,128]{1,0:T(8,128)S(1)}, u32[]{:S(2)}, u32[]{:S(2)}) collective-permute-start(f32[32,128]{1,0:T(8,128)S(1)} %get-tuple-element.20), channel_id=1, source_target_pairs={{2,4},{6,0},{4,2},{0,6},{3,5},{7,1},{5,3},{1,7},{10,12},{14,8},{12... | collective-permute-start | bytes 49160 | tf_op jit(solution)/shard_map/ppermute | solution.py:19
  18.9 2.2 %shard_map.53 = (f32[864,64]{1,0:T(8,128)S(1)}, f32[64,128]{1,0:T(8,128)S(1)}, f32[64,128]{1,0:T(8,128)S(1)}) custom-call(s32[1]{0:T(128)} %bitcast.chan, s32[1]{0:T(128)} %bitcast.1.along, f32[512,128]{1,0:T(8,128)S(1)} %bitcast.18, f32[512,128]{1,0:T(8,128)S(1)} %collective-permute-done.5.other, f32[512,128]{1,0:T(8,128)S(1)} %bitcast.14, ...), custom_call_target="tpu_custom_call" | custom-call | flops 700000000 | bytes 4194304 | tf_op jit(solution)/shard_map/pallas_call | solution.py:309
  21.2 0.4 shard_map.54
  21.6 0.5 collective-permute-start.6
  22.1 1.0 %collective-permute-done.6.received = f32[256,128]{1,0:T(8,128)S(1)} collective-permute-done((f32[256,128]{1,0:T(8,128)S(1)}, f32[256,128]{1,0:T(8,128)S(1)}, u32[]{:S(2)}, u32[]{:S(2)}) %collective-permute-start.6) | collective-permute-done | bytes 131104 | tf_op jit(solution)/shard_map/ppermute | solution.py:19
  23.1 0.1 collective-permute-start.7
  23.2 0.1 collective-permute-start.8
  23.3 3.7 %collective-permute-start.9 = (f32[64,128]{1,0:T(8,128)S(1)}, f32[64,128]{1,0:T(8,128)S(1)}, u32[]{:S(2)}, u32[]{:S(2)}) collective-permute-start(f32[64,128]{1,0:T(8,128)S(1)} %get-tuple-element.31), channel_id=1, source_target_pairs={{0,24},{8,16},{16,8},{24,0},{1,25},{9,17},{17,9},{25,1},{2,26},{10... | collective-permute-start | bytes 98312 | tf_op jit(solution)/shard_map/ppermute | solution.py:271
  27.1 0.5 collective-permute-done.8.two
  27.6 1.1 %collective-permute-done.9.three = f32[64,128]{1,0:T(8,128)S(1)} collective-permute-done((f32[64,128]{1,0:T(8,128)S(1)}, f32[64,128]{1,0:T(8,128)S(1)}, u32[]{:S(2)}, u32[]{:S(2)}) %collective-permute-start.9) | collective-permute-done | bytes 32800 | tf_op jit(solution)/shard_map/ppermute | solution.py:271
  28.7 2.3 %collective-permute-start.10 = (f32[64,128]{1,0:T(8,128)S(1)}, f32[64,128]{1,0:T(8,128)S(1)}, u32[]{:S(2)}, u32[]{:S(2)}) collective-permute-start(f32[64,128]{1,0:T(8,128)S(1)} %shard_map.56.own), channel_id=1, source_target_pairs={{0,4},{4,0},{1,5},{5,1},{2,6},{6,2},{3,7},{7,3},{8,12},{12,8},{9,1... | collective-permute-start | bytes 98312 | tf_op jit(solution)/shard_map/ppermute | solution.py:19
  31.0 2.1 %collective-permute-done.10.other = f32[64,128]{1,0:T(8,128)S(1)} collective-permute-done((f32[64,128]{1,0:T(8,128)S(1)}, f32[64,128]{1,0:T(8,128)S(1)}, u32[]{:S(2)}, u32[]{:S(2)}) %collective-permute-start.10) | collective-permute-done | bytes 32800 | tf_op jit(solution)/shard_map/ppermute | solution.py:19
  33.1 0.7 %shard_map.57 = f32[512,128]{1,0:T(8,128)} custom-call(f32[64,128]{1,0:T(8,128)S(1)} %shard_map.56.own, f32[64,128]{1,0:T(8,128)S(1)} %collective-permute-done.10.other), custom_call_target="tpu_custom_call" | custom-call | tf_op jit(solution)/shard_map/pallas_call | solution.py:282
  33.8 6.4 %all-to-all-start = ((f32[8,64,128]{2,1,0:T(8,128)}), f32[8,64,128]{2,1,0:T(8,128)S(1)}, u32[]{:S(2)}, u32[]{:S(2)}) async-start(f32[8,64,128]{2,1,0:T(8,128)} %bitcast.9), calls=%async_computation | async-start | bytes 524288 | tf_op jit(solution)/shard_map/all_to_all | solution.py:283
  40.2 2.0 %shard_map.52 = (f32[512,128]{1,0:T(8,128)S(1)}, f32[512,128]{1,0:T(8,128)S(1)}) custom-call(s32[1]{0:T(128)} %bitcast.chan, s32[1]{0:T(128)} %bitcast.1.along, s32[1]{0:T(128)} %bitcast.2.across, f32[27,32,64]{2,1,0:T(8,128)S(1)} %copy-done.2, f32[512,128]{1,0:T(8,128)S(1)} %bitcast.15, f32[128,128]{1,0:T(8,128)S(1)} %collective-permute-done.near_row, ...), custom_call_target="tpu_custom_call" | custom-call | flops 700000000 | bytes 4194304 | tf_op jit(solution)/shard_map/pallas_call | solution.py:315
  42.3 0.3 collective-permute-start.4
  42.5 7.1 %all-to-all-done = f32[8,64,128]{2,1,0:T(8,128)S(1)} async-done(((f32[8,64,128]{2,1,0:T(8,128)}), f32[8,64,128]{2,1,0:T(8,128)S(1)}, u32[]{:S(2)}, u32[]{:S(2)}) %all-to-all-start) | async-done | bytes 262176 | tf_op jit(solution)/shard_map/all_to_all | solution.py:283
  49.7 4.6 %collective-permute-start.11 = (f32[64,128]{1,0:T(8,128)S(1)}, f32[64,128]{1,0:T(8,128)S(1)}, u32[]{:S(2)}, u32[]{:S(2)}) collective-permute-start(f32[64,128]{1,0:T(8,128)S(1)} %shard_map.58.own), channel_id=1, source_target_pairs={{0,2},{2,0},{1,3},{3,1},{4,6},{6,4},{5,7},{7,5},{8,10},{10,8},{9,1... | collective-permute-start | bytes 98312 | tf_op jit(solution)/shard_map/ppermute | solution.py:19
  54.3 0.9 %collective-permute-done.11.other = f32[64,128]{1,0:T(8,128)S(1)} collective-permute-done((f32[64,128]{1,0:T(8,128)S(1)}, f32[64,128]{1,0:T(8,128)S(1)}, u32[]{:S(2)}, u32[]{:S(2)}) %collective-permute-start.11) | collective-permute-done | bytes 32800 | tf_op jit(solution)/shard_map/ppermute | solution.py:19
  55.3 3.2 %collective-permute-start.13 = (f32[128,128]{1,0:T(8,128)S(1)}, f32[128,128]{1,0:T(8,128)S(1)}, u32[]{:S(2)}, u32[]{:S(2)}) collective-permute-start(f32[128,128]{1,0:T(8,128)S(1)} %shard_map.59.own), channel_id=1, source_target_pairs={{0,16},{8,24},{16,0},{24,8},{1,17},{9,25},{17,1},{25,9},{2,18},{10... | collective-permute-start | bytes 196616 | tf_op jit(solution)/shard_map/ppermute | solution.py:271
  58.4 0.7 %collective-permute-start.14 = (f32[128,128]{1,0:T(8,128)S(1)}, f32[128,128]{1,0:T(8,128)S(1)}, u32[]{:S(2)}, u32[]{:S(2)}) collective-permute-start(f32[128,128]{1,0:T(8,128)S(1)} %shard_map.59.own), channel_id=1, source_target_pairs={{0,24},{8,16},{16,8},{24,0},{1,25},{9,17},{17,9},{25,1},{2,26},{10... | collective-permute-start | bytes 196616 | tf_op jit(solution)/shard_map/ppermute | solution.py:271
  59.1 0.7 %add.11 = f32[512,128]{1,0:T(8,128)} add(f32[512,128]{1,0:T(8,128)S(1)} %get-tuple-element.21, f32[512,128]{1,0:T(8,128)S(1)} %collective-permute-done.4) | non-fusion elementwise | flops 65536 | bytes 786432 | tf_op jit(solution)/shard_map/add | solution.py:318
  59.9 1.5 %collective-permute-done.13.two = f32[128,128]{1,0:T(8,128)S(1)} collective-permute-done((f32[128,128]{1,0:T(8,128)S(1)}, f32[128,128]{1,0:T(8,128)S(1)}, u32[]{:S(2)}, u32[]{:S(2)}) %collective-permute-start.13) | collective-permute-done | bytes 65568 | tf_op jit(solution)/shard_map/ppermute | solution.py:271
  61.4 1.5 %collective-permute-done.14.three = f32[128,128]{1,0:T(8,128)S(1)} collective-permute-done((f32[128,128]{1,0:T(8,128)S(1)}, f32[128,128]{1,0:T(8,128)S(1)}, u32[]{:S(2)}, u32[]{:S(2)}) %collective-permute-start.14) | collective-permute-done | bytes 65568 | tf_op jit(solution)/shard_map/ppermute | solution.py:271
  62.9 0.9 %shard_map.60 = f32[27,32,64]{2,1,0:T(8,128)} custom-call(s32[1]{0:T(128)} %bitcast.6.row, f32[128,128]{1,0:T(8,128)S(1)} %shard_map.59.own, f32[128,128]{1,0:T(8,128)S(1)} %collective-permute-done.12.one, f32[128,128]{1,0:T(8,128)S(1)} %collective-permute-done.13.two, f32[128,128]{1,0:T(8,128)S(1)} %collective-permute-done.14.three), custom_call_target="tpu_custom_call" | custom-call | tf_op jit(solution)/shard_map/pallas_call | solution.py:287
  (20 shorter events, 0.3 us)
Async XLA Ops:
  0.6 18.3 %collective-permute-start.5 = (f32[512,128]{1,0:T(8,128)}, f32[512,128]{1,0:T(8,128)S(1)}, u32[]{:S(2)}, u32[]{:S(2)}) collective-permute-start(f32[512,128]{1,0:T(8,128)} %bitcast.17), channel_id=1, source_target_pairs={{0,1},{1,0},{2,3},{3,2},{4,5},{5,4},{6,7},{7,6},{8,9},{9,8},{10,11... | collective-permute-start | bytes 786440 | tf_op jit(solution)/shard_map/ppermute | solution.py:19
  2.8 0.9 %copy-start = (f32[32,1,4,4,128]{4,3,2,1,0:T(4,128)S(1)}, f32[32,1,4,4,128]{4,3,2,1,0:T(4,128)}, u32[]{:S(2)}) copy-start(f32[32,1,4,4,128]{4,3,2,1,0:T(4,128)} %param.4) | copy-start | bytes 786436
  3.7 10.3 %copy-start.1 = (f32[32,1,4,4,128]{4,3,2,1,0:T(4,128)S(1)}, f32[32,1,4,4,128]{4,3,2,1,0:T(4,128)}, u32[]{:S(2)}) copy-start(f32[32,1,4,4,128]{4,3,2,1,0:T(4,128)} %param.4) | copy-start | bytes 786436
  3.8 15.2 %copy-start.3 = (f32[32,1,4,4,128]{4,3,2,1,0:T(4,128)S(1)}, f32[32,1,4,4,128]{4,3,2,1,0:T(4,128)}, u32[]{:S(2)}) copy-start(f32[32,1,4,4,128]{4,3,2,1,0:T(4,128)} %param.3) | copy-start | bytes 786436
  3.8 8.6 %collective-permute-start = (f32[128,128]{1,0:T(8,128)S(1)}, f32[128,128]{1,0:T(8,128)S(1)}, u32[]{:S(2)}, u32[]{:S(2)}) collective-permute-start(f32[128,128]{1,0:T(8,128)S(1)} %get-tuple-element.17), channel_id=1, source_target_pairs={{0,8},{16,24},{32,40},{48,56},{64,72},{80,88},{96,104},{112,120},{... | collective-permute-start | bytes 196616 | tf_op jit(solution)/shard_map/ppermute | solution.py:19
  5.2 8.8 %collective-permute-start.1 = (f32[128,128]{1,0:T(8,128)S(1)}, f32[128,128]{1,0:T(8,128)S(1)}, u32[]{:S(2)}, u32[]{:S(2)}) collective-permute-start(f32[128,128]{1,0:T(8,128)S(1)} %get-tuple-element.18), channel_id=1, source_target_pairs={{8,16},{24,32},{40,48},{56,64},{72,80},{88,96},{104,112},{120,128}... | collective-permute-start | bytes 196616 | tf_op jit(solution)/shard_map/ppermute | solution.py:19
  14.3 6.9 %collective-permute-start.2 = (f32[32,128]{1,0:T(8,128)S(1)}, f32[32,128]{1,0:T(8,128)S(1)}, u32[]{:S(2)}, u32[]{:S(2)}) collective-permute-start(f32[32,128]{1,0:T(8,128)S(1)} %get-tuple-element.19), channel_id=1, source_target_pairs={{0,2},{2,0},{1,3},{3,1},{4,6},{6,4},{5,7},{7,5},{8,10},{10,8},{9,1... | collective-permute-start | bytes 49160 | tf_op jit(solution)/shard_map/ppermute | solution.py:19
  16.5 4.7 %collective-permute-start.3 = (f32[32,128]{1,0:T(8,128)S(1)}, f32[32,128]{1,0:T(8,128)S(1)}, u32[]{:S(2)}, u32[]{:S(2)}) collective-permute-start(f32[32,128]{1,0:T(8,128)S(1)} %get-tuple-element.20), channel_id=1, source_target_pairs={{2,4},{6,0},{4,2},{0,6},{3,5},{7,1},{5,3},{1,7},{10,12},{14,8},{12... | collective-permute-start | bytes 49160 | tf_op jit(solution)/shard_map/ppermute | solution.py:19
  21.6 1.5 %collective-permute-start.6 = (f32[256,128]{1,0:T(8,128)S(1)}, f32[256,128]{1,0:T(8,128)S(1)}, u32[]{:S(2)}, u32[]{:S(2)}) collective-permute-start(f32[256,128]{1,0:T(8,128)S(1)} %get-tuple-element.27), channel_id=1, source_target_pairs={{0,2},{2,0},{1,3},{3,1},{4,6},{6,4},{5,7},{7,5},{8,10},{10,8},{9,1... | collective-permute-start | bytes 393224 | tf_op jit(solution)/shard_map/ppermute | solution.py:19
  23.1 3.9 %collective-permute-start.7 = (f32[64,128]{1,0:T(8,128)S(1)}, f32[64,128]{1,0:T(8,128)S(1)}, u32[]{:S(2)}, u32[]{:S(2)}) collective-permute-start(f32[64,128]{1,0:T(8,128)S(1)} %get-tuple-element.29), channel_id=1, source_target_pairs={{0,8},{8,0},{16,24},{24,16},{1,9},{9,1},{17,25},{25,17},{2,10},{10... | collective-permute-start | bytes 98312 | tf_op jit(solution)/shard_map/ppermute | solution.py:271
  23.2 4.4 %collective-permute-start.8 = (f32[64,128]{1,0:T(8,128)S(1)}, f32[64,128]{1,0:T(8,128)S(1)}, u32[]{:S(2)}, u32[]{:S(2)}) collective-permute-start(f32[64,128]{1,0:T(8,128)S(1)} %get-tuple-element.30), channel_id=1, source_target_pairs={{0,16},{8,24},{16,0},{24,8},{1,17},{9,25},{17,1},{25,9},{2,18},{10... | collective-permute-start | bytes 98312 | tf_op jit(solution)/shard_map/ppermute | solution.py:271
  23.3 5.4 %collective-permute-start.9 = (f32[64,128]{1,0:T(8,128)S(1)}, f32[64,128]{1,0:T(8,128)S(1)}, u32[]{:S(2)}, u32[]{:S(2)}) collective-permute-start(f32[64,128]{1,0:T(8,128)S(1)} %get-tuple-element.31), channel_id=1, source_target_pairs={{0,24},{8,16},{16,8},{24,0},{1,25},{9,17},{17,9},{25,1},{2,26},{10... | collective-permute-start | bytes 98312 | tf_op jit(solution)/shard_map/ppermute | solution.py:271
  28.7 11.5 %copy-start.2 = (f32[27,32,64]{2,1,0:T(8,128)S(1)}, f32[27,32,64]{2,1,0:T(8,128)}, u32[]{:S(2)}) copy-start(f32[27,32,64]{2,1,0:T(8,128)} %weights.1) | copy-start | bytes 663556
  28.7 4.4 %collective-permute-start.10 = (f32[64,128]{1,0:T(8,128)S(1)}, f32[64,128]{1,0:T(8,128)S(1)}, u32[]{:S(2)}, u32[]{:S(2)}) collective-permute-start(f32[64,128]{1,0:T(8,128)S(1)} %shard_map.56.own), channel_id=1, source_target_pairs={{0,4},{4,0},{1,5},{5,1},{2,6},{6,2},{3,7},{7,3},{8,12},{12,8},{9,1... | collective-permute-start | bytes 98312 | tf_op jit(solution)/shard_map/ppermute | solution.py:19
  33.8 15.8 %all-to-all-start = ((f32[8,64,128]{2,1,0:T(8,128)}), f32[8,64,128]{2,1,0:T(8,128)S(1)}, u32[]{:S(2)}, u32[]{:S(2)}) async-start(f32[8,64,128]{2,1,0:T(8,128)} %bitcast.9), calls=%async_computation | async-start | bytes 524288 | tf_op jit(solution)/shard_map/all_to_all | solution.py:283
  42.3 16.9 %collective-permute-start.4 = (f32[512,128]{1,0:T(8,128)S(1)}, f32[512,128]{1,0:T(8,128)S(1)}, u32[]{:S(2)}, u32[]{:S(2)}) collective-permute-start(f32[512,128]{1,0:T(8,128)S(1)} %get-tuple-element.22), channel_id=1, source_target_pairs={{0,1},{1,0},{2,3},{3,2},{4,5},{5,4},{6,7},{7,6},{8,9},{9,8},{10,11... | collective-permute-start | bytes 786440 | tf_op jit(solution)/shard_map/ppermute | solution.py:19
  49.7 5.5 %collective-permute-start.11 = (f32[64,128]{1,0:T(8,128)S(1)}, f32[64,128]{1,0:T(8,128)S(1)}, u32[]{:S(2)}, u32[]{:S(2)}) collective-permute-start(f32[64,128]{1,0:T(8,128)S(1)} %shard_map.58.own), channel_id=1, source_target_pairs={{0,2},{2,0},{1,3},{3,1},{4,6},{6,4},{5,7},{7,5},{8,10},{10,8},{9,1... | collective-permute-start | bytes 98312 | tf_op jit(solution)/shard_map/ppermute | solution.py:19
  55.2 4.7 %collective-permute-start.12 = (f32[128,128]{1,0:T(8,128)S(1)}, f32[128,128]{1,0:T(8,128)S(1)}, u32[]{:S(2)}, u32[]{:S(2)}) collective-permute-start(f32[128,128]{1,0:T(8,128)S(1)} %shard_map.59.own), channel_id=1, source_target_pairs={{0,8},{8,0},{16,24},{24,16},{1,9},{9,1},{17,25},{25,17},{2,10},{10... | collective-permute-start | bytes 196616 | tf_op jit(solution)/shard_map/ppermute | solution.py:271
  55.3 6.1 %collective-permute-start.13 = (f32[128,128]{1,0:T(8,128)S(1)}, f32[128,128]{1,0:T(8,128)S(1)}, u32[]{:S(2)}, u32[]{:S(2)}) collective-permute-start(f32[128,128]{1,0:T(8,128)S(1)} %shard_map.59.own), channel_id=1, source_target_pairs={{0,16},{8,24},{16,0},{24,8},{1,17},{9,25},{17,1},{25,9},{2,18},{10... | collective-permute-start | bytes 196616 | tf_op jit(solution)/shard_map/ppermute | solution.py:271
  58.4 4.5 %collective-permute-start.14 = (f32[128,128]{1,0:T(8,128)S(1)}, f32[128,128]{1,0:T(8,128)S(1)}, u32[]{:S(2)}, u32[]{:S(2)}) collective-permute-start(f32[128,128]{1,0:T(8,128)S(1)} %shard_map.59.own), channel_id=1, source_target_pairs={{0,24},{8,16},{16,8},{24,0},{1,25},{9,17},{17,9},{25,1},{2,26},{10... | collective-permute-start | bytes 196616 | tf_op jit(solution)/shard_map/ppermute | solution.py:271

commit v4 on v3

--- a/solution.py
+++ b/solution.py
@@ -24,22 +24,22 @@
     return high, (value - high.astype(F32)).astype(BF16)
 
 
-def rows_kernel(along, grad, near, far):
+def rows_kernel(along, grad, far, near):
     odd = is_odd(along)
     for z in range(4):
         top = grad[pl.ds(12 + z, CI, stride=16), :]
         bottom = grad[pl.ds(z, CI, stride=16), :]
+        far[pl.ds(z, CI, stride=4), :] = jnp.where(odd, top, bottom)
         near[pl.ds(z, CI, stride=4), :] = jnp.where(odd, bottom, top)
-        far[pl.ds(z, CI, stride=4), :] = jnp.where(odd, top, bottom)
-
-
-def edges_kernel(along, across, grad, near_row, far_row, to_core, to_chip):
+
+
+def edges_kernel(along, across, grad, far_row, near_row, to_chip, to_core):
     lane = lax.broadcasted_iota(jnp.int32, (CI, 128), 1)
     heads = jnp.zeros((CI, 128), F32)
     tails = jnp.zeros((CI, 128), F32)
     for xp in range(6):
         for z in range(4):
-            tile = extended(along, grad, near_row, far_row, xp, z)
+            tile = extended(along, grad, far_row, near_row, xp, z)
             at = 6 * xp + z + 1
             heads = jnp.where(lane == at, pltpu.roll(tile, at, 1), heads)
             tails = jnp.where(lane == at, pltpu.roll(tile, at + 1, 1), tails)
@@ -48,7 +48,7 @@
     to_chip[...] = jnp.where(odd, tails, heads)
 
 
-def extended(along, grad, near_row, far_row, xp, z):
+def extended(along, grad, far_row, near_row, xp, z):
     if 0 < xp < 5:
         return grad[pl.ds((xp - 1) * 4 + z, CI, stride=16), :]
     near = near_row[pl.ds(z, CI, stride=4), :]
@@ -61,7 +61,7 @@
     return (place[0] & 1) == 1
 
 
-def spread(along, grad, near_row, far_row, left, right, high, low):
+def spread(along, grad, far_row, near_row, left, right, high, low):
     lane = lax.broadcasted_iota(jnp.int32, (CI, 128), 1)
     zero = jnp.zeros((CI, 128), BF16)
     for xp in range(6):
@@ -70,7 +70,7 @@
                 ref[d, xp, :, 0:128] = zero
                 ref[d, xp, :, 640:768] = zero
         for z in range(4):
-            tile = extended(along, grad, near_row, far_row, xp, z)
+            tile = extended(along, grad, far_row, near_row, xp, z)
             before, after = pltpu.roll(tile, 1, 1), pltpu.roll(tile, 127, 1)
             if left is None:
                 before = jnp.where(lane == 0, 0.0, before)
@@ -102,9 +102,9 @@
 
 
 def filter_kernel(
-    chan, along, own, other, grad, near_row, far_row, total_out, first_out, last_out, high, low
+    chan, along, own, other, grad, far_row, near_row, total_out, first_out, last_out, high, low
 ):
-    spread(along, grad, near_row, far_row, None, None, high, low)
+    spread(along, grad, far_row, near_row, None, None, high, low)
     is_first = chan[0] == 0
     lane = lax.broadcasted_iota(jnp.int32, (64, 128), 1)
     heads = jnp.zeros((64, 128), F32)
@@ -130,7 +130,7 @@
     last_out[...] = tails
 
 
-def rims(across, from_core, from_chip):
+def rims(across, from_chip, from_core):
     odd = is_odd(across)
     left = jnp.where(odd, from_core[...], from_chip[...])
     right = jnp.where(odd, from_chip[...], from_core[...])
@@ -154,8 +154,8 @@
     return p[:, :64] + p[:, 64:] + q
 
 
-def rim_kernel(across, total, first, last, from_core, from_chip, keep, give):
-    left, right = rims(across, from_core, from_chip)
+def rim_kernel(across, total, first, last, from_chip, from_core, keep, give):
+    left, right = rims(across, from_chip, from_core)
     extra = {2: rim_taps(left, first[...]), 0: rim_taps(right, last[...])}
 
     def of_tap(tap):
@@ -168,20 +168,20 @@
         return value * (1.0 / 512.0)
 
     odd = is_odd(across)
-    for j in range(8):
+    for j in range(7):
         pairs = [
             jnp.concatenate([of_tap(2 * pair), of_tap(2 * pair + 1)], axis=1)
-            for pair in (j, j + 8)
+            for pair in (j, j + 7)
         ]
         keep[32 * j : 32 * j + 32, :] = jnp.where(odd, pairs[1], pairs[0])
         give[32 * j : 32 * j + 32, :] = jnp.where(odd, pairs[0], pairs[1])
 
 
 def data_kernel(
-    chan, along, across, weights, grad, near_row, far_row, from_core, from_chip, kept, sent, high, low
+    chan, along, across, weights, grad, far_row, near_row, from_chip, from_core, kept, sent, high, low
 ):
-    left, right = rims(across, from_core, from_chip)
-    spread(along, grad, near_row, far_row, left, right, high, low)
+    left, right = rims(across, from_chip, from_core)
+    spread(along, grad, far_row, near_row, left, right, high, low)
     w = weights[...].reshape(864, 64)
     w = jnp.where(chan[0] == 0, w, jnp.concatenate([w[:, 32:], w[:, :32]], axis=1))
     w_high = w.astype(BF16).astype(F32)
@@ -199,7 +199,7 @@
 
 
 def quarter(ref, index):
-    return ref[pl.ds(pl.multiple_of(index * 64, 64), 64), :]
+    return ref[pl.ds(pl.multiple_of(index * 56, 8), 56), :]
 
 
 def quarters_kernel(row, kept, received, own, one, two, three, both):
@@ -208,42 +208,46 @@
         out[...] = quarter(both, row[0] ^ bits)
 
 
-def sum_kernel(own, one, two, three, out):
+def sum_kernel(two, one, three, own, out):
     out[...] = (own[...] + one[...]) + (two[...] + three[...])
 
 
 def copies_kernel(own, other, out):
     total = own[...] + other[...]
     for j in range(8):
-        out[64 * j : 64 * j + 64, :] = total
+        out[56 * j : 56 * j + 56, :] = total
 
 
 def fold_kernel(pieces, out):
-    total = pieces[0:64, :]
+    total = pieces[0:56, :]
     for j in range(1, 8):
-        total = total + pieces[64 * j : 64 * j + 64, :]
+        total = total + pieces[56 * j : 56 * j + 56, :]
     out[...] = total
 
 
-def join_kernel(core, own, other, out):
-    at_left = core[0] == 0
-    out[0:64, :] = jnp.where(at_left, own[...], other[...])
-    out[64:128, :] = jnp.where(at_left, other[...], own[...])
-
-
-def unpack_kernel(row, own, one, two, three, out):
+def join_kernel(row, two, one, three, own, out):
     low_bit, high_bit = (row[0] & 1) == 0, (row[0] & 2) == 0
     refs = (own, one, two, three)
     for part in range(4):
         a, b, c, d = (refs[part ^ bits][...] for bits in range(4))
-        value = jnp.where(high_bit, jnp.where(low_bit, a, b), jnp.where(low_bit, c, d))
+        out[56 * part : 56 * part + 56, :] = jnp.where(
+            high_bit, jnp.where(low_bit, a, b), jnp.where(low_bit, c, d)
+        )
+
+
+def unpack_kernel(core, own, other, out):
+    odd = is_odd(core)
+    for j in range(7):
+        rows = slice(32 * j, 32 * j + 32)
+        halves = (
+            jnp.where(odd, other[rows, :], own[rows, :]),
+            jnp.where(odd, own[rows, :], other[rows, :]),
+        )
         for half in range(2):
-            for j in range(2):
-                pair = 8 * half + 2 * part + j
-                rows = value[64 * half + 32 * j : 64 * half + 32 * j + 32]
-                for k in range(2):
-                    if 2 * pair + k < 27:
-                        out[2 * pair + k, :, :] = rows[:, 64 * k : 64 * k + 64]
+            for k in range(2):
+                tap = 14 * half + 2 * j + k
+                if tap < 27:
+                    out[tap, :, :] = halves[half][:, 64 * k : 64 * k + 64]
 
 
 VMEM = pl.BlockSpec(memory_space=pltpu.VMEM)
@@ -267,24 +271,25 @@
     )
 
 
-def crossed(value, bits):
-    return lax.ppermute(value, "y", [(s, s ^ bits) for s in range(4)])
+def crossed(value, axis, bits):
+    return lax.ppermute(value, axis, [(s, s ^ bits) for s in range(lax.axis_size(axis))])
 
 
 def summed_over_tiles(keep, give):
     row, core = place("y"), place("c")
-    small = shape(64, 128)
+    small = shape(56, 128)
     own, one, two, three = call(
-        quarters_kernel, (small,) * 4, [SMEM, VMEM, VMEM], [pltpu.VMEM((256, 128), F32)]
+        quarters_kernel, (small,) * 4, [SMEM, VMEM, VMEM], [pltpu.VMEM((224, 128), F32)]
     )(row, keep, swapped(give, "c", 0))
-    two, one, three = crossed(two, 2), crossed(one, 1), crossed(three, 3)
-    part = call(sum_kernel, small, [VMEM] * 4)(own, one, two, three)
-    copies = call(copies_kernel, shape(512, 128), [VMEM] * 2)(part, swapped(part, "xh", 0))
-    copies = lax.all_to_all(copies, "z", 0, 0, tiled=True)
-    part = call(fold_kernel, small, [VMEM])(copies)
-    part = call(join_kernel, shape(128, 128), [SMEM, VMEM, VMEM])(core, part, swapped(part, "c", 0))
-    two, one, three = crossed(part, 2), crossed(part, 1), crossed(part, 3)
-    return call(unpack_kernel, shape(27, 32, 64), [SMEM] + [VMEM] * 4)(row, part, one, two, three)
+    two, one, three = (crossed(v, "y", bits) for v, bits in ((two, 2), (one, 1), (three, 3)))
+    part = call(sum_kernel, small, [VMEM] * 4)(two, one, three, own)
+    copies = call(copies_kernel, shape(448, 128), [VMEM] * 2)(part, swapped(part, "xh", 0))
+    part = call(fold_kernel, small, [VMEM])(lax.all_to_all(copies, "z", 0, 0, tiled=True))
+    two, one, three = (crossed(part, "y", bits) for bits in (2, 1, 3))
+    half = call(join_kernel, shape(224, 128), [SMEM] + [VMEM] * 4)(row, two, one, three, part)
+    return call(unpack_kernel, shape(27, 32, 64), [SMEM, VMEM, VMEM])(
+        core, half, swapped(half, "c", 0)
+    )
 
 
 def place(axis):
@@ -295,26 +300,26 @@
     act = activation.reshape(512, 128)
     grad = out_grad.reshape(512, 128)
     chan, along, across = place("chan"), place(ALONG_X), place(ALONG_Y)
+    to_far, to_near = call(rows_kernel, (shape(128, 128),) * 2, [SMEM, VMEM])(along, grad)
+    far_row = swapped(to_far, ALONG_X, 1)
     other = swapped(act, "chan", 0)
-    to_near, to_far = call(rows_kernel, (shape(128, 128),) * 2, [SMEM, VMEM])(along, grad)
-    far_row = swapped(to_far, ALONG_X, 1)
     near_row = swapped(to_near, ALONG_X, 0)
-    to_core, to_chip = call(edges_kernel, (shape(CI, 128),) * 2, [SMEM] * 2 + [VMEM] * 3)(
-        along, across, grad, near_row, far_row
-    )
+    to_chip, to_core = call(edges_kernel, (shape(CI, 128),) * 2, [SMEM] * 2 + [VMEM] * 3)(
+        along, across, grad, far_row, near_row
+    )
+    from_chip = swapped(to_chip, ALONG_Y, 1)
     from_core = swapped(to_core, "c", 0)
-    from_chip = swapped(to_chip, ALONG_Y, 1)
     halves = [pltpu.VMEM((3, 6, CI, 768), BF16)] * 2
     column = shape(64, 128)
     total, first, last = call(
         filter_kernel, (shape(864, 64), column, column), [SMEM] * 2 + [VMEM] * 5, halves, 700_000_000, 1 << 22
-    )(chan, along, act, other, grad, near_row, far_row)
-    keep, give = call(rim_kernel, (shape(256, 128),) * 2, [SMEM] + [VMEM] * 5)(
-        across, total, first, last, from_core, from_chip
+    )(chan, along, act, other, grad, far_row, near_row)
+    keep, give = call(rim_kernel, (shape(224, 128),) * 2, [SMEM] + [VMEM] * 5)(
+        across, total, first, last, from_chip, from_core
     )
     kept, sent = call(
         data_kernel, (shape(512, 128),) * 2, [SMEM] * 3 + [VMEM] * 6, halves, 700_000_000, 1 << 22
-    )(chan, along, across, kernel, grad, near_row, far_row, from_core, from_chip)
+    )(chan, along, across, kernel, grad, far_row, near_row, from_chip, from_core)
     input_grad = (kept + swapped(sent, "chan", 0)).reshape(activation.shape)
     kernel_grad = summed_over_tiles(keep, give)
     return (input_grad, kernel_grad)

time: 64 us -> 62 us (0.969)
  starting transfers between devices: 37.3 us -> 35.4 us
    all_to_all x1, starting transfers between devices: 6.4 us -> 4.71 us  [summed_over_tiles(): lax.all_to_all(copies, 'z', 0, 0, tiled=True)]
    ppermute x6, starting transfers between devices: 7.87 us -> 6.67 us  [crossed(): lax.ppermute(value, axis, [(s, s ^ bits) for s in range(lax.axis_size(axi...]
    ppermute x9, starting transfers between devices: 23.1 us -> 24 us  [swapped(): return lax.ppermute(value, axis, pairs + [(t, s) for s, t in pairs])]
    ppermute x9, waiting for transfers between devices: 5.58 us -> 6.51 us  [swapped(): return lax.ppermute(value, axis, pairs + [(t, s) for s, t in pairs])]
    ppermute x6, waiting for transfers between devices: 4.68 us -> 3.81 us  [crossed(): lax.ppermute(value, axis, [(s, s ^ bits) for s in range(lax.axis_size(axi...]
  transfers between devices with their start and end apart: 16 -> 16, of which waited for: 9 -> 10; matrix products, arithmetic and copies ran while one was open for 1% -> 1% of each run, Pallas kernels for 7% -> 7%
where the time goes in v4:
time: 62 us; the launch traced here: 61.8 us
  starting transfers between devices  35.4 us (57%)
  waiting for transfers between devices  17.3 us (28%)
  Pallas kernels  6.66 us (11%)
  local copies, waits for them, and re-layouts  0.96 us (2%)
  other arithmetic  0.73 us (1%)
  between operations  0.73 us (1%)
    ppermute x9, starting transfers between devices, swapped(): return lax.ppermute(value, axis, pairs + [(t, s) for s, t in pairs])  24 us
    all_to_all x1, waiting for transfers between devices, summed_over_tiles(): lax.all_to_all(copies, 'z', 0, 0, tiled=True)  6.97 us
    ppermute x6, starting transfers between devices, crossed(): lax.ppermute(value, axis, [(s, s ^ bits) for s in range(lax.axis_size(axi...  6.67 us
    ppermute x9, waiting for transfers between devices, swapped(): return lax.ppermute(value, axis, pairs + [(t, s) for s, t in pairs])  6.51 us
    all_to_all x1, starting transfers between devices, summed_over_tiles(): lax.all_to_all(copies, 'z', 0, 0, tiled=True)  4.71 us
    ppermute x6, waiting for transfers between devices, crossed(): lax.ppermute(value, axis, [(s, s ^ bits) for s in range(lax.axis_size(axi...  3.81 us
    pallas_call x1, Pallas kernels, body(): call(filter_kernel, (shape(864, 64), column, column), [SMEM] * 2 + [VMEM]...  2.22 us
    pallas_call x1, Pallas kernels, body(): call(data_kernel, (shape(512, 128),) * 2, [SMEM] * 3 + [VMEM] * 6, halves...  2.03 us
  transfers between devices with their start and end apart: 16, of which 10 were waited for; matrix products, arithmetic and copies ran while one was open for 1% of the time, Pallas kernels for 7%

profile of v4, /device:TPU:1, one launch (start us, length us, event | category | flops | bytes accessed | tf_op | source)
XLA Modules:
  0.0 61.8 jit_solution(11406224679845748474)
XLA Ops:
  0.6 2.1 %collective-permute-start.5 = (f32[512,128]{1,0:T(8,128)}, f32[512,128]{1,0:T(8,128)S(1)}, u32[]{:S(2)}, u32[]{:S(2)}) collective-permute-start(f32[512,128]{1,0:T(8,128)} %bitcast.17), channel_id=1, source_target_pairs={{0,1},{1,0},{2,3},{3,2},{4,5},{5,4},{6,7},{7,6},{8,9},{9,8},{10,11... | collective-permute-start | bytes 786440 | tf_op jit(solution)/shard_map/ppermute | solution.py:19
  2.8 0.9 %copy-done = f32[32,1,4,4,128]{4,3,2,1,0:T(4,128)S(1)} copy-done((f32[32,1,4,4,128]{4,3,2,1,0:T(4,128)S(1)}, f32[32,1,4,4,128]{4,3,2,1,0:T(4,128)}, u32[]{:S(2)}) %copy-start) | copy-done | bytes 262168
  3.8 8.1 %collective-permute-start = (f32[128,128]{1,0:T(8,128)S(1)}, f32[128,128]{1,0:T(8,128)S(1)}, u32[]{:S(2)}, u32[]{:S(2)}) collective-permute-start(f32[128,128]{1,0:T(8,128)S(1)} %get-tuple-element.17), channel_id=1, source_target_pairs={{8,16},{24,32},{40,48},{56,64},{72,80},{88,96},{104,112},{120,128}... | collective-permute-start | bytes 196616 | tf_op jit(solution)/shard_map/ppermute | solution.py:19
  11.9 1.7 %collective-permute-done.far_row = f32[128,128]{1,0:T(8,128)S(1)} collective-permute-done((f32[128,128]{1,0:T(8,128)S(1)}, f32[128,128]{1,0:T(8,128)S(1)}, u32[]{:S(2)}, u32[]{:S(2)}) %collective-permute-start) | collective-permute-done | bytes 65568 | tf_op jit(solution)/shard_map/ppermute | solution.py:19
  13.5 1.5 %collective-permute-done.1.near_row = f32[128,128]{1,0:T(8,128)S(1)} collective-permute-done((f32[128,128]{1,0:T(8,128)S(1)}, f32[128,128]{1,0:T(8,128)S(1)}, u32[]{:S(2)}, u32[]{:S(2)}) %collective-permute-start.1) | collective-permute-done | bytes 65568 | tf_op jit(solution)/shard_map/ppermute | solution.py:19
  15.0 0.3 shard_map.51
  15.3 4.8 %collective-permute-start.2 = (f32[32,128]{1,0:T(8,128)S(1)}, f32[32,128]{1,0:T(8,128)S(1)}, u32[]{:S(2)}, u32[]{:S(2)}) collective-permute-start(f32[32,128]{1,0:T(8,128)S(1)} %get-tuple-element.19), channel_id=1, source_target_pairs={{2,4},{6,0},{4,2},{0,6},{3,5},{7,1},{5,3},{1,7},{10,12},{14,8},{12... | collective-permute-start | bytes 49160 | tf_op jit(solution)/shard_map/ppermute | solution.py:19
  20.1 2.2 %shard_map.53 = (f32[864,64]{1,0:T(8,128)S(1)}, f32[64,128]{1,0:T(8,128)S(1)}, f32[64,128]{1,0:T(8,128)S(1)}) custom-call(s32[1]{0:T(128)} %bitcast.chan, s32[1]{0:T(128)} %bitcast.1.along, f32[512,128]{1,0:T(8,128)S(1)} %bitcast.18, f32[512,128]{1,0:T(8,128)S(1)} %collective-permute-done.5.other, f32[512,128]{1,0:T(8,128)S(1)} %bitcast.14, ...), custom_call_target="tpu_custom_call" | custom-call | flops 700000000 | bytes 4194304 | tf_op jit(solution)/shard_map/pallas_call | solution.py:314
  22.3 0.4 shard_map.54
  22.8 0.6 collective-permute-start.6
  23.4 1.0 %collective-permute-done.6.received = f32[224,128]{1,0:T(8,128)S(1)} collective-permute-done((f32[224,128]{1,0:T(8,128)S(1)}, f32[224,128]{1,0:T(8,128)S(1)}, u32[]{:S(2)}, u32[]{:S(2)}) %collective-permute-start.6) | collective-permute-done | bytes 114720 | tf_op jit(solution)/shard_map/ppermute | solution.py:19
  24.3 0.1 collective-permute-start.7
  24.4 0.1 collective-permute-start.8
  24.6 3.1 %collective-permute-start.9 = (f32[56,128]{1,0:T(8,128)S(1)}, f32[56,128]{1,0:T(8,128)S(1)}, u32[]{:S(2)}, u32[]{:S(2)}) collective-permute-start(f32[56,128]{1,0:T(8,128)S(1)} %get-tuple-element.30), channel_id=1, source_target_pairs={{0,24},{8,16},{16,8},{24,0},{1,25},{9,17},{17,9},{25,1},{2,26},{10... | collective-permute-start | bytes 86024 | tf_op jit(solution)/shard_map/ppermute | solution.py:275
  27.7 1.0 %collective-permute-done.7.two = f32[56,128]{1,0:T(8,128)S(1)} collective-permute-done((f32[56,128]{1,0:T(8,128)S(1)}, f32[56,128]{1,0:T(8,128)S(1)}, u32[]{:S(2)}, u32[]{:S(2)}) %collective-permute-start.7) | collective-permute-done | bytes 28704 | tf_op jit(solution)/shard_map/ppermute | solution.py:275
  28.7 0.3 collective-permute-done.9.three
  29.0 2.1 %collective-permute-start.10 = (f32[56,128]{1,0:T(8,128)S(1)}, f32[56,128]{1,0:T(8,128)S(1)}, u32[]{:S(2)}, u32[]{:S(2)}) collective-permute-start(f32[56,128]{1,0:T(8,128)S(1)} %shard_map.56.own), channel_id=1, source_target_pairs={{0,4},{4,0},{1,5},{5,1},{2,6},{6,2},{3,7},{7,3},{8,12},{12,8},{9,1... | collective-permute-start | bytes 86024 | tf_op jit(solution)/shard_map/ppermute | solution.py:19
  31.1 2.2 %collective-permute-done.10.other = f32[56,128]{1,0:T(8,128)S(1)} collective-permute-done((f32[56,128]{1,0:T(8,128)S(1)}, f32[56,128]{1,0:T(8,128)S(1)}, u32[]{:S(2)}, u32[]{:S(2)}) %collective-permute-start.10) | collective-permute-done | bytes 28704 | tf_op jit(solution)/shard_map/ppermute | solution.py:19
  33.3 0.7 %shard_map.57 = f32[448,128]{1,0:T(8,128)} custom-call(f32[56,128]{1,0:T(8,128)S(1)} %shard_map.56.own, f32[56,128]{1,0:T(8,128)S(1)} %collective-permute-done.10.other), custom_call_target="tpu_custom_call" | custom-call | tf_op jit(solution)/shard_map/pallas_call | solution.py:286
  34.0 4.7 %all-to-all-start = ((f32[8,56,128]{2,1,0:T(8,128)}), f32[8,56,128]{2,1,0:T(8,128)S(1)}, u32[]{:S(2)}, u32[]{:S(2)}) async-start(f32[8,56,128]{2,1,0:T(8,128)} %bitcast.9), calls=%async_computation | async-start | bytes 458752 | tf_op jit(solution)/shard_map/all_to_all | solution.py:287
  38.7 2.0 %shard_map.52 = (f32[512,128]{1,0:T(8,128)S(1)}, f32[512,128]{1,0:T(8,128)S(1)}) custom-call(s32[1]{0:T(128)} %bitcast.chan, s32[1]{0:T(128)} %bitcast.1.along, s32[1]{0:T(128)} %bitcast.2.across, f32[27,32,64]{2,1,0:T(8,128)S(1)} %copy-done.2, f32[512,128]{1,0:T(8,128)S(1)} %bitcast.15, f32[128,128]{1,0:T(8,128)S(1)} %collective-permute-done.far_row, ...), custom_call_target="tpu_custom_call" | custom-call | flops 700000000 | bytes 4194304 | tf_op jit(solution)/shard_map/pallas_call | solution.py:320
  40.8 0.1 collective-permute-start.4
  40.9 7.0 %all-to-all-done = f32[8,56,128]{2,1,0:T(8,128)S(1)} async-done(((f32[8,56,128]{2,1,0:T(8,128)}), f32[8,56,128]{2,1,0:T(8,128)S(1)}, u32[]{:S(2)}, u32[]{:S(2)}) %all-to-all-start) | async-done | bytes 229408 | tf_op jit(solution)/shard_map/all_to_all | solution.py:287
  47.9 0.1 collective-permute-start.11
  48.0 1.8 %collective-permute-start.12 = (f32[56,128]{1,0:T(8,128)S(1)}, f32[56,128]{1,0:T(8,128)S(1)}, u32[]{:S(2)}, u32[]{:S(2)}) collective-permute-start(f32[56,128]{1,0:T(8,128)S(1)} %shard_map.58.own), channel_id=1, source_target_pairs={{0,8},{8,0},{16,24},{24,16},{1,9},{9,1},{17,25},{25,17},{2,10},{10... | collective-permute-start | bytes 86024 | tf_op jit(solution)/shard_map/ppermute | solution.py:275
  49.8 1.4 %collective-permute-start.13 = (f32[56,128]{1,0:T(8,128)S(1)}, f32[56,128]{1,0:T(8,128)S(1)}, u32[]{:S(2)}, u32[]{:S(2)}) collective-permute-start(f32[56,128]{1,0:T(8,128)S(1)} %shard_map.58.own), channel_id=1, source_target_pairs={{0,24},{8,16},{16,8},{24,0},{1,25},{9,17},{17,9},{25,1},{2,26},{10... | collective-permute-start | bytes 86024 | tf_op jit(solution)/shard_map/ppermute | solution.py:275
  51.2 1.0 %collective-permute-done.11.two = f32[56,128]{1,0:T(8,128)S(1)} collective-permute-done((f32[56,128]{1,0:T(8,128)S(1)}, f32[56,128]{1,0:T(8,128)S(1)}, u32[]{:S(2)}, u32[]{:S(2)}) %collective-permute-start.11) | collective-permute-done | bytes 28704 | tf_op jit(solution)/shard_map/ppermute | solution.py:275
  52.2 1.6 %collective-permute-done.13.three = f32[56,128]{1,0:T(8,128)S(1)} collective-permute-done((f32[56,128]{1,0:T(8,128)S(1)}, f32[56,128]{1,0:T(8,128)S(1)}, u32[]{:S(2)}, u32[]{:S(2)}) %collective-permute-start.13) | collective-permute-done | bytes 28704 | tf_op jit(solution)/shard_map/ppermute | solution.py:275
  53.7 6.2 %collective-permute-start.14 = (f32[224,128]{1,0:T(8,128)S(1)}, f32[224,128]{1,0:T(8,128)S(1)}, u32[]{:S(2)}, u32[]{:S(2)}) collective-permute-start(f32[224,128]{1,0:T(8,128)S(1)} %shard_map.59.own), channel_id=1, source_target_pairs={{0,2},{2,0},{1,3},{3,1},{4,6},{6,4},{5,7},{7,5},{8,10},{10,8},{9,1... | collective-permute-start | bytes 344072 | tf_op jit(solution)/shard_map/ppermute | solution.py:19
  59.9 0.7 %add.11 = f32[512,128]{1,0:T(8,128)} add(f32[512,128]{1,0:T(8,128)S(1)} %get-tuple-element.21, f32[512,128]{1,0:T(8,128)S(1)} %collective-permute-done.4) | non-fusion elementwise | flops 65536 | bytes 786432 | tf_op jit(solution)/shard_map/add | solution.py:323
  60.7 0.2 collective-permute-done.14.other
  60.9 0.9 %shard_map.60 = f32[27,32,64]{2,1,0:T(8,128)} custom-call(s32[1]{0:T(128)} %bitcast.6.core, f32[224,128]{1,0:T(8,128)S(1)} %shard_map.59.own, f32[224,128]{1,0:T(8,128)S(1)} %collective-permute-done.14.other), custom_call_target="tpu_custom_call" | custom-call | tf_op jit(solution)/shard_map/pallas_call | solution.py:290
  (20 shorter events, 0.1 us)
Async XLA Ops:
  0.6 19.5 %collective-permute-start.5 = (f32[512,128]{1,0:T(8,128)}, f32[512,128]{1,0:T(8,128)S(1)}, u32[]{:S(2)}, u32[]{:S(2)}) collective-permute-start(f32[512,128]{1,0:T(8,128)} %bitcast.17), channel_id=1, source_target_pairs={{0,1},{1,0},{2,3},{3,2},{4,5},{5,4},{6,7},{7,6},{8,9},{9,8},{10,11... | collective-permute-start | bytes 786440 | tf_op jit(solution)/shard_map/ppermute | solution.py:19
  2.8 0.9 %copy-start = (f32[32,1,4,4,128]{4,3,2,1,0:T(4,128)S(1)}, f32[32,1,4,4,128]{4,3,2,1,0:T(4,128)}, u32[]{:S(2)}) copy-start(f32[32,1,4,4,128]{4,3,2,1,0:T(4,128)} %param.4) | copy-start | bytes 786436
  3.7 11.3 %copy-start.1 = (f32[32,1,4,4,128]{4,3,2,1,0:T(4,128)S(1)}, f32[32,1,4,4,128]{4,3,2,1,0:T(4,128)}, u32[]{:S(2)}) copy-start(f32[32,1,4,4,128]{4,3,2,1,0:T(4,128)} %param.4) | copy-start | bytes 786436
  3.8 16.3 %copy-start.3 = (f32[32,1,4,4,128]{4,3,2,1,0:T(4,128)S(1)}, f32[32,1,4,4,128]{4,3,2,1,0:T(4,128)}, u32[]{:S(2)}) copy-start(f32[32,1,4,4,128]{4,3,2,1,0:T(4,128)} %param.3) | copy-start | bytes 786436
  3.8 9.8 %collective-permute-start = (f32[128,128]{1,0:T(8,128)S(1)}, f32[128,128]{1,0:T(8,128)S(1)}, u32[]{:S(2)}, u32[]{:S(2)}) collective-permute-start(f32[128,128]{1,0:T(8,128)S(1)} %get-tuple-element.17), channel_id=1, source_target_pairs={{8,16},{24,32},{40,48},{56,64},{72,80},{88,96},{104,112},{120,128}... | collective-permute-start | bytes 196616 | tf_op jit(solution)/shard_map/ppermute | solution.py:19
  11.9 3.1 %collective-permute-start.1 = (f32[128,128]{1,0:T(8,128)S(1)}, f32[128,128]{1,0:T(8,128)S(1)}, u32[]{:S(2)}, u32[]{:S(2)}) collective-permute-start(f32[128,128]{1,0:T(8,128)S(1)} %get-tuple-element.18), channel_id=1, source_target_pairs={{0,8},{16,24},{32,40},{48,56},{64,72},{80,88},{96,104},{112,120},{... | collective-permute-start | bytes 196616 | tf_op jit(solution)/shard_map/ppermute | solution.py:19
  15.3 7.0 %collective-permute-start.2 = (f32[32,128]{1,0:T(8,128)S(1)}, f32[32,128]{1,0:T(8,128)S(1)}, u32[]{:S(2)}, u32[]{:S(2)}) collective-permute-start(f32[32,128]{1,0:T(8,128)S(1)} %get-tuple-element.19), channel_id=1, source_target_pairs={{2,4},{6,0},{4,2},{0,6},{3,5},{7,1},{5,3},{1,7},{10,12},{14,8},{12... | collective-permute-start | bytes 49160 | tf_op jit(solution)/shard_map/ppermute | solution.py:19
  20.1 2.2 %collective-permute-start.3 = (f32[32,128]{1,0:T(8,128)S(1)}, f32[32,128]{1,0:T(8,128)S(1)}, u32[]{:S(2)}, u32[]{:S(2)}) collective-permute-start(f32[32,128]{1,0:T(8,128)S(1)} %get-tuple-element.20), channel_id=1, source_target_pairs={{0,2},{2,0},{1,3},{3,1},{4,6},{6,4},{5,7},{7,5},{8,10},{10,8},{9,1... | collective-permute-start | bytes 49160 | tf_op jit(solution)/shard_map/ppermute | solution.py:19
  22.8 1.6 %collective-permute-start.6 = (f32[224,128]{1,0:T(8,128)S(1)}, f32[224,128]{1,0:T(8,128)S(1)}, u32[]{:S(2)}, u32[]{:S(2)}) collective-permute-start(f32[224,128]{1,0:T(8,128)S(1)} %get-tuple-element.27), channel_id=1, source_target_pairs={{0,2},{2,0},{1,3},{3,1},{4,6},{6,4},{5,7},{7,5},{8,10},{10,8},{9,1... | collective-permute-start | bytes 344072 | tf_op jit(solution)/shard_map/ppermute | solution.py:19
  24.3 4.3 %collective-permute-start.7 = (f32[56,128]{1,0:T(8,128)S(1)}, f32[56,128]{1,0:T(8,128)S(1)}, u32[]{:S(2)}, u32[]{:S(2)}) collective-permute-start(f32[56,128]{1,0:T(8,128)S(1)} %get-tuple-element.28), channel_id=1, source_target_pairs={{0,16},{8,24},{16,0},{24,8},{1,17},{9,25},{17,1},{25,9},{2,18},{10... | collective-permute-start | bytes 86024 | tf_op jit(solution)/shard_map/ppermute | solution.py:275
  24.4 4.2 %collective-permute-start.8 = (f32[56,128]{1,0:T(8,128)S(1)}, f32[56,128]{1,0:T(8,128)S(1)}, u32[]{:S(2)}, u32[]{:S(2)}) collective-permute-start(f32[56,128]{1,0:T(8,128)S(1)} %get-tuple-element.29), channel_id=1, source_target_pairs={{0,8},{8,0},{16,24},{24,16},{1,9},{9,1},{17,25},{25,17},{2,10},{10... | collective-permute-start | bytes 86024 | tf_op jit(solution)/shard_map/ppermute | solution.py:275
  24.6 4.4 %collective-permute-start.9 = (f32[56,128]{1,0:T(8,128)S(1)}, f32[56,128]{1,0:T(8,128)S(1)}, u32[]{:S(2)}, u32[]{:S(2)}) collective-permute-start(f32[56,128]{1,0:T(8,128)S(1)} %get-tuple-element.30), channel_id=1, source_target_pairs={{0,24},{8,16},{16,8},{24,0},{1,25},{9,17},{17,9},{25,1},{2,26},{10... | collective-permute-start | bytes 86024 | tf_op jit(solution)/shard_map/ppermute | solution.py:275
  29.0 9.7 %copy-start.2 = (f32[27,32,64]{2,1,0:T(8,128)S(1)}, f32[27,32,64]{2,1,0:T(8,128)}, u32[]{:S(2)}) copy-start(f32[27,32,64]{2,1,0:T(8,128)} %weights.1) | copy-start | bytes 663556
  29.0 4.3 %collective-permute-start.10 = (f32[56,128]{1,0:T(8,128)S(1)}, f32[56,128]{1,0:T(8,128)S(1)}, u32[]{:S(2)}, u32[]{:S(2)}) collective-permute-start(f32[56,128]{1,0:T(8,128)S(1)} %shard_map.56.own), channel_id=1, source_target_pairs={{0,4},{4,0},{1,5},{5,1},{2,6},{6,2},{3,7},{7,3},{8,12},{12,8},{9,1... | collective-permute-start | bytes 86024 | tf_op jit(solution)/shard_map/ppermute | solution.py:19
  34.0 13.8 %all-to-all-start = ((f32[8,56,128]{2,1,0:T(8,128)}), f32[8,56,128]{2,1,0:T(8,128)S(1)}, u32[]{:S(2)}, u32[]{:S(2)}) async-start(f32[8,56,128]{2,1,0:T(8,128)} %bitcast.9), calls=%async_computation | async-start | bytes 458752 | tf_op jit(solution)/shard_map/all_to_all | solution.py:287
  40.8 19.2 %collective-permute-start.4 = (f32[512,128]{1,0:T(8,128)S(1)}, f32[512,128]{1,0:T(8,128)S(1)}, u32[]{:S(2)}, u32[]{:S(2)}) collective-permute-start(f32[512,128]{1,0:T(8,128)S(1)} %get-tuple-element.22), channel_id=1, source_target_pairs={{0,1},{1,0},{2,3},{3,2},{4,5},{5,4},{6,7},{7,6},{8,9},{9,8},{10,11... | collective-permute-start | bytes 786440 | tf_op jit(solution)/shard_map/ppermute | solution.py:19
  47.9 4.3 %collective-permute-start.11 = (f32[56,128]{1,0:T(8,128)S(1)}, f32[56,128]{1,0:T(8,128)S(1)}, u32[]{:S(2)}, u32[]{:S(2)}) collective-permute-start(f32[56,128]{1,0:T(8,128)S(1)} %shard_map.58.own), channel_id=1, source_target_pairs={{0,16},{8,24},{16,0},{24,8},{1,17},{9,25},{17,1},{25,9},{2,18},{10... | collective-permute-start | bytes 86024 | tf_op jit(solution)/shard_map/ppermute | solution.py:275
  48.0 4.2 %collective-permute-start.12 = (f32[56,128]{1,0:T(8,128)S(1)}, f32[56,128]{1,0:T(8,128)S(1)}, u32[]{:S(2)}, u32[]{:S(2)}) collective-permute-start(f32[56,128]{1,0:T(8,128)S(1)} %shard_map.58.own), channel_id=1, source_target_pairs={{0,8},{8,0},{16,24},{24,16},{1,9},{9,1},{17,25},{25,17},{2,10},{10... | collective-permute-start | bytes 86024 | tf_op jit(solution)/shard_map/ppermute | solution.py:275
  49.8 3.9 %collective-permute-start.13 = (f32[56,128]{1,0:T(8,128)S(1)}, f32[56,128]{1,0:T(8,128)S(1)}, u32[]{:S(2)}, u32[]{:S(2)}) collective-permute-start(f32[56,128]{1,0:T(8,128)S(1)} %shard_map.58.own), channel_id=1, source_target_pairs={{0,24},{8,16},{16,8},{24,0},{1,25},{9,17},{17,9},{25,1},{2,26},{10... | collective-permute-start | bytes 86024 | tf_op jit(solution)/shard_map/ppermute | solution.py:275
  53.7 7.1 %collective-permute-start.14 = (f32[224,128]{1,0:T(8,128)S(1)}, f32[224,128]{1,0:T(8,128)S(1)}, u32[]{:S(2)}, u32[]{:S(2)}) collective-permute-start(f32[224,128]{1,0:T(8,128)S(1)} %shard_map.59.own), channel_id=1, source_target_pairs={{0,2},{2,0},{1,3},{3,1},{4,6},{6,4},{5,7},{7,5},{8,10},{10,8},{9,1... | collective-permute-start | bytes 344072 | tf_op jit(solution)/shard_map/ppermute | solution.py:19

commit v5 on v4

--- a/solution.py
+++ b/solution.py
@@ -178,7 +178,7 @@
 
 
 def data_kernel(
-    chan, along, across, weights, grad, far_row, near_row, from_chip, from_core, kept, sent, high, low
+    chan, along, across, after, weights, grad, far_row, near_row, from_chip, from_core, kept, sent, high, low
 ):
     left, right = rims(across, from_chip, from_core)
     spread(along, grad, far_row, near_row, left, right, high, low)
@@ -198,6 +198,10 @@
             sent[pl.ds(x * 4 + z, CI, stride=16), :] = tile[32:]
 
 
+def gate_kernel(value, after, out):
+    out[...] = value[...]
+
+
 def quarter(ref, index):
     return ref[pl.ds(pl.multiple_of(index * 56, 8), 56), :]
 
@@ -208,24 +212,11 @@
         out[...] = quarter(both, row[0] ^ bits)
 
 
-def sum_kernel(two, one, three, own, out):
+def sum_kernel(two, three, one, own, out):
     out[...] = (own[...] + one[...]) + (two[...] + three[...])
 
 
-def copies_kernel(own, other, out):
-    total = own[...] + other[...]
-    for j in range(8):
-        out[56 * j : 56 * j + 56, :] = total
-
-
-def fold_kernel(pieces, out):
-    total = pieces[0:56, :]
-    for j in range(1, 8):
-        total = total + pieces[56 * j : 56 * j + 56, :]
-    out[...] = total
-
-
-def join_kernel(row, two, one, three, own, out):
+def join_kernel(row, two, three, one, own, out):
     low_bit, high_bit = (row[0] & 1) == 0, (row[0] & 2) == 0
     refs = (own, one, two, three)
     for part in range(4):
@@ -235,7 +226,12 @@
         )
 
 
-def unpack_kernel(core, own, other, out):
+def add_kernel(one, two, out, done):
+    out[...] = one[...] + two[...]
+    done[...] = one[0:8, :]
+
+
+def unpack_kernel(core, own, other, after, out):
     odd = is_odd(core)
     for j in range(7):
         rows = slice(32 * j, 32 * j + 32)
@@ -275,20 +271,29 @@
     return lax.ppermute(value, axis, [(s, s ^ bits) for s in range(lax.axis_size(axis))])
 
 
-def summed_over_tiles(keep, give):
-    row, core = place("y"), place("c")
+def summed_near(keep, give):
+    row = place("y")
     small = shape(56, 128)
     own, one, two, three = call(
         quarters_kernel, (small,) * 4, [SMEM, VMEM, VMEM], [pltpu.VMEM((224, 128), F32)]
     )(row, keep, swapped(give, "c", 0))
-    two, one, three = (crossed(v, "y", bits) for v, bits in ((two, 2), (one, 1), (three, 3)))
-    part = call(sum_kernel, small, [VMEM] * 4)(two, one, three, own)
-    copies = call(copies_kernel, shape(448, 128), [VMEM] * 2)(part, swapped(part, "xh", 0))
-    part = call(fold_kernel, small, [VMEM])(lax.all_to_all(copies, "z", 0, 0, tiled=True))
-    two, one, three = (crossed(part, "y", bits) for bits in (2, 1, 3))
-    half = call(join_kernel, shape(224, 128), [SMEM] + [VMEM] * 4)(row, two, one, three, part)
-    return call(unpack_kernel, shape(27, 32, 64), [SMEM, VMEM, VMEM])(
-        core, half, swapped(half, "c", 0)
+    two, three, one = (crossed(v, "y", bits) for v, bits in ((two, 2), (three, 3), (one, 1)))
+    return call(sum_kernel, small, [VMEM] * 4)(two, three, one, own)
+
+
+def summed_far(part):
+    part = part + swapped(part, "xh", 0)
+    parts = [crossed(part, "z", bits) for bits in (3, 2, 1)]
+    part = call(sum_kernel, shape(56, 128), [VMEM] * 4)(*parts, part)
+    return part + crossed(part, "z", 6)
+
+
+def gathered(part, done):
+    row, core = place("y"), place("c")
+    two, three, one = (crossed(part, "y", bits) for bits in (2, 3, 1))
+    half = call(join_kernel, shape(224, 128), [SMEM] + [VMEM] * 4)(row, two, three, one, part)
+    return call(unpack_kernel, shape(27, 32, 64), [SMEM, VMEM, VMEM, VMEM])(
+        core, half, swapped(half, "c", 0), done
     )
 
 
@@ -317,11 +322,17 @@
     keep, give = call(rim_kernel, (shape(224, 128),) * 2, [SMEM] + [VMEM] * 5)(
         across, total, first, last, from_chip, from_core
     )
+    part = summed_near(keep, give)
     kept, sent = call(
-        data_kernel, (shape(512, 128),) * 2, [SMEM] * 3 + [VMEM] * 6, halves, 700_000_000, 1 << 22
-    )(chan, along, across, kernel, grad, far_row, near_row, from_chip, from_core)
-    input_grad = (kept + swapped(sent, "chan", 0)).reshape(activation.shape)
-    kernel_grad = summed_over_tiles(keep, give)
+        data_kernel, (shape(512, 128),) * 2, [SMEM] * 3 + [VMEM] * 7, halves, 700_000_000, 1 << 22
+    )(chan, along, across, part, kernel, grad, far_row, near_row, from_chip, from_core)
+    part = summed_far(part)
+    sent = call(gate_kernel, shape(512, 128), [VMEM] * 2)(sent, part)
+    input_grad, done = call(add_kernel, (shape(512, 128), shape(8, 128)), [VMEM] * 2)(
+        kept, swapped(sent, "chan", 0)
+    )
+    input_grad = input_grad.reshape(activation.shape)
+    kernel_grad = gathered(part, done)
     return (input_grad, kernel_grad)
 
 

time: 62 us -> 59.1 us (0.953)
  waiting for transfers between devices: 17.3 us -> 13.3 us
  starting transfers between devices: 35.4 us -> 37.3 us
  other arithmetic: 0.73 us -> 0.01 us
    all_to_all x1 -> x0, waiting for transfers between devices: 6.97 us -> none  [summed_over_tiles(): lax.all_to_all(copies, 'z', 0, 0, tiled=True)]
    ppermute x6 -> x10, starting transfers between devices: 6.67 us -> 12 us  [crossed(): lax.ppermute(value, axis, [(s, s ^ bits) for s in range(lax.axis_size(axi...]
    all_to_all x1 -> x0, starting transfers between devices: 4.71 us -> none  [summed_over_tiles(): lax.all_to_all(copies, 'z', 0, 0, tiled=True)]
    ppermute x6 -> x10, waiting for transfers between devices: 3.81 us -> 6.78 us  [crossed(): lax.ppermute(value, axis, [(s, s ^ bits) for s in range(lax.axis_size(axi...]
    ppermute x9, starting transfers between devices: 24 us -> 25.3 us  [swapped(): return lax.ppermute(value, axis, pairs + [(t, s) for s, t in pairs])]
    add x1 -> x2, other arithmetic: 0.73 us -> 0.01 us  [the longest x1 0.01 us: summed_far(): part = part + swapped(part, 'xh', 0)]
    pallas_call x7 -> x8, Pallas kernels: 3.69 us -> 3.73 us  [the longest x1 2.03 us: body(): call(data_kernel, (shape(512, 128),) * 2, [SMEM] * 3 + [VMEM] * 7, halves...]
  transfers between devices with their start and end apart: 16 -> 19, of which waited for: 10 -> 12; matrix products, arithmetic and copies ran while one was open for 1% -> 0% of each run, Pallas kernels for 7% -> 9%
where the time goes in v5:
time: 59.1 us; the launch traced here: 59 us
  starting transfers between devices  37.3 us (63%)
  waiting for transfers between devices  13.3 us (23%)
  Pallas kernels  6.69 us (11%)
  local copies, waits for them, and re-layouts  0.97 us (2%)
  between operations  0.75 us (1%)
    ppermute x9, starting transfers between devices, swapped(): return lax.ppermute(value, axis, pairs + [(t, s) for s, t in pairs])  25.3 us
    ppermute x10, starting transfers between devices, crossed(): lax.ppermute(value, axis, [(s, s ^ bits) for s in range(lax.axis_size(axi...  12 us
    ppermute x10, waiting for transfers between devices, crossed(): lax.ppermute(value, axis, [(s, s ^ bits) for s in range(lax.axis_size(axi...  6.78 us
    ppermute x9, waiting for transfers between devices, swapped(): return lax.ppermute(value, axis, pairs + [(t, s) for s, t in pairs])  6.51 us
    pallas_call x1, Pallas kernels, body(): call(filter_kernel, (shape(864, 64), column, column), [SMEM] * 2 + [VMEM]...  2.22 us
    pallas_call x1, Pallas kernels, body(): call(data_kernel, (shape(512, 128),) * 2, [SMEM] * 3 + [VMEM] * 7, halves...  2.03 us
  transfers between devices with their start and end apart: 19, of which 12 were waited for; matrix products, arithmetic and copies ran while one was open for 0% of the time, Pallas kernels for 9%

profile of v5, /device:TPU:1, one launch (start us, length us, event | category | flops | bytes accessed | tf_op | source)
XLA Modules:
  0.0 59.0 jit_solution(957440504798979306)
XLA Ops:
  0.6 2.1 %collective-permute-start = (f32[512,128]{1,0:T(8,128)}, f32[512,128]{1,0:T(8,128)S(1)}, u32[]{:S(2)}, u32[]{:S(2)}) collective-permute-start(f32[512,128]{1,0:T(8,128)} %bitcast.14), channel_id=1, source_target_pairs={{0,1},{1,0},{2,3},{3,2},{4,5},{5,4},{6,7},{7,6},{8,9},{9,8},{10,11... | collective-permute-start | bytes 786440 | tf_op jit(solution)/shard_map/ppermute | solution.py:19
  2.8 0.9 %copy-done = f32[32,1,4,4,128]{4,3,2,1,0:T(4,128)S(1)} copy-done((f32[32,1,4,4,128]{4,3,2,1,0:T(4,128)S(1)}, f32[32,1,4,4,128]{4,3,2,1,0:T(4,128)}, u32[]{:S(2)}) %copy-start) | copy-done | bytes 262168
  3.8 8.1 %collective-permute-start.1 = (f32[128,128]{1,0:T(8,128)S(1)}, f32[128,128]{1,0:T(8,128)S(1)}, u32[]{:S(2)}, u32[]{:S(2)}) collective-permute-start(f32[128,128]{1,0:T(8,128)S(1)} %get-tuple-element.19), channel_id=1, source_target_pairs={{8,16},{24,32},{40,48},{56,64},{72,80},{88,96},{104,112},{120,128}... | collective-permute-start | bytes 196616 | tf_op jit(solution)/shard_map/ppermute | solution.py:19
  11.9 1.7 %collective-permute-done.1.far_row = f32[128,128]{1,0:T(8,128)S(1)} collective-permute-done((f32[128,128]{1,0:T(8,128)S(1)}, f32[128,128]{1,0:T(8,128)S(1)}, u32[]{:S(2)}, u32[]{:S(2)}) %collective-permute-start.1) | collective-permute-done | bytes 65568 | tf_op jit(solution)/shard_map/ppermute | solution.py:19
  13.5 1.5 %collective-permute-done.2.near_row = f32[128,128]{1,0:T(8,128)S(1)} collective-permute-done((f32[128,128]{1,0:T(8,128)S(1)}, f32[128,128]{1,0:T(8,128)S(1)}, u32[]{:S(2)}, u32[]{:S(2)}) %collective-permute-start.2) | collective-permute-done | bytes 65568 | tf_op jit(solution)/shard_map/ppermute | solution.py:19
  15.0 0.3 shard_map.52
  15.3 4.8 %collective-permute-start.3 = (f32[32,128]{1,0:T(8,128)S(1)}, f32[32,128]{1,0:T(8,128)S(1)}, u32[]{:S(2)}, u32[]{:S(2)}) collective-permute-start(f32[32,128]{1,0:T(8,128)S(1)} %get-tuple-element.24), channel_id=1, source_target_pairs={{2,4},{6,0},{4,2},{0,6},{3,5},{7,1},{5,3},{1,7},{10,12},{14,8},{12... | collective-permute-start | bytes 49160 | tf_op jit(solution)/shard_map/ppermute | solution.py:19
  20.1 2.2 %shard_map.51 = (f32[864,64]{1,0:T(8,128)S(1)}, f32[64,128]{1,0:T(8,128)S(1)}, f32[64,128]{1,0:T(8,128)S(1)}) custom-call(s32[1]{0:T(128)} %bitcast.chan, s32[1]{0:T(128)} %bitcast.1.along, f32[512,128]{1,0:T(8,128)S(1)} %bitcast.15, f32[512,128]{1,0:T(8,128)S(1)} %collective-permute-done.other, f32[512,128]{1,0:T(8,128)S(1)} %bitcast.12, ...), custom_call_target="tpu_custom_call" | custom-call | flops 700000000 | bytes 4194304 | tf_op jit(solution)/shard_map/pallas_call | solution.py:319
  22.3 0.4 shard_map.53
  22.8 0.6 %collective-permute-start.5 = (f32[224,128]{1,0:T(8,128)S(1)}, f32[224,128]{1,0:T(8,128)S(1)}, u32[]{:S(2)}, u32[]{:S(2)}) collective-permute-start(f32[224,128]{1,0:T(8,128)S(1)} %get-tuple-element.27), channel_id=1, source_target_pairs={{0,2},{2,0},{1,3},{3,1},{4,6},{6,4},{5,7},{7,5},{8,10},{10,8},{9,1... | collective-permute-start | bytes 344072 | tf_op jit(solution)/shard_map/ppermute | solution.py:19
  23.4 1.0 %collective-permute-done.5.received = f32[224,128]{1,0:T(8,128)S(1)} collective-permute-done((f32[224,128]{1,0:T(8,128)S(1)}, f32[224,128]{1,0:T(8,128)S(1)}, u32[]{:S(2)}, u32[]{:S(2)}) %collective-permute-start.5) | collective-permute-done | bytes 114720 | tf_op jit(solution)/shard_map/ppermute | solution.py:19
  24.5 2.1 %collective-permute-start.7 = (f32[56,128]{1,0:T(8,128)S(1)}, f32[56,128]{1,0:T(8,128)S(1)}, u32[]{:S(2)}, u32[]{:S(2)}) collective-permute-start(f32[56,128]{1,0:T(8,128)S(1)} %get-tuple-element.29), channel_id=1, source_target_pairs={{0,24},{8,16},{16,8},{24,0},{1,25},{9,17},{17,9},{25,1},{2,26},{10... | collective-permute-start | bytes 86024 | tf_op jit(solution)/shard_map/ppermute | solution.py:271
  26.6 0.5 collective-permute-start.8
  27.1 1.7 %collective-permute-done.6.two = f32[56,128]{1,0:T(8,128)S(1)} collective-permute-done((f32[56,128]{1,0:T(8,128)S(1)}, f32[56,128]{1,0:T(8,128)S(1)}, u32[]{:S(2)}, u32[]{:S(2)}) %collective-permute-start.6) | collective-permute-done | bytes 28704 | tf_op jit(solution)/shard_map/ppermute | solution.py:271
  28.8 0.8 %collective-permute-done.8.one = f32[56,128]{1,0:T(8,128)S(1)} collective-permute-done((f32[56,128]{1,0:T(8,128)S(1)}, f32[56,128]{1,0:T(8,128)S(1)}, u32[]{:S(2)}, u32[]{:S(2)}) %collective-permute-start.8) | collective-permute-done | bytes 28704 | tf_op jit(solution)/shard_map/ppermute | solution.py:271
  29.6 2.1 %collective-permute-start.9 = (f32[56,128]{1,0:T(8,128)S(1)}, f32[56,128]{1,0:T(8,128)S(1)}, u32[]{:S(2)}, u32[]{:S(2)}) collective-permute-start(f32[56,128]{1,0:T(8,128)S(1)} %shard_map.55.after), channel_id=1, source_target_pairs={{0,4},{4,0},{1,5},{5,1},{2,6},{6,2},{3,7},{7,3},{8,12},{12,8},{9,1... | collective-permute-start | bytes 86024 | tf_op jit(solution)/shard_map/ppermute | solution.py:19
  31.7 2.2 %collective-permute-done.9 = f32[56,128]{1,0:T(8,128)S(1)} collective-permute-done((f32[56,128]{1,0:T(8,128)S(1)}, f32[56,128]{1,0:T(8,128)S(1)}, u32[]{:S(2)}, u32[]{:S(2)}) %collective-permute-start.9) | collective-permute-done | bytes 28704 | tf_op jit(solution)/shard_map/ppermute | solution.py:19
  33.9 0.1 collective-permute-start.11
  34.0 3.4 %collective-permute-start.12 = (f32[56,128]{1,0:T(8,128)S(1)}, f32[56,128]{1,0:T(8,128)S(1)}, u32[]{:S(2)}, u32[]{:S(2)}) collective-permute-start(f32[56,128]{1,0:T(8,128)S(1)} %add.14.own), channel_id=1, source_target_pairs={{0,32},{32,0},{64,96},{96,64},{128,160},{160,128},{192,224},{224,1... | collective-permute-start | bytes 86024 | tf_op jit(solution)/shard_map/ppermute | solution.py:271
  37.5 1.0 %collective-permute-done.10.two = f32[56,128]{1,0:T(8,128)S(1)} collective-permute-done((f32[56,128]{1,0:T(8,128)S(1)}, f32[56,128]{1,0:T(8,128)S(1)}, u32[]{:S(2)}, u32[]{:S(2)}) %collective-permute-start.10) | collective-permute-done | bytes 28704 | tf_op jit(solution)/shard_map/ppermute | solution.py:271
  38.4 0.3 collective-permute-done.12.one
  38.8 2.9 %collective-permute-start.13 = (f32[56,128]{1,0:T(8,128)S(1)}, f32[56,128]{1,0:T(8,128)S(1)}, u32[]{:S(2)}, u32[]{:S(2)}) collective-permute-start(f32[56,128]{1,0:T(8,128)S(1)} %shard_map.57), channel_id=1, source_target_pairs={{0,192},{32,224},{64,128},{96,160},{128,64},{160,96},{192,0},{224,... | collective-permute-start | bytes 86024 | tf_op jit(solution)/shard_map/ppermute | solution.py:271
  41.6 2.0 %shard_map.56 = (f32[512,128]{1,0:T(8,128)S(1)}, f32[512,128]{1,0:T(8,128)S(1)}) custom-call(s32[1]{0:T(128)} %bitcast.chan, s32[1]{0:T(128)} %bitcast.1.along, s32[1]{0:T(128)} %bitcast.2.across, f32[56,128]{1,0:T(8,128)S(1)} %shard_map.55.after, f32[27,32,64]{2,1,0:T(8,128)S(1)} %copy-done.2, f32[512,128]{1,0:T(8,128)S(1)} %bitcast.13, ...), custom_call_target="tpu_custom_call" | custom-call | flops 700000000 | bytes 4194304 | tf_op jit(solution)/shard_map/pallas_call | solution.py:326
  43.7 0.2 collective-permute-done.13
  44.0 1.8 %collective-permute-start.15 = (f32[56,128]{1,0:T(8,128)S(1)}, f32[56,128]{1,0:T(8,128)S(1)}, u32[]{:S(2)}, u32[]{:S(2)}) collective-permute-start(f32[56,128]{1,0:T(8,128)S(1)} %add.15.after.own), channel_id=1, source_target_pairs={{0,16},{8,24},{16,0},{24,8},{1,17},{9,25},{17,1},{25,9},{2,18},{10... | collective-permute-start | bytes 86024 | tf_op jit(solution)/shard_map/ppermute | solution.py:271
  45.8 1.1 %collective-permute-start.16 = (f32[56,128]{1,0:T(8,128)S(1)}, f32[56,128]{1,0:T(8,128)S(1)}, u32[]{:S(2)}, u32[]{:S(2)}) collective-permute-start(f32[56,128]{1,0:T(8,128)S(1)} %add.15.after.own), channel_id=1, source_target_pairs={{0,24},{8,16},{16,8},{24,0},{1,25},{9,17},{17,9},{25,1},{2,26},{10... | collective-permute-start | bytes 86024 | tf_op jit(solution)/shard_map/ppermute | solution.py:271
  46.8 1.5 %collective-permute-done.15.two = f32[56,128]{1,0:T(8,128)S(1)} collective-permute-done((f32[56,128]{1,0:T(8,128)S(1)}, f32[56,128]{1,0:T(8,128)S(1)}, u32[]{:S(2)}, u32[]{:S(2)}) %collective-permute-start.15) | collective-permute-done | bytes 28704 | tf_op jit(solution)/shard_map/ppermute | solution.py:271
  48.3 1.4 %collective-permute-done.16.three = f32[56,128]{1,0:T(8,128)S(1)} collective-permute-done((f32[56,128]{1,0:T(8,128)S(1)}, f32[56,128]{1,0:T(8,128)S(1)}, u32[]{:S(2)}, u32[]{:S(2)}) %collective-permute-start.16) | collective-permute-done | bytes 28704 | tf_op jit(solution)/shard_map/ppermute | solution.py:271
  49.7 7.4 %collective-permute-start.18 = (f32[224,128]{1,0:T(8,128)S(1)}, f32[224,128]{1,0:T(8,128)S(1)}, u32[]{:S(2)}, u32[]{:S(2)}) collective-permute-start(f32[224,128]{1,0:T(8,128)S(1)} %shard_map.60.own), channel_id=1, source_target_pairs={{0,2},{2,0},{1,3},{3,1},{4,6},{6,4},{5,7},{7,5},{8,10},{10,8},{9,1... | collective-permute-start | bytes 344072 | tf_op jit(solution)/shard_map/ppermute | solution.py:19
  57.1 0.7 %shard_map.59 = (f32[512,128]{1,0:T(8,128)}, f32[8,128]{1,0:T(8,128)S(1)}) custom-call(f32[512,128]{1,0:T(8,128)S(1)} %get-tuple-element.32.one, f32[512,128]{1,0:T(8,128)S(1)} %collective-permute-done.14.two), custom_call_target="tpu_custom_call" | custom-call | tf_op jit(solution)/shard_map/pallas_call | solution.py:331
  57.9 0.2 collective-permute-done.18.other
  58.1 0.9 %shard_map.61 = f32[27,32,64]{2,1,0:T(8,128)} custom-call(s32[1]{0:T(128)} %bitcast.8.core, f32[224,128]{1,0:T(8,128)S(1)} %shard_map.60.own, f32[224,128]{1,0:T(8,128)S(1)} %collective-permute-done.18.other, f32[8,128]{1,0:T(8,128)S(1)} %get-tuple-element.35.after), custom_call_target="tpu_custom_call" | custom-call | tf_op jit(solution)/shard_map/pallas_call | solution.py:295
  (28 shorter events, 0.4 us)
Async XLA Ops:
  0.6 19.5 %collective-permute-start = (f32[512,128]{1,0:T(8,128)}, f32[512,128]{1,0:T(8,128)S(1)}, u32[]{:S(2)}, u32[]{:S(2)}) collective-permute-start(f32[512,128]{1,0:T(8,128)} %bitcast.14), channel_id=1, source_target_pairs={{0,1},{1,0},{2,3},{3,2},{4,5},{5,4},{6,7},{7,6},{8,9},{9,8},{10,11... | collective-permute-start | bytes 786440 | tf_op jit(solution)/shard_map/ppermute | solution.py:19
  2.8 0.9 %copy-start = (f32[32,1,4,4,128]{4,3,2,1,0:T(4,128)S(1)}, f32[32,1,4,4,128]{4,3,2,1,0:T(4,128)}, u32[]{:S(2)}) copy-start(f32[32,1,4,4,128]{4,3,2,1,0:T(4,128)} %param.4) | copy-start | bytes 786436
  3.7 11.3 %copy-start.1 = (f32[32,1,4,4,128]{4,3,2,1,0:T(4,128)S(1)}, f32[32,1,4,4,128]{4,3,2,1,0:T(4,128)}, u32[]{:S(2)}) copy-start(f32[32,1,4,4,128]{4,3,2,1,0:T(4,128)} %param.4) | copy-start | bytes 786436
  3.8 16.3 %copy-start.3 = (f32[32,1,4,4,128]{4,3,2,1,0:T(4,128)S(1)}, f32[32,1,4,4,128]{4,3,2,1,0:T(4,128)}, u32[]{:S(2)}) copy-start(f32[32,1,4,4,128]{4,3,2,1,0:T(4,128)} %param.3) | copy-start | bytes 786436
  3.8 9.8 %collective-permute-start.1 = (f32[128,128]{1,0:T(8,128)S(1)}, f32[128,128]{1,0:T(8,128)S(1)}, u32[]{:S(2)}, u32[]{:S(2)}) collective-permute-start(f32[128,128]{1,0:T(8,128)S(1)} %get-tuple-element.19), channel_id=1, source_target_pairs={{8,16},{24,32},{40,48},{56,64},{72,80},{88,96},{104,112},{120,128}... | collective-permute-start | bytes 196616 | tf_op jit(solution)/shard_map/ppermute | solution.py:19
  11.9 3.1 %collective-permute-start.2 = (f32[128,128]{1,0:T(8,128)S(1)}, f32[128,128]{1,0:T(8,128)S(1)}, u32[]{:S(2)}, u32[]{:S(2)}) collective-permute-start(f32[128,128]{1,0:T(8,128)S(1)} %get-tuple-element.20), channel_id=1, source_target_pairs={{0,8},{16,24},{32,40},{48,56},{64,72},{80,88},{96,104},{112,120},{... | collective-permute-start | bytes 196616 | tf_op jit(solution)/shard_map/ppermute | solution.py:19
  15.3 7.0 %collective-permute-start.3 = (f32[32,128]{1,0:T(8,128)S(1)}, f32[32,128]{1,0:T(8,128)S(1)}, u32[]{:S(2)}, u32[]{:S(2)}) collective-permute-start(f32[32,128]{1,0:T(8,128)S(1)} %get-tuple-element.24), channel_id=1, source_target_pairs={{2,4},{6,0},{4,2},{0,6},{3,5},{7,1},{5,3},{1,7},{10,12},{14,8},{12... | collective-permute-start | bytes 49160 | tf_op jit(solution)/shard_map/ppermute | solution.py:19
  20.1 2.2 %collective-permute-start.4 = (f32[32,128]{1,0:T(8,128)S(1)}, f32[32,128]{1,0:T(8,128)S(1)}, u32[]{:S(2)}, u32[]{:S(2)}) collective-permute-start(f32[32,128]{1,0:T(8,128)S(1)} %get-tuple-element.25), channel_id=1, source_target_pairs={{0,2},{2,0},{1,3},{3,1},{4,6},{6,4},{5,7},{7,5},{8,10},{10,8},{9,1... | collective-permute-start | bytes 49160 | tf_op jit(solution)/shard_map/ppermute | solution.py:19
  22.8 18.9 %copy-start.2 = (f32[27,32,64]{2,1,0:T(8,128)S(1)}, f32[27,32,64]{2,1,0:T(8,128)}, u32[]{:S(2)}) copy-start(f32[27,32,64]{2,1,0:T(8,128)} %weights.1) | copy-start | bytes 663556
  22.8 1.6 %collective-permute-start.5 = (f32[224,128]{1,0:T(8,128)S(1)}, f32[224,128]{1,0:T(8,128)S(1)}, u32[]{:S(2)}, u32[]{:S(2)}) collective-permute-start(f32[224,128]{1,0:T(8,128)S(1)} %get-tuple-element.27), channel_id=1, source_target_pairs={{0,2},{2,0},{1,3},{3,1},{4,6},{6,4},{5,7},{7,5},{8,10},{10,8},{9,1... | collective-permute-start | bytes 344072 | tf_op jit(solution)/shard_map/ppermute | solution.py:19
  24.4 4.4 %collective-permute-start.6 = (f32[56,128]{1,0:T(8,128)S(1)}, f32[56,128]{1,0:T(8,128)S(1)}, u32[]{:S(2)}, u32[]{:S(2)}) collective-permute-start(f32[56,128]{1,0:T(8,128)S(1)} %get-tuple-element.28), channel_id=1, source_target_pairs={{0,16},{8,24},{16,0},{24,8},{1,17},{9,25},{17,1},{25,9},{2,18},{10... | collective-permute-start | bytes 86024 | tf_op jit(solution)/shard_map/ppermute | solution.py:271
  24.5 4.3 %collective-permute-start.7 = (f32[56,128]{1,0:T(8,128)S(1)}, f32[56,128]{1,0:T(8,128)S(1)}, u32[]{:S(2)}, u32[]{:S(2)}) collective-permute-start(f32[56,128]{1,0:T(8,128)S(1)} %get-tuple-element.29), channel_id=1, source_target_pairs={{0,24},{8,16},{16,8},{24,0},{1,25},{9,17},{17,9},{25,1},{2,26},{10... | collective-permute-start | bytes 86024 | tf_op jit(solution)/shard_map/ppermute | solution.py:271
  26.6 3.0 %collective-permute-start.8 = (f32[56,128]{1,0:T(8,128)S(1)}, f32[56,128]{1,0:T(8,128)S(1)}, u32[]{:S(2)}, u32[]{:S(2)}) collective-permute-start(f32[56,128]{1,0:T(8,128)S(1)} %get-tuple-element.30), channel_id=1, source_target_pairs={{0,8},{8,0},{16,24},{24,16},{1,9},{9,1},{17,25},{25,17},{2,10},{10... | collective-permute-start | bytes 86024 | tf_op jit(solution)/shard_map/ppermute | solution.py:271
  29.6 4.3 %collective-permute-start.9 = (f32[56,128]{1,0:T(8,128)S(1)}, f32[56,128]{1,0:T(8,128)S(1)}, u32[]{:S(2)}, u32[]{:S(2)}) collective-permute-start(f32[56,128]{1,0:T(8,128)S(1)} %shard_map.55.after), channel_id=1, source_target_pairs={{0,4},{4,0},{1,5},{5,1},{2,6},{6,2},{3,7},{7,3},{8,12},{12,8},{9,1... | collective-permute-start | bytes 86024 | tf_op jit(solution)/shard_map/ppermute | solution.py:19
  33.9 4.5 %collective-permute-start.10 = (f32[56,128]{1,0:T(8,128)S(1)}, f32[56,128]{1,0:T(8,128)S(1)}, u32[]{:S(2)}, u32[]{:S(2)}) collective-permute-start(f32[56,128]{1,0:T(8,128)S(1)} %add.14.own), channel_id=1, source_target_pairs={{0,96},{32,64},{64,32},{96,0},{128,224},{160,192},{192,160},{224,1... | collective-permute-start | bytes 86024 | tf_op jit(solution)/shard_map/ppermute | solution.py:271
  33.9 4.5 %collective-permute-start.11 = (f32[56,128]{1,0:T(8,128)S(1)}, f32[56,128]{1,0:T(8,128)S(1)}, u32[]{:S(2)}, u32[]{:S(2)}) collective-permute-start(f32[56,128]{1,0:T(8,128)S(1)} %add.14.own), channel_id=1, source_target_pairs={{0,64},{32,96},{64,0},{96,32},{128,192},{160,224},{192,128},{224,1... | collective-permute-start | bytes 86024 | tf_op jit(solution)/shard_map/ppermute | solution.py:271
  34.0 4.7 %collective-permute-start.12 = (f32[56,128]{1,0:T(8,128)S(1)}, f32[56,128]{1,0:T(8,128)S(1)}, u32[]{:S(2)}, u32[]{:S(2)}) collective-permute-start(f32[56,128]{1,0:T(8,128)S(1)} %add.14.own), channel_id=1, source_target_pairs={{0,32},{32,0},{64,96},{96,64},{128,160},{160,128},{192,224},{224,1... | collective-permute-start | bytes 86024 | tf_op jit(solution)/shard_map/ppermute | solution.py:271
  38.8 5.1 %collective-permute-start.13 = (f32[56,128]{1,0:T(8,128)S(1)}, f32[56,128]{1,0:T(8,128)S(1)}, u32[]{:S(2)}, u32[]{:S(2)}) collective-permute-start(f32[56,128]{1,0:T(8,128)S(1)} %shard_map.57), channel_id=1, source_target_pairs={{0,192},{32,224},{64,128},{96,160},{128,64},{160,96},{192,0},{224,... | collective-permute-start | bytes 86024 | tf_op jit(solution)/shard_map/ppermute | solution.py:271
  43.9 13.3 %collective-permute-start.14 = (f32[512,128]{1,0:T(8,128)S(1)}, f32[512,128]{1,0:T(8,128)S(1)}, u32[]{:S(2)}, u32[]{:S(2)}) collective-permute-start(f32[512,128]{1,0:T(8,128)S(1)} %shard_map.58), channel_id=1, source_target_pairs={{0,1},{1,0},{2,3},{3,2},{4,5},{5,4},{6,7},{7,6},{8,9},{9,8},{10,11... | collective-permute-start | bytes 786440 | tf_op jit(solution)/shard_map/ppermute | solution.py:19
  44.0 4.3 %collective-permute-start.15 = (f32[56,128]{1,0:T(8,128)S(1)}, f32[56,128]{1,0:T(8,128)S(1)}, u32[]{:S(2)}, u32[]{:S(2)}) collective-permute-start(f32[56,128]{1,0:T(8,128)S(1)} %add.15.after.own), channel_id=1, source_target_pairs={{0,16},{8,24},{16,0},{24,8},{1,17},{9,25},{17,1},{25,9},{2,18},{10... | collective-permute-start | bytes 86024 | tf_op jit(solution)/shard_map/ppermute | solution.py:271
  45.8 3.9 %collective-permute-start.16 = (f32[56,128]{1,0:T(8,128)S(1)}, f32[56,128]{1,0:T(8,128)S(1)}, u32[]{:S(2)}, u32[]{:S(2)}) collective-permute-start(f32[56,128]{1,0:T(8,128)S(1)} %add.15.after.own), channel_id=1, source_target_pairs={{0,24},{8,16},{16,8},{24,0},{1,25},{9,17},{17,9},{25,1},{2,26},{10... | collective-permute-start | bytes 86024 | tf_op jit(solution)/shard_map/ppermute | solution.py:271
  46.8 2.8 %collective-permute-start.17 = (f32[56,128]{1,0:T(8,128)S(1)}, f32[56,128]{1,0:T(8,128)S(1)}, u32[]{:S(2)}, u32[]{:S(2)}) collective-permute-start(f32[56,128]{1,0:T(8,128)S(1)} %add.15.after.own), channel_id=1, source_target_pairs={{0,8},{8,0},{16,24},{24,16},{1,9},{9,1},{17,25},{25,17},{2,10},{10... | collective-permute-start | bytes 86024 | tf_op jit(solution)/shard_map/ppermute | solution.py:271
  49.7 8.4 %collective-permute-start.18 = (f32[224,128]{1,0:T(8,128)S(1)}, f32[224,128]{1,0:T(8,128)S(1)}, u32[]{:S(2)}, u32[]{:S(2)}) collective-permute-start(f32[224,128]{1,0:T(8,128)S(1)} %shard_map.60.own), channel_id=1, source_target_pairs={{0,2},{2,0},{1,3},{3,1},{4,6},{6,4},{5,7},{7,5},{8,10},{10,8},{9,1... | collective-permute-start | bytes 344072 | tf_op jit(solution)/shard_map/ppermute | solution.py:19

commit v6 on v5

--- a/solution.py
+++ b/solution.py
@@ -212,11 +212,11 @@
         out[...] = quarter(both, row[0] ^ bits)
 
 
-def sum_kernel(two, three, one, own, out):
+def sum_kernel(three, two, one, own, out):
     out[...] = (own[...] + one[...]) + (two[...] + three[...])
 
 
-def join_kernel(row, two, three, one, own, out):
+def join_kernel(row, three, two, one, own, out):
     low_bit, high_bit = (row[0] & 1) == 0, (row[0] & 2) == 0
     refs = (own, one, two, three)
     for part in range(4):
@@ -267,34 +267,40 @@
     )
 
 
-def crossed(value, axis, bits):
+def crossed(value, bits):
+    axis = ("z", "y", "xh")
     return lax.ppermute(value, axis, [(s, s ^ bits) for s in range(lax.axis_size(axis))])
 
 
 def summed_near(keep, give):
-    row = place("y")
     small = shape(56, 128)
     own, one, two, three = call(
         quarters_kernel, (small,) * 4, [SMEM, VMEM, VMEM], [pltpu.VMEM((224, 128), F32)]
-    )(row, keep, swapped(give, "c", 0))
-    two, three, one = (crossed(v, "y", bits) for v, bits in ((two, 2), (three, 3), (one, 1)))
-    return call(sum_kernel, small, [VMEM] * 4)(two, three, one, own)
+    )(quarter_place(), keep, swapped(give, "c", 0))
+    three, two, one = (crossed(v, bits) for v, bits in ((three, 10), (two, 8), (one, 2)))
+    return call(sum_kernel, small, [VMEM] * 4)(three, two, one, own)
 
 
 def summed_far(part):
-    part = part + swapped(part, "xh", 0)
-    parts = [crossed(part, "z", bits) for bits in (3, 2, 1)]
-    part = call(sum_kernel, shape(56, 128), [VMEM] * 4)(*parts, part)
-    return part + crossed(part, "z", 6)
+    for steps in ((7, 1, 6), (32, 48, 16)):
+        parts = [crossed(part, bits) for bits in steps]
+        part = call(sum_kernel, shape(56, 128), [VMEM] * 4)(*parts, part)
+    return part
 
 
 def gathered(part, done):
-    row, core = place("y"), place("c")
-    two, three, one = (crossed(part, "y", bits) for bits in (2, 3, 1))
-    half = call(join_kernel, shape(224, 128), [SMEM] + [VMEM] * 4)(row, two, three, one, part)
+    three, two, one = (crossed(part, bits) for bits in (10, 8, 2))
+    half = call(join_kernel, shape(224, 128), [SMEM] + [VMEM] * 4)(
+        quarter_place(), three, two, one, part
+    )
     return call(unpack_kernel, shape(27, 32, 64), [SMEM, VMEM, VMEM, VMEM])(
-        core, half, swapped(half, "c", 0), done
-    )
+        place("c"), half, swapped(half, "c", 0), done
+    )
+
+
+def quarter_place():
+    y, z = place("y"), place("z")
+    return ((y ^ (y >> 1)) & 1) + 2 * (z & 1)
 
 
 def place(axis):

time: 59.1 us -> 56.6 us (0.958)
  waiting for transfers between devices: 13.3 us -> 9.27 us
  starting transfers between devices: 37.3 us -> 38.8 us
    ppermute x10 -> x12, starting transfers between devices: 12 us -> 16.7 us  [crossed(): lax.ppermute(value, axis, [(s, s ^ bits) for s in range(lax.axis_size(axi...]
    ppermute x9 -> x8, starting transfers between devices: 25.3 us -> 22.2 us  [swapped(): return lax.ppermute(value, axis, pairs + [(t, s) for s, t in pairs])]
    ppermute x9 -> x8, waiting for transfers between devices: 6.51 us -> 4.32 us  [swapped(): return lax.ppermute(value, axis, pairs + [(t, s) for s, t in pairs])]
    ppermute x10 -> x12, waiting for transfers between devices: 6.78 us -> 4.95 us  [crossed(): lax.ppermute(value, axis, [(s, s ^ bits) for s in range(lax.axis_size(axi...]
  transfers between devices with their start and end apart: 19 -> 20, of which waited for: 12 -> 11; matrix products, arithmetic and copies ran while one was open for 0% -> 0% of each run, Pallas kernels for 9% -> 9%
where the time goes in v6:
time: 56.6 us; the launch traced here: 56.5 us
  starting transfers between devices  38.8 us (69%)
  waiting for transfers between devices  9.27 us (16%)
  Pallas kernels  6.69 us (12%)
  local copies, waits for them, and re-layouts  0.97 us (2%)
  between operations  0.76 us (1%)
    ppermute x8, starting transfers between devices, swapped(): return lax.ppermute(value, axis, pairs + [(t, s) for s, t in pairs])  22.2 us
    ppermute x12, starting transfers between devices, crossed(): lax.ppermute(value, axis, [(s, s ^ bits) for s in range(lax.axis_size(axi...  16.7 us
    ppermute x12, waiting for transfers between devices, crossed(): lax.ppermute(value, axis, [(s, s ^ bits) for s in range(lax.axis_size(axi...  4.95 us
    ppermute x8, waiting for transfers between devices, swapped(): return lax.ppermute(value, axis, pairs + [(t, s) for s, t in pairs])  4.32 us
    pallas_call x1, Pallas kernels, body(): call(filter_kernel, (shape(864, 64), column, column), [SMEM] * 2 + [VMEM]...  2.22 us
    pallas_call x1, Pallas kernels, body(): call(data_kernel, (shape(512, 128),) * 2, [SMEM] * 3 + [VMEM] * 7, halves...  2.02 us
  transfers between devices with their start and end apart: 20, of which 11 were waited for; matrix products, arithmetic and copies ran while one was open for 0% of the time, Pallas kernels for 9%

profile of v6, /device:TPU:1, one launch (start us, length us, event | category | flops | bytes accessed | tf_op | source)
XLA Modules:
  0.0 56.5 jit_solution(5904113364599986420)
XLA Ops:
  0.6 2.1 %collective-permute-start = (f32[512,128]{1,0:T(8,128)}, f32[512,128]{1,0:T(8,128)S(1)}, u32[]{:S(2)}, u32[]{:S(2)}) collective-permute-start(f32[512,128]{1,0:T(8,128)} %bitcast.15), channel_id=1, source_target_pairs={{0,1},{1,0},{2,3},{3,2},{4,5},{5,4},{6,7},{7,6},{8,9},{9,8},{10,11... | collective-permute-start | bytes 786440 | tf_op jit(solution)/shard_map/ppermute | solution.py:19
  2.8 0.9 %copy-done = f32[32,1,4,4,128]{4,3,2,1,0:T(4,128)S(1)} copy-done((f32[32,1,4,4,128]{4,3,2,1,0:T(4,128)S(1)}, f32[32,1,4,4,128]{4,3,2,1,0:T(4,128)}, u32[]{:S(2)}) %copy-start) | copy-done | bytes 262168
  3.8 8.1 %collective-permute-start.1 = (f32[128,128]{1,0:T(8,128)S(1)}, f32[128,128]{1,0:T(8,128)S(1)}, u32[]{:S(2)}, u32[]{:S(2)}) collective-permute-start(f32[128,128]{1,0:T(8,128)S(1)} %get-tuple-element.19), channel_id=1, source_target_pairs={{8,16},{24,32},{40,48},{56,64},{72,80},{88,96},{104,112},{120,128}... | collective-permute-start | bytes 196616 | tf_op jit(solution)/shard_map/ppermute | solution.py:19
  11.9 1.7 %collective-permute-done.1.far_row = f32[128,128]{1,0:T(8,128)S(1)} collective-permute-done((f32[128,128]{1,0:T(8,128)S(1)}, f32[128,128]{1,0:T(8,128)S(1)}, u32[]{:S(2)}, u32[]{:S(2)}) %collective-permute-start.1) | collective-permute-done | bytes 65568 | tf_op jit(solution)/shard_map/ppermute | solution.py:19
  13.5 1.5 %collective-permute-done.2.near_row = f32[128,128]{1,0:T(8,128)S(1)} collective-permute-done((f32[128,128]{1,0:T(8,128)S(1)}, f32[128,128]{1,0:T(8,128)S(1)}, u32[]{:S(2)}, u32[]{:S(2)}) %collective-permute-start.2) | collective-permute-done | bytes 65568 | tf_op jit(solution)/shard_map/ppermute | solution.py:19
  15.0 0.3 shard_map.52
  15.3 4.8 %collective-permute-start.3 = (f32[32,128]{1,0:T(8,128)S(1)}, f32[32,128]{1,0:T(8,128)S(1)}, u32[]{:S(2)}, u32[]{:S(2)}) collective-permute-start(f32[32,128]{1,0:T(8,128)S(1)} %get-tuple-element.24), channel_id=1, source_target_pairs={{2,4},{6,0},{4,2},{0,6},{3,5},{7,1},{5,3},{1,7},{10,12},{14,8},{12... | collective-permute-start | bytes 49160 | tf_op jit(solution)/shard_map/ppermute | solution.py:19
  20.1 2.2 %shard_map.51 = (f32[864,64]{1,0:T(8,128)S(1)}, f32[64,128]{1,0:T(8,128)S(1)}, f32[64,128]{1,0:T(8,128)S(1)}) custom-call(s32[1]{0:T(128)} %bitcast.chan, s32[1]{0:T(128)} %bitcast.1.along, f32[512,128]{1,0:T(8,128)S(1)} %bitcast.16, f32[512,128]{1,0:T(8,128)S(1)} %collective-permute-done.other, f32[512,128]{1,0:T(8,128)S(1)} %bitcast.13, ...), custom_call_target="tpu_custom_call" | custom-call | flops 700000000 | bytes 4194304 | tf_op jit(solution)/shard_map/pallas_call | solution.py:325
  22.3 0.4 shard_map.53
  22.8 0.6 %collective-permute-start.5 = (f32[224,128]{1,0:T(8,128)S(1)}, f32[224,128]{1,0:T(8,128)S(1)}, u32[]{:S(2)}, u32[]{:S(2)}) collective-permute-start(f32[224,128]{1,0:T(8,128)S(1)} %get-tuple-element.27), channel_id=1, source_target_pairs={{0,2},{2,0},{1,3},{3,1},{4,6},{6,4},{5,7},{7,5},{8,10},{10,8},{9,1... | collective-permute-start | bytes 344072 | tf_op jit(solution)/shard_map/ppermute | solution.py:19
  23.4 1.0 %collective-permute-done.5.received = f32[224,128]{1,0:T(8,128)S(1)} collective-permute-done((f32[224,128]{1,0:T(8,128)S(1)}, f32[224,128]{1,0:T(8,128)S(1)}, u32[]{:S(2)}, u32[]{:S(2)}) %collective-permute-start.5) | collective-permute-done | bytes 114720 | tf_op jit(solution)/shard_map/ppermute | solution.py:19
  24.5 0.9 %collective-permute-start.7 = (f32[56,128]{1,0:T(8,128)S(1)}, f32[56,128]{1,0:T(8,128)S(1)}, u32[]{:S(2)}, u32[]{:S(2)}) collective-permute-start(f32[56,128]{1,0:T(8,128)S(1)} %get-tuple-element.29), channel_id=1, source_target_pairs={{0,32},{4,36},{8,40},{12,44},{16,48},{20,52},{24,56},{28,60},{32,0... | collective-permute-start | bytes 86024 | tf_op jit(solution)/shard_map/ppermute | solution.py:272
  25.4 1.7 %collective-permute-start.8 = (f32[56,128]{1,0:T(8,128)S(1)}, f32[56,128]{1,0:T(8,128)S(1)}, u32[]{:S(2)}, u32[]{:S(2)}) collective-permute-start(f32[56,128]{1,0:T(8,128)S(1)} %get-tuple-element.30), channel_id=1, source_target_pairs={{0,8},{4,12},{8,0},{12,4},{16,24},{20,28},{24,16},{28,20},{32,40},... | collective-permute-start | bytes 86024 | tf_op jit(solution)/shard_map/ppermute | solution.py:272
  27.1 1.0 %collective-permute-done.6.three = f32[56,128]{1,0:T(8,128)S(1)} collective-permute-done((f32[56,128]{1,0:T(8,128)S(1)}, f32[56,128]{1,0:T(8,128)S(1)}, u32[]{:S(2)}, u32[]{:S(2)}) %collective-permute-start.6) | collective-permute-done | bytes 28704 | tf_op jit(solution)/shard_map/ppermute | solution.py:272
  28.1 0.3 collective-permute-done.8.one
  28.5 2.1 %collective-permute-start.10 = (f32[56,128]{1,0:T(8,128)S(1)}, f32[56,128]{1,0:T(8,128)S(1)}, u32[]{:S(2)}, u32[]{:S(2)}) collective-permute-start(f32[56,128]{1,0:T(8,128)S(1)} %shard_map.55.after.own), channel_id=1, source_target_pairs={{0,4},{4,0},{8,12},{12,8},{16,20},{20,16},{24,28},{28,24},{32,36},... | collective-permute-start | bytes 86024 | tf_op jit(solution)/shard_map/ppermute | solution.py:272
  30.6 3.2 %collective-permute-start.11 = (f32[56,128]{1,0:T(8,128)S(1)}, f32[56,128]{1,0:T(8,128)S(1)}, u32[]{:S(2)}, u32[]{:S(2)}) collective-permute-start(f32[56,128]{1,0:T(8,128)S(1)} %shard_map.55.after.own), channel_id=1, source_target_pairs={{0,24},{4,28},{8,16},{12,20},{16,8},{20,12},{24,0},{28,4},{32,56},... | collective-permute-start | bytes 86024 | tf_op jit(solution)/shard_map/ppermute | solution.py:272
  33.9 1.0 %collective-permute-done.9.three = f32[56,128]{1,0:T(8,128)S(1)} collective-permute-done((f32[56,128]{1,0:T(8,128)S(1)}, f32[56,128]{1,0:T(8,128)S(1)}, u32[]{:S(2)}, u32[]{:S(2)}) %collective-permute-start.9) | collective-permute-done | bytes 28704 | tf_op jit(solution)/shard_map/ppermute | solution.py:272
  34.8 0.5 collective-permute-done.11.one
  35.3 3.6 %collective-permute-start.12 = (f32[56,128]{1,0:T(8,128)S(1)}, f32[56,128]{1,0:T(8,128)S(1)}, u32[]{:S(2)}, u32[]{:S(2)}) collective-permute-start(f32[56,128]{1,0:T(8,128)S(1)} %shard_map.57.own), channel_id=1, source_target_pairs={{0,128},{4,132},{8,136},{12,140},{16,144},{20,148},{24,152},{28,15... | collective-permute-start | bytes 86024 | tf_op jit(solution)/shard_map/ppermute | solution.py:272
  39.0 1.0 %collective-permute-start.13 = (f32[56,128]{1,0:T(8,128)S(1)}, f32[56,128]{1,0:T(8,128)S(1)}, u32[]{:S(2)}, u32[]{:S(2)}) collective-permute-start(f32[56,128]{1,0:T(8,128)S(1)} %shard_map.57.own), channel_id=1, source_target_pairs={{0,192},{4,196},{8,200},{12,204},{16,208},{20,212},{24,216},{28,22... | collective-permute-start | bytes 86024 | tf_op jit(solution)/shard_map/ppermute | solution.py:272
  40.0 1.1 %collective-permute-start.14 = (f32[56,128]{1,0:T(8,128)S(1)}, f32[56,128]{1,0:T(8,128)S(1)}, u32[]{:S(2)}, u32[]{:S(2)}) collective-permute-start(f32[56,128]{1,0:T(8,128)S(1)} %shard_map.57.own), channel_id=1, source_target_pairs={{0,64},{4,68},{8,72},{12,76},{16,80},{20,84},{24,88},{28,92},{32,9... | collective-permute-start | bytes 86024 | tf_op jit(solution)/shard_map/ppermute | solution.py:272
  41.1 2.0 %shard_map.56 = (f32[512,128]{1,0:T(8,128)S(1)}, f32[512,128]{1,0:T(8,128)S(1)}) custom-call(s32[1]{0:T(128)} %bitcast.chan, s32[1]{0:T(128)} %bitcast.1.along, s32[1]{0:T(128)} %bitcast.2.across, f32[56,128]{1,0:T(8,128)S(1)} %shard_map.55.after.own, f32[27,32,64]{2,1,0:T(8,128)S(1)} %copy-done.2, f32[512,128]{1,0:T(8,128)S(1)} %bitcast.14, ...), custom_call_target="tpu_custom_call" | custom-call | flops 700000000 | bytes 4194304 | tf_op jit(solution)/shard_map/pallas_call | solution.py:332
  43.1 0.7 %collective-permute-done.13.two = f32[56,128]{1,0:T(8,128)S(1)} collective-permute-done((f32[56,128]{1,0:T(8,128)S(1)}, f32[56,128]{1,0:T(8,128)S(1)}, u32[]{:S(2)}, u32[]{:S(2)}) %collective-permute-start.13) | collective-permute-done | bytes 28704 | tf_op jit(solution)/shard_map/ppermute | solution.py:272
  43.9 1.0 %collective-permute-start.16 = (f32[56,128]{1,0:T(8,128)S(1)}, f32[56,128]{1,0:T(8,128)S(1)}, u32[]{:S(2)}, u32[]{:S(2)}) collective-permute-start(f32[56,128]{1,0:T(8,128)S(1)} %shard_map.58.after.own), channel_id=1, source_target_pairs={{0,40},{4,44},{8,32},{12,36},{16,56},{20,60},{24,48},{28,52},{32,8... | collective-permute-start | bytes 86024 | tf_op jit(solution)/shard_map/ppermute | solution.py:272
  45.1 1.5 %collective-permute-start.18 = (f32[56,128]{1,0:T(8,128)S(1)}, f32[56,128]{1,0:T(8,128)S(1)}, u32[]{:S(2)}, u32[]{:S(2)}) collective-permute-start(f32[56,128]{1,0:T(8,128)S(1)} %shard_map.58.after.own), channel_id=1, source_target_pairs={{0,8},{4,12},{8,0},{12,4},{16,24},{20,28},{24,16},{28,20},{32,40},... | collective-permute-start | bytes 86024 | tf_op jit(solution)/shard_map/ppermute | solution.py:272
  46.7 1.3 %collective-permute-done.16.three = f32[56,128]{1,0:T(8,128)S(1)} collective-permute-done((f32[56,128]{1,0:T(8,128)S(1)}, f32[56,128]{1,0:T(8,128)S(1)}, u32[]{:S(2)}, u32[]{:S(2)}) %collective-permute-start.16) | collective-permute-done | bytes 28704 | tf_op jit(solution)/shard_map/ppermute | solution.py:272
  47.9 0.3 collective-permute-done.18.one
  48.2 6.5 %collective-permute-start.19 = (f32[224,128]{1,0:T(8,128)S(1)}, f32[224,128]{1,0:T(8,128)S(1)}, u32[]{:S(2)}, u32[]{:S(2)}) collective-permute-start(f32[224,128]{1,0:T(8,128)S(1)} %shard_map.61.own), channel_id=1, source_target_pairs={{0,2},{2,0},{1,3},{3,1},{4,6},{6,4},{5,7},{7,5},{8,10},{10,8},{9,1... | collective-permute-start | bytes 344072 | tf_op jit(solution)/shard_map/ppermute | solution.py:19
  54.7 0.7 %shard_map.60 = (f32[512,128]{1,0:T(8,128)}, f32[8,128]{1,0:T(8,128)S(1)}) custom-call(f32[512,128]{1,0:T(8,128)S(1)} %get-tuple-element.32.one, f32[512,128]{1,0:T(8,128)S(1)} %collective-permute-done.15.two), custom_call_target="tpu_custom_call" | custom-call | tf_op jit(solution)/shard_map/pallas_call | solution.py:337
  55.4 0.2 collective-permute-done.19.other
  55.6 0.9 %shard_map.62 = f32[27,32,64]{2,1,0:T(8,128)} custom-call(s32[1]{0:T(128)} %bitcast.9.core, f32[224,128]{1,0:T(8,128)S(1)} %shard_map.61.own, f32[224,128]{1,0:T(8,128)S(1)} %collective-permute-done.19.other, f32[8,128]{1,0:T(8,128)S(1)} %get-tuple-element.35.after), custom_call_target="tpu_custom_call" | custom-call | tf_op jit(solution)/shard_map/pallas_call | solution.py:296
  (29 shorter events, 0.7 us)
Async XLA Ops:
  0.6 19.5 %collective-permute-start = (f32[512,128]{1,0:T(8,128)}, f32[512,128]{1,0:T(8,128)S(1)}, u32[]{:S(2)}, u32[]{:S(2)}) collective-permute-start(f32[512,128]{1,0:T(8,128)} %bitcast.15), channel_id=1, source_target_pairs={{0,1},{1,0},{2,3},{3,2},{4,5},{5,4},{6,7},{7,6},{8,9},{9,8},{10,11... | collective-permute-start | bytes 786440 | tf_op jit(solution)/shard_map/ppermute | solution.py:19
  2.8 0.9 %copy-start = (f32[32,1,4,4,128]{4,3,2,1,0:T(4,128)S(1)}, f32[32,1,4,4,128]{4,3,2,1,0:T(4,128)}, u32[]{:S(2)}) copy-start(f32[32,1,4,4,128]{4,3,2,1,0:T(4,128)} %param.4) | copy-start | bytes 786436
  3.7 11.3 %copy-start.1 = (f32[32,1,4,4,128]{4,3,2,1,0:T(4,128)S(1)}, f32[32,1,4,4,128]{4,3,2,1,0:T(4,128)}, u32[]{:S(2)}) copy-start(f32[32,1,4,4,128]{4,3,2,1,0:T(4,128)} %param.4) | copy-start | bytes 786436
  3.8 16.3 %copy-start.3 = (f32[32,1,4,4,128]{4,3,2,1,0:T(4,128)S(1)}, f32[32,1,4,4,128]{4,3,2,1,0:T(4,128)}, u32[]{:S(2)}) copy-start(f32[32,1,4,4,128]{4,3,2,1,0:T(4,128)} %param.3) | copy-start | bytes 786436
  3.8 9.8 %collective-permute-start.1 = (f32[128,128]{1,0:T(8,128)S(1)}, f32[128,128]{1,0:T(8,128)S(1)}, u32[]{:S(2)}, u32[]{:S(2)}) collective-permute-start(f32[128,128]{1,0:T(8,128)S(1)} %get-tuple-element.19), channel_id=1, source_target_pairs={{8,16},{24,32},{40,48},{56,64},{72,80},{88,96},{104,112},{120,128}... | collective-permute-start | bytes 196616 | tf_op jit(solution)/shard_map/ppermute | solution.py:19
  11.9 3.1 %collective-permute-start.2 = (f32[128,128]{1,0:T(8,128)S(1)}, f32[128,128]{1,0:T(8,128)S(1)}, u32[]{:S(2)}, u32[]{:S(2)}) collective-permute-start(f32[128,128]{1,0:T(8,128)S(1)} %get-tuple-element.20), channel_id=1, source_target_pairs={{0,8},{16,24},{32,40},{48,56},{64,72},{80,88},{96,104},{112,120},{... | collective-permute-start | bytes 196616 | tf_op jit(solution)/shard_map/ppermute | solution.py:19
  15.3 7.0 %collective-permute-start.3 = (f32[32,128]{1,0:T(8,128)S(1)}, f32[32,128]{1,0:T(8,128)S(1)}, u32[]{:S(2)}, u32[]{:S(2)}) collective-permute-start(f32[32,128]{1,0:T(8,128)S(1)} %get-tuple-element.24), channel_id=1, source_target_pairs={{2,4},{6,0},{4,2},{0,6},{3,5},{7,1},{5,3},{1,7},{10,12},{14,8},{12... | collective-permute-start | bytes 49160 | tf_op jit(solution)/shard_map/ppermute | solution.py:19
  20.1 2.2 %collective-permute-start.4 = (f32[32,128]{1,0:T(8,128)S(1)}, f32[32,128]{1,0:T(8,128)S(1)}, u32[]{:S(2)}, u32[]{:S(2)}) collective-permute-start(f32[32,128]{1,0:T(8,128)S(1)} %get-tuple-element.25), channel_id=1, source_target_pairs={{0,2},{2,0},{1,3},{3,1},{4,6},{6,4},{5,7},{7,5},{8,10},{10,8},{9,1... | collective-permute-start | bytes 49160 | tf_op jit(solution)/shard_map/ppermute | solution.py:19
  22.3 18.8 %copy-start.2 = (f32[27,32,64]{2,1,0:T(8,128)S(1)}, f32[27,32,64]{2,1,0:T(8,128)}, u32[]{:S(2)}) copy-start(f32[27,32,64]{2,1,0:T(8,128)} %weights.1) | copy-start | bytes 663556
  22.8 1.6 %collective-permute-start.5 = (f32[224,128]{1,0:T(8,128)S(1)}, f32[224,128]{1,0:T(8,128)S(1)}, u32[]{:S(2)}, u32[]{:S(2)}) collective-permute-start(f32[224,128]{1,0:T(8,128)S(1)} %get-tuple-element.27), channel_id=1, source_target_pairs={{0,2},{2,0},{1,3},{3,1},{4,6},{6,4},{5,7},{7,5},{8,10},{10,8},{9,1... | collective-permute-start | bytes 344072 | tf_op jit(solution)/shard_map/ppermute | solution.py:19
  24.4 3.7 %collective-permute-start.6 = (f32[56,128]{1,0:T(8,128)S(1)}, f32[56,128]{1,0:T(8,128)S(1)}, u32[]{:S(2)}, u32[]{:S(2)}) collective-permute-start(f32[56,128]{1,0:T(8,128)S(1)} %get-tuple-element.28), channel_id=1, source_target_pairs={{0,40},{4,44},{8,32},{12,36},{16,56},{20,60},{24,48},{28,52},{32,8... | collective-permute-start | bytes 86024 | tf_op jit(solution)/shard_map/ppermute | solution.py:272
  24.5 3.6 %collective-permute-start.7 = (f32[56,128]{1,0:T(8,128)S(1)}, f32[56,128]{1,0:T(8,128)S(1)}, u32[]{:S(2)}, u32[]{:S(2)}) collective-permute-start(f32[56,128]{1,0:T(8,128)S(1)} %get-tuple-element.29), channel_id=1, source_target_pairs={{0,32},{4,36},{8,40},{12,44},{16,48},{20,52},{24,56},{28,60},{32,0... | collective-permute-start | bytes 86024 | tf_op jit(solution)/shard_map/ppermute | solution.py:272
  25.4 3.0 %collective-permute-start.8 = (f32[56,128]{1,0:T(8,128)S(1)}, f32[56,128]{1,0:T(8,128)S(1)}, u32[]{:S(2)}, u32[]{:S(2)}) collective-permute-start(f32[56,128]{1,0:T(8,128)S(1)} %get-tuple-element.30), channel_id=1, source_target_pairs={{0,8},{4,12},{8,0},{12,4},{16,24},{20,28},{24,16},{28,20},{32,40},... | collective-permute-start | bytes 86024 | tf_op jit(solution)/shard_map/ppermute | solution.py:272
  28.4 6.4 %collective-permute-start.9 = (f32[56,128]{1,0:T(8,128)S(1)}, f32[56,128]{1,0:T(8,128)S(1)}, u32[]{:S(2)}, u32[]{:S(2)}) collective-permute-start(f32[56,128]{1,0:T(8,128)S(1)} %shard_map.55.after.own), channel_id=1, source_target_pairs={{0,28},{4,24},{8,20},{12,16},{16,12},{20,8},{24,4},{28,0},{32,60},... | collective-permute-start | bytes 86024 | tf_op jit(solution)/shard_map/ppermute | solution.py:272
  28.5 6.3 %collective-permute-start.10 = (f32[56,128]{1,0:T(8,128)S(1)}, f32[56,128]{1,0:T(8,128)S(1)}, u32[]{:S(2)}, u32[]{:S(2)}) collective-permute-start(f32[56,128]{1,0:T(8,128)S(1)} %shard_map.55.after.own), channel_id=1, source_target_pairs={{0,4},{4,0},{8,12},{12,8},{16,20},{20,16},{24,28},{28,24},{32,36},... | collective-permute-start | bytes 86024 | tf_op jit(solution)/shard_map/ppermute | solution.py:272
  30.6 4.7 %collective-permute-start.11 = (f32[56,128]{1,0:T(8,128)S(1)}, f32[56,128]{1,0:T(8,128)S(1)}, u32[]{:S(2)}, u32[]{:S(2)}) collective-permute-start(f32[56,128]{1,0:T(8,128)S(1)} %shard_map.55.after.own), channel_id=1, source_target_pairs={{0,24},{4,28},{8,16},{12,20},{16,8},{20,12},{24,0},{28,4},{32,56},... | collective-permute-start | bytes 86024 | tf_op jit(solution)/shard_map/ppermute | solution.py:272
  35.3 7.8 %collective-permute-start.12 = (f32[56,128]{1,0:T(8,128)S(1)}, f32[56,128]{1,0:T(8,128)S(1)}, u32[]{:S(2)}, u32[]{:S(2)}) collective-permute-start(f32[56,128]{1,0:T(8,128)S(1)} %shard_map.57.own), channel_id=1, source_target_pairs={{0,128},{4,132},{8,136},{12,140},{16,144},{20,148},{24,152},{28,15... | collective-permute-start | bytes 86024 | tf_op jit(solution)/shard_map/ppermute | solution.py:272
  39.0 4.8 %collective-permute-start.13 = (f32[56,128]{1,0:T(8,128)S(1)}, f32[56,128]{1,0:T(8,128)S(1)}, u32[]{:S(2)}, u32[]{:S(2)}) collective-permute-start(f32[56,128]{1,0:T(8,128)S(1)} %shard_map.57.own), channel_id=1, source_target_pairs={{0,192},{4,196},{8,200},{12,204},{16,208},{20,212},{24,216},{28,22... | collective-permute-start | bytes 86024 | tf_op jit(solution)/shard_map/ppermute | solution.py:272
  40.0 3.8 %collective-permute-start.14 = (f32[56,128]{1,0:T(8,128)S(1)}, f32[56,128]{1,0:T(8,128)S(1)}, u32[]{:S(2)}, u32[]{:S(2)}) collective-permute-start(f32[56,128]{1,0:T(8,128)S(1)} %shard_map.57.own), channel_id=1, source_target_pairs={{0,64},{4,68},{8,72},{12,76},{16,80},{20,84},{24,88},{28,92},{32,9... | collective-permute-start | bytes 86024 | tf_op jit(solution)/shard_map/ppermute | solution.py:272
  43.8 10.8 %collective-permute-start.15 = (f32[512,128]{1,0:T(8,128)S(1)}, f32[512,128]{1,0:T(8,128)S(1)}, u32[]{:S(2)}, u32[]{:S(2)}) collective-permute-start(f32[512,128]{1,0:T(8,128)S(1)} %shard_map.59), channel_id=1, source_target_pairs={{0,1},{1,0},{2,3},{3,2},{4,5},{5,4},{6,7},{7,6},{8,9},{9,8},{10,11... | collective-permute-start | bytes 786440 | tf_op jit(solution)/shard_map/ppermute | solution.py:19
  43.9 4.0 %collective-permute-start.16 = (f32[56,128]{1,0:T(8,128)S(1)}, f32[56,128]{1,0:T(8,128)S(1)}, u32[]{:S(2)}, u32[]{:S(2)}) collective-permute-start(f32[56,128]{1,0:T(8,128)S(1)} %shard_map.58.after.own), channel_id=1, source_target_pairs={{0,40},{4,44},{8,32},{12,36},{16,56},{20,60},{24,48},{28,52},{32,8... | collective-permute-start | bytes 86024 | tf_op jit(solution)/shard_map/ppermute | solution.py:272
  44.9 3.0 %collective-permute-start.17 = (f32[56,128]{1,0:T(8,128)S(1)}, f32[56,128]{1,0:T(8,128)S(1)}, u32[]{:S(2)}, u32[]{:S(2)}) collective-permute-start(f32[56,128]{1,0:T(8,128)S(1)} %shard_map.58.after.own), channel_id=1, source_target_pairs={{0,32},{4,36},{8,40},{12,44},{16,48},{20,52},{24,56},{28,60},{32,0... | collective-permute-start | bytes 86024 | tf_op jit(solution)/shard_map/ppermute | solution.py:272
  45.1 3.1 %collective-permute-start.18 = (f32[56,128]{1,0:T(8,128)S(1)}, f32[56,128]{1,0:T(8,128)S(1)}, u32[]{:S(2)}, u32[]{:S(2)}) collective-permute-start(f32[56,128]{1,0:T(8,128)S(1)} %shard_map.58.after.own), channel_id=1, source_target_pairs={{0,8},{4,12},{8,0},{12,4},{16,24},{20,28},{24,16},{28,20},{32,40},... | collective-permute-start | bytes 86024 | tf_op jit(solution)/shard_map/ppermute | solution.py:272
  48.2 7.4 %collective-permute-start.19 = (f32[224,128]{1,0:T(8,128)S(1)}, f32[224,128]{1,0:T(8,128)S(1)}, u32[]{:S(2)}, u32[]{:S(2)}) collective-permute-start(f32[224,128]{1,0:T(8,128)S(1)} %shard_map.61.own), channel_id=1, source_target_pairs={{0,2},{2,0},{1,3},{3,1},{4,6},{6,4},{5,7},{7,5},{8,10},{10,8},{9,1... | collective-permute-start | bytes 344072 | tf_op jit(solution)/shard_map/ppermute | solution.py:19

commit v7 on v6

--- a/solution.py
+++ b/solution.py
@@ -198,10 +198,6 @@
             sent[pl.ds(x * 4 + z, CI, stride=16), :] = tile[32:]
 
 
-def gate_kernel(value, after, out):
-    out[...] = value[...]
-
-
 def quarter(ref, index):
     return ref[pl.ds(pl.multiple_of(index * 56, 8), 56), :]
 
@@ -281,11 +277,9 @@
     return call(sum_kernel, small, [VMEM] * 4)(three, two, one, own)
 
 
-def summed_far(part):
-    for steps in ((7, 1, 6), (32, 48, 16)):
-        parts = [crossed(part, bits) for bits in steps]
-        part = call(sum_kernel, shape(56, 128), [VMEM] * 4)(*parts, part)
-    return part
+def summed_over(part, steps):
+    parts = [crossed(part, bits) for bits in steps]
+    return call(sum_kernel, shape(56, 128), [VMEM] * 4)(*parts, part)
 
 
 def gathered(part, done):
@@ -332,11 +326,12 @@
     kept, sent = call(
         data_kernel, (shape(512, 128),) * 2, [SMEM] * 3 + [VMEM] * 7, halves, 700_000_000, 1 << 22
     )(chan, along, across, part, kernel, grad, far_row, near_row, from_chip, from_core)
-    part = summed_far(part)
-    sent = call(gate_kernel, shape(512, 128), [VMEM] * 2)(sent, part)
+    part = summed_over(part, (7, 1, 6))
+    part, sent = lax.optimization_barrier((part, sent))
     input_grad, done = call(add_kernel, (shape(512, 128), shape(8, 128)), [VMEM] * 2)(
         kept, swapped(sent, "chan", 0)
     )
+    part = summed_over(part, (32, 48, 16))
     input_grad = input_grad.reshape(activation.shape)
     kernel_grad = gathered(part, done)
     return (input_grad, kernel_grad)

time: 56.6 us -> 56.7 us (level)
  transfers between devices with their start and end apart: 20 -> 20, of which waited for: 11 -> 10; matrix products, arithmetic and copies ran while one was open for 0% -> 0% of each run, Pallas kernels for 9% -> 9%
where the time goes in v7:
time: 56.7 us; the launch traced here: 56.6 us
  starting transfers between devices  38.9 us (69%)
  waiting for transfers between devices  9.29 us (16%)
  Pallas kernels  6.68 us (12%)
  local copies, waits for them, and re-layouts  0.97 us (2%)
  between operations  0.77 us (1%)
    ppermute x8, starting transfers between devices, swapped(): return lax.ppermute(value, axis, pairs + [(t, s) for s, t in pairs])  22 us
    ppermute x12, starting transfers between devices, crossed(): lax.ppermute(value, axis, [(s, s ^ bits) for s in range(lax.axis_size(axi...  16.8 us
    ppermute x12, waiting for transfers between devices, crossed(): lax.ppermute(value, axis, [(s, s ^ bits) for s in range(lax.axis_size(axi...  4.97 us
    ppermute x8, waiting for transfers between devices, swapped(): return lax.ppermute(value, axis, pairs + [(t, s) for s, t in pairs])  4.32 us
    pallas_call x1, Pallas kernels, body(): call(filter_kernel, (shape(864, 64), column, column), [SMEM] * 2 + [VMEM]...  2.22 us
    pallas_call x1, Pallas kernels, body(): call(data_kernel, (shape(512, 128),) * 2, [SMEM] * 3 + [VMEM] * 7, halves...  2.03 us
  transfers between devices with their start and end apart: 20, of which 10 were waited for; matrix products, arithmetic and copies ran while one was open for 0% of the time, Pallas kernels for 9%

profile of v7, /device:TPU:1, one launch (start us, length us, event | category | flops | bytes accessed | tf_op | source)
XLA Modules:
  0.0 56.6 jit_solution(14220688544535881766)
XLA Ops:
  0.6 2.1 %collective-permute-start = (f32[512,128]{1,0:T(8,128)}, f32[512,128]{1,0:T(8,128)S(1)}, u32[]{:S(2)}, u32[]{:S(2)}) collective-permute-start(f32[512,128]{1,0:T(8,128)} %bitcast.15), channel_id=1, source_target_pairs={{0,1},{1,0},{2,3},{3,2},{4,5},{5,4},{6,7},{7,6},{8,9},{9,8},{10,11... | collective-permute-start | bytes 786440 | tf_op jit(solution)/shard_map/ppermute | solution.py:19
  2.8 0.9 %copy-done = f32[32,1,4,4,128]{4,3,2,1,0:T(4,128)S(1)} copy-done((f32[32,1,4,4,128]{4,3,2,1,0:T(4,128)S(1)}, f32[32,1,4,4,128]{4,3,2,1,0:T(4,128)}, u32[]{:S(2)}) %copy-start) | copy-done | bytes 262168
  3.8 8.1 %collective-permute-start.1 = (f32[128,128]{1,0:T(8,128)S(1)}, f32[128,128]{1,0:T(8,128)S(1)}, u32[]{:S(2)}, u32[]{:S(2)}) collective-permute-start(f32[128,128]{1,0:T(8,128)S(1)} %get-tuple-element.21), channel_id=1, source_target_pairs={{8,16},{24,32},{40,48},{56,64},{72,80},{88,96},{104,112},{120,128}... | collective-permute-start | bytes 196616 | tf_op jit(solution)/shard_map/ppermute | solution.py:19
  11.9 1.7 %collective-permute-done.1.far_row = f32[128,128]{1,0:T(8,128)S(1)} collective-permute-done((f32[128,128]{1,0:T(8,128)S(1)}, f32[128,128]{1,0:T(8,128)S(1)}, u32[]{:S(2)}, u32[]{:S(2)}) %collective-permute-start.1) | collective-permute-done | bytes 65568 | tf_op jit(solution)/shard_map/ppermute | solution.py:19
  13.5 1.5 %collective-permute-done.2.near_row = f32[128,128]{1,0:T(8,128)S(1)} collective-permute-done((f32[128,128]{1,0:T(8,128)S(1)}, f32[128,128]{1,0:T(8,128)S(1)}, u32[]{:S(2)}, u32[]{:S(2)}) %collective-permute-start.2) | collective-permute-done | bytes 65568 | tf_op jit(solution)/shard_map/ppermute | solution.py:19
  15.0 0.3 shard_map.52
  15.3 4.8 %collective-permute-start.3 = (f32[32,128]{1,0:T(8,128)S(1)}, f32[32,128]{1,0:T(8,128)S(1)}, u32[]{:S(2)}, u32[]{:S(2)}) collective-permute-start(f32[32,128]{1,0:T(8,128)S(1)} %get-tuple-element.26), channel_id=1, source_target_pairs={{2,4},{6,0},{4,2},{0,6},{3,5},{7,1},{5,3},{1,7},{10,12},{14,8},{12... | collective-permute-start | bytes 49160 | tf_op jit(solution)/shard_map/ppermute | solution.py:19
  20.1 2.2 %shard_map.51 = (f32[864,64]{1,0:T(8,128)S(1)}, f32[64,128]{1,0:T(8,128)S(1)}, f32[64,128]{1,0:T(8,128)S(1)}) custom-call(s32[1]{0:T(128)} %bitcast.chan, s32[1]{0:T(128)} %bitcast.1.along, f32[512,128]{1,0:T(8,128)S(1)} %bitcast.16, f32[512,128]{1,0:T(8,128)S(1)} %collective-permute-done.other, f32[512,128]{1,0:T(8,128)S(1)} %bitcast.13, ...), custom_call_target="tpu_custom_call" | custom-call | flops 700000000 | bytes 4194304 | tf_op jit(solution)/shard_map/pallas_call | solution.py:319
  22.3 0.4 shard_map.53
  22.8 0.6 %collective-permute-start.5 = (f32[224,128]{1,0:T(8,128)S(1)}, f32[224,128]{1,0:T(8,128)S(1)}, u32[]{:S(2)}, u32[]{:S(2)}) collective-permute-start(f32[224,128]{1,0:T(8,128)S(1)} %get-tuple-element.29), channel_id=1, source_target_pairs={{0,2},{2,0},{1,3},{3,1},{4,6},{6,4},{5,7},{7,5},{8,10},{10,8},{9,1... | collective-permute-start | bytes 344072 | tf_op jit(solution)/shard_map/ppermute | solution.py:19
  23.4 1.0 %collective-permute-done.5.received = f32[224,128]{1,0:T(8,128)S(1)} collective-permute-done((f32[224,128]{1,0:T(8,128)S(1)}, f32[224,128]{1,0:T(8,128)S(1)}, u32[]{:S(2)}, u32[]{:S(2)}) %collective-permute-start.5) | collective-permute-done | bytes 114720 | tf_op jit(solution)/shard_map/ppermute | solution.py:19
  24.5 0.9 %collective-permute-start.7 = (f32[56,128]{1,0:T(8,128)S(1)}, f32[56,128]{1,0:T(8,128)S(1)}, u32[]{:S(2)}, u32[]{:S(2)}) collective-permute-start(f32[56,128]{1,0:T(8,128)S(1)} %get-tuple-element.31), channel_id=1, source_target_pairs={{0,32},{4,36},{8,40},{12,44},{16,48},{20,52},{24,56},{28,60},{32,0... | collective-permute-start | bytes 86024 | tf_op jit(solution)/shard_map/ppermute | solution.py:268
  25.4 1.7 %collective-permute-start.8 = (f32[56,128]{1,0:T(8,128)S(1)}, f32[56,128]{1,0:T(8,128)S(1)}, u32[]{:S(2)}, u32[]{:S(2)}) collective-permute-start(f32[56,128]{1,0:T(8,128)S(1)} %get-tuple-element.32), channel_id=1, source_target_pairs={{0,8},{4,12},{8,0},{12,4},{16,24},{20,28},{24,16},{28,20},{32,40},... | collective-permute-start | bytes 86024 | tf_op jit(solution)/shard_map/ppermute | solution.py:268
  27.1 1.0 %collective-permute-done.6.three = f32[56,128]{1,0:T(8,128)S(1)} collective-permute-done((f32[56,128]{1,0:T(8,128)S(1)}, f32[56,128]{1,0:T(8,128)S(1)}, u32[]{:S(2)}, u32[]{:S(2)}) %collective-permute-start.6) | collective-permute-done | bytes 28704 | tf_op jit(solution)/shard_map/ppermute | solution.py:268
  28.1 0.3 collective-permute-done.8.one
  28.5 2.1 %collective-permute-start.10 = (f32[56,128]{1,0:T(8,128)S(1)}, f32[56,128]{1,0:T(8,128)S(1)}, u32[]{:S(2)}, u32[]{:S(2)}) collective-permute-start(f32[56,128]{1,0:T(8,128)S(1)} %shard_map.55.after.own), channel_id=1, source_target_pairs={{0,4},{4,0},{8,12},{12,8},{16,20},{20,16},{24,28},{28,24},{32,36},... | collective-permute-start | bytes 86024 | tf_op jit(solution)/shard_map/ppermute | solution.py:268
  30.6 3.2 %collective-permute-start.11 = (f32[56,128]{1,0:T(8,128)S(1)}, f32[56,128]{1,0:T(8,128)S(1)}, u32[]{:S(2)}, u32[]{:S(2)}) collective-permute-start(f32[56,128]{1,0:T(8,128)S(1)} %shard_map.55.after.own), channel_id=1, source_target_pairs={{0,24},{4,28},{8,16},{12,20},{16,8},{20,12},{24,0},{28,4},{32,56},... | collective-permute-start | bytes 86024 | tf_op jit(solution)/shard_map/ppermute | solution.py:268
  33.9 2.0 %shard_map.56 = (f32[512,128]{1,0:T(8,128)S(1)}, f32[512,128]{1,0:T(8,128)S(1)}) custom-call(s32[1]{0:T(128)} %bitcast.chan, s32[1]{0:T(128)} %bitcast.1.along, s32[1]{0:T(128)} %bitcast.2.across, f32[56,128]{1,0:T(8,128)S(1)} %shard_map.55.after.own, f32[27,32,64]{2,1,0:T(8,128)S(1)} %copy-done.2, f32[512,128]{1,0:T(8,128)S(1)} %bitcast.14, ...), custom_call_target="tpu_custom_call" | custom-call | flops 700000000 | bytes 4194304 | tf_op jit(solution)/shard_map/pallas_call | solution.py:326
  36.0 3.2 %collective-permute-start.13 = (f32[56,128]{1,0:T(8,128)S(1)}, f32[56,128]{1,0:T(8,128)S(1)}, u32[]{:S(2)}, u32[]{:S(2)}) collective-permute-start(f32[56,128]{1,0:T(8,128)S(1)} %shard_map.57.own), channel_id=1, source_target_pairs={{0,128},{4,132},{8,136},{12,140},{16,144},{20,148},{24,152},{28,15... | collective-permute-start | bytes 86024 | tf_op jit(solution)/shard_map/ppermute | solution.py:268
  39.2 1.0 %collective-permute-start.14 = (f32[56,128]{1,0:T(8,128)S(1)}, f32[56,128]{1,0:T(8,128)S(1)}, u32[]{:S(2)}, u32[]{:S(2)}) collective-permute-start(f32[56,128]{1,0:T(8,128)S(1)} %shard_map.57.own), channel_id=1, source_target_pairs={{0,192},{4,196},{8,200},{12,204},{16,208},{20,212},{24,216},{28,22... | collective-permute-start | bytes 86024 | tf_op jit(solution)/shard_map/ppermute | solution.py:268
  40.2 1.7 %collective-permute-start.15 = (f32[56,128]{1,0:T(8,128)S(1)}, f32[56,128]{1,0:T(8,128)S(1)}, u32[]{:S(2)}, u32[]{:S(2)}) collective-permute-start(f32[56,128]{1,0:T(8,128)S(1)} %shard_map.57.own), channel_id=1, source_target_pairs={{0,64},{4,68},{8,72},{12,76},{16,80},{20,84},{24,88},{28,92},{32,9... | collective-permute-start | bytes 86024 | tf_op jit(solution)/shard_map/ppermute | solution.py:268
  42.0 1.0 %collective-permute-done.13.three = f32[56,128]{1,0:T(8,128)S(1)} collective-permute-done((f32[56,128]{1,0:T(8,128)S(1)}, f32[56,128]{1,0:T(8,128)S(1)}, u32[]{:S(2)}, u32[]{:S(2)}) %collective-permute-start.13) | collective-permute-done | bytes 28704 | tf_op jit(solution)/shard_map/ppermute | solution.py:268
  42.9 1.1 %collective-permute-done.14.two = f32[56,128]{1,0:T(8,128)S(1)} collective-permute-done((f32[56,128]{1,0:T(8,128)S(1)}, f32[56,128]{1,0:T(8,128)S(1)}, u32[]{:S(2)}, u32[]{:S(2)}) %collective-permute-start.14) | collective-permute-done | bytes 28704 | tf_op jit(solution)/shard_map/ppermute | solution.py:268
  44.1 1.0 %collective-permute-start.16 = (f32[56,128]{1,0:T(8,128)S(1)}, f32[56,128]{1,0:T(8,128)S(1)}, u32[]{:S(2)}, u32[]{:S(2)}) collective-permute-start(f32[56,128]{1,0:T(8,128)S(1)} %shard_map.59.own), channel_id=1, source_target_pairs={{0,40},{4,44},{8,32},{12,36},{16,56},{20,60},{24,48},{28,52},{32,8... | collective-permute-start | bytes 86024 | tf_op jit(solution)/shard_map/ppermute | solution.py:268
  45.1 0.2 collective-permute-start.17
  45.2 1.6 %collective-permute-start.18 = (f32[56,128]{1,0:T(8,128)S(1)}, f32[56,128]{1,0:T(8,128)S(1)}, u32[]{:S(2)}, u32[]{:S(2)}) collective-permute-start(f32[56,128]{1,0:T(8,128)S(1)} %shard_map.59.own), channel_id=1, source_target_pairs={{0,8},{4,12},{8,0},{12,4},{16,24},{20,28},{24,16},{28,20},{32,40},... | collective-permute-start | bytes 86024 | tf_op jit(solution)/shard_map/ppermute | solution.py:268
  46.8 1.3 %collective-permute-done.16.three = f32[56,128]{1,0:T(8,128)S(1)} collective-permute-done((f32[56,128]{1,0:T(8,128)S(1)}, f32[56,128]{1,0:T(8,128)S(1)}, u32[]{:S(2)}, u32[]{:S(2)}) %collective-permute-start.16) | collective-permute-done | bytes 28704 | tf_op jit(solution)/shard_map/ppermute | solution.py:268
  48.1 0.3 collective-permute-done.18.one
  48.4 6.3 %collective-permute-start.19 = (f32[224,128]{1,0:T(8,128)S(1)}, f32[224,128]{1,0:T(8,128)S(1)}, u32[]{:S(2)}, u32[]{:S(2)}) collective-permute-start(f32[224,128]{1,0:T(8,128)S(1)} %shard_map.60.own), channel_id=1, source_target_pairs={{0,2},{2,0},{1,3},{3,1},{4,6},{6,4},{5,7},{7,5},{8,10},{10,8},{9,1... | collective-permute-start | bytes 344072 | tf_op jit(solution)/shard_map/ppermute | solution.py:19
  54.7 0.7 %shard_map.58 = (f32[512,128]{1,0:T(8,128)}, f32[8,128]{1,0:T(8,128)S(1)}) custom-call(f32[512,128]{1,0:T(8,128)S(1)} %get-tuple-element.34.one, f32[512,128]{1,0:T(8,128)S(1)} %collective-permute-done.12.two), custom_call_target="tpu_custom_call" | custom-call | tf_op jit(solution)/shard_map/pallas_call | solution.py:331
  55.4 0.2 collective-permute-done.19.other
  55.7 0.9 %shard_map.61 = f32[27,32,64]{2,1,0:T(8,128)} custom-call(s32[1]{0:T(128)} %bitcast.9.core, f32[224,128]{1,0:T(8,128)S(1)} %shard_map.60.own, f32[224,128]{1,0:T(8,128)S(1)} %collective-permute-done.19.other, f32[8,128]{1,0:T(8,128)S(1)} %get-tuple-element.39.after), custom_call_target="tpu_custom_call" | custom-call | tf_op jit(solution)/shard_map/pallas_call | solution.py:290
  (28 shorter events, 0.4 us)
Async XLA Ops:
  0.6 19.5 %collective-permute-start = (f32[512,128]{1,0:T(8,128)}, f32[512,128]{1,0:T(8,128)S(1)}, u32[]{:S(2)}, u32[]{:S(2)}) collective-permute-start(f32[512,128]{1,0:T(8,128)} %bitcast.15), channel_id=1, source_target_pairs={{0,1},{1,0},{2,3},{3,2},{4,5},{5,4},{6,7},{7,6},{8,9},{9,8},{10,11... | collective-permute-start | bytes 786440 | tf_op jit(solution)/shard_map/ppermute | solution.py:19
  2.8 0.9 %copy-start = (f32[32,1,4,4,128]{4,3,2,1,0:T(4,128)S(1)}, f32[32,1,4,4,128]{4,3,2,1,0:T(4,128)}, u32[]{:S(2)}) copy-start(f32[32,1,4,4,128]{4,3,2,1,0:T(4,128)} %param.4) | copy-start | bytes 786436
  3.7 11.3 %copy-start.1 = (f32[32,1,4,4,128]{4,3,2,1,0:T(4,128)S(1)}, f32[32,1,4,4,128]{4,3,2,1,0:T(4,128)}, u32[]{:S(2)}) copy-start(f32[32,1,4,4,128]{4,3,2,1,0:T(4,128)} %param.4) | copy-start | bytes 786436
  3.8 16.3 %copy-start.3 = (f32[32,1,4,4,128]{4,3,2,1,0:T(4,128)S(1)}, f32[32,1,4,4,128]{4,3,2,1,0:T(4,128)}, u32[]{:S(2)}) copy-start(f32[32,1,4,4,128]{4,3,2,1,0:T(4,128)} %param.3) | copy-start | bytes 786436
  3.8 9.8 %collective-permute-start.1 = (f32[128,128]{1,0:T(8,128)S(1)}, f32[128,128]{1,0:T(8,128)S(1)}, u32[]{:S(2)}, u32[]{:S(2)}) collective-permute-start(f32[128,128]{1,0:T(8,128)S(1)} %get-tuple-element.21), channel_id=1, source_target_pairs={{8,16},{24,32},{40,48},{56,64},{72,80},{88,96},{104,112},{120,128}... | collective-permute-start | bytes 196616 | tf_op jit(solution)/shard_map/ppermute | solution.py:19
  11.9 3.1 %collective-permute-start.2 = (f32[128,128]{1,0:T(8,128)S(1)}, f32[128,128]{1,0:T(8,128)S(1)}, u32[]{:S(2)}, u32[]{:S(2)}) collective-permute-start(f32[128,128]{1,0:T(8,128)S(1)} %get-tuple-element.22), channel_id=1, source_target_pairs={{0,8},{16,24},{32,40},{48,56},{64,72},{80,88},{96,104},{112,120},{... | collective-permute-start | bytes 196616 | tf_op jit(solution)/shard_map/ppermute | solution.py:19
  15.3 7.0 %collective-permute-start.3 = (f32[32,128]{1,0:T(8,128)S(1)}, f32[32,128]{1,0:T(8,128)S(1)}, u32[]{:S(2)}, u32[]{:S(2)}) collective-permute-start(f32[32,128]{1,0:T(8,128)S(1)} %get-tuple-element.26), channel_id=1, source_target_pairs={{2,4},{6,0},{4,2},{0,6},{3,5},{7,1},{5,3},{1,7},{10,12},{14,8},{12... | collective-permute-start | bytes 49160 | tf_op jit(solution)/shard_map/ppermute | solution.py:19
  20.1 2.2 %collective-permute-start.4 = (f32[32,128]{1,0:T(8,128)S(1)}, f32[32,128]{1,0:T(8,128)S(1)}, u32[]{:S(2)}, u32[]{:S(2)}) collective-permute-start(f32[32,128]{1,0:T(8,128)S(1)} %get-tuple-element.27), channel_id=1, source_target_pairs={{0,2},{2,0},{1,3},{3,1},{4,6},{6,4},{5,7},{7,5},{8,10},{10,8},{9,1... | collective-permute-start | bytes 49160 | tf_op jit(solution)/shard_map/ppermute | solution.py:19
  22.3 11.5 %copy-start.2 = (f32[27,32,64]{2,1,0:T(8,128)S(1)}, f32[27,32,64]{2,1,0:T(8,128)}, u32[]{:S(2)}) copy-start(f32[27,32,64]{2,1,0:T(8,128)} %weights.1) | copy-start | bytes 663556
  22.8 1.6 %collective-permute-start.5 = (f32[224,128]{1,0:T(8,128)S(1)}, f32[224,128]{1,0:T(8,128)S(1)}, u32[]{:S(2)}, u32[]{:S(2)}) collective-permute-start(f32[224,128]{1,0:T(8,128)S(1)} %get-tuple-element.29), channel_id=1, source_target_pairs={{0,2},{2,0},{1,3},{3,1},{4,6},{6,4},{5,7},{7,5},{8,10},{10,8},{9,1... | collective-permute-start | bytes 344072 | tf_op jit(solution)/shard_map/ppermute | solution.py:19
  24.4 3.7 %collective-permute-start.6 = (f32[56,128]{1,0:T(8,128)S(1)}, f32[56,128]{1,0:T(8,128)S(1)}, u32[]{:S(2)}, u32[]{:S(2)}) collective-permute-start(f32[56,128]{1,0:T(8,128)S(1)} %get-tuple-element.30), channel_id=1, source_target_pairs={{0,40},{4,44},{8,32},{12,36},{16,56},{20,60},{24,48},{28,52},{32,8... | collective-permute-start | bytes 86024 | tf_op jit(solution)/shard_map/ppermute | solution.py:268
  24.5 3.6 %collective-permute-start.7 = (f32[56,128]{1,0:T(8,128)S(1)}, f32[56,128]{1,0:T(8,128)S(1)}, u32[]{:S(2)}, u32[]{:S(2)}) collective-permute-start(f32[56,128]{1,0:T(8,128)S(1)} %get-tuple-element.31), channel_id=1, source_target_pairs={{0,32},{4,36},{8,40},{12,44},{16,48},{20,52},{24,56},{28,60},{32,0... | collective-permute-start | bytes 86024 | tf_op jit(solution)/shard_map/ppermute | solution.py:268
  25.4 3.0 %collective-permute-start.8 = (f32[56,128]{1,0:T(8,128)S(1)}, f32[56,128]{1,0:T(8,128)S(1)}, u32[]{:S(2)}, u32[]{:S(2)}) collective-permute-start(f32[56,128]{1,0:T(8,128)S(1)} %get-tuple-element.32), channel_id=1, source_target_pairs={{0,8},{4,12},{8,0},{12,4},{16,24},{20,28},{24,16},{28,20},{32,40},... | collective-permute-start | bytes 86024 | tf_op jit(solution)/shard_map/ppermute | solution.py:268
  28.4 7.5 %collective-permute-start.9 = (f32[56,128]{1,0:T(8,128)S(1)}, f32[56,128]{1,0:T(8,128)S(1)}, u32[]{:S(2)}, u32[]{:S(2)}) collective-permute-start(f32[56,128]{1,0:T(8,128)S(1)} %shard_map.55.after.own), channel_id=1, source_target_pairs={{0,28},{4,24},{8,20},{12,16},{16,12},{20,8},{24,4},{28,0},{32,60},... | collective-permute-start | bytes 86024 | tf_op jit(solution)/shard_map/ppermute | solution.py:268
  28.5 7.4 %collective-permute-start.10 = (f32[56,128]{1,0:T(8,128)S(1)}, f32[56,128]{1,0:T(8,128)S(1)}, u32[]{:S(2)}, u32[]{:S(2)}) collective-permute-start(f32[56,128]{1,0:T(8,128)S(1)} %shard_map.55.after.own), channel_id=1, source_target_pairs={{0,4},{4,0},{8,12},{12,8},{16,20},{20,16},{24,28},{28,24},{32,36},... | collective-permute-start | bytes 86024 | tf_op jit(solution)/shard_map/ppermute | solution.py:268
  30.6 5.3 %collective-permute-start.11 = (f32[56,128]{1,0:T(8,128)S(1)}, f32[56,128]{1,0:T(8,128)S(1)}, u32[]{:S(2)}, u32[]{:S(2)}) collective-permute-start(f32[56,128]{1,0:T(8,128)S(1)} %shard_map.55.after.own), channel_id=1, source_target_pairs={{0,24},{4,28},{8,16},{12,20},{16,8},{20,12},{24,0},{28,4},{32,56},... | collective-permute-start | bytes 86024 | tf_op jit(solution)/shard_map/ppermute | solution.py:268
  35.9 18.8 %collective-permute-start.12 = (f32[512,128]{1,0:T(8,128)S(1)}, f32[512,128]{1,0:T(8,128)S(1)}, u32[]{:S(2)}, u32[]{:S(2)}) collective-permute-start(f32[512,128]{1,0:T(8,128)S(1)} %get-tuple-element.36), channel_id=1, source_target_pairs={{0,1},{1,0},{2,3},{3,2},{4,5},{5,4},{6,7},{7,6},{8,9},{9,8},{10,11... | collective-permute-start | bytes 786440 | tf_op jit(solution)/shard_map/ppermute | solution.py:19
  36.0 6.9 %collective-permute-start.13 = (f32[56,128]{1,0:T(8,128)S(1)}, f32[56,128]{1,0:T(8,128)S(1)}, u32[]{:S(2)}, u32[]{:S(2)}) collective-permute-start(f32[56,128]{1,0:T(8,128)S(1)} %shard_map.57.own), channel_id=1, source_target_pairs={{0,128},{4,132},{8,136},{12,140},{16,144},{20,148},{24,152},{28,15... | collective-permute-start | bytes 86024 | tf_op jit(solution)/shard_map/ppermute | solution.py:268
  39.2 4.8 %collective-permute-start.14 = (f32[56,128]{1,0:T(8,128)S(1)}, f32[56,128]{1,0:T(8,128)S(1)}, u32[]{:S(2)}, u32[]{:S(2)}) collective-permute-start(f32[56,128]{1,0:T(8,128)S(1)} %shard_map.57.own), channel_id=1, source_target_pairs={{0,192},{4,196},{8,200},{12,204},{16,208},{20,212},{24,216},{28,22... | collective-permute-start | bytes 86024 | tf_op jit(solution)/shard_map/ppermute | solution.py:268
  40.2 3.8 %collective-permute-start.15 = (f32[56,128]{1,0:T(8,128)S(1)}, f32[56,128]{1,0:T(8,128)S(1)}, u32[]{:S(2)}, u32[]{:S(2)}) collective-permute-start(f32[56,128]{1,0:T(8,128)S(1)} %shard_map.57.own), channel_id=1, source_target_pairs={{0,64},{4,68},{8,72},{12,76},{16,80},{20,84},{24,88},{28,92},{32,9... | collective-permute-start | bytes 86024 | tf_op jit(solution)/shard_map/ppermute | solution.py:268
  44.1 4.0 %collective-permute-start.16 = (f32[56,128]{1,0:T(8,128)S(1)}, f32[56,128]{1,0:T(8,128)S(1)}, u32[]{:S(2)}, u32[]{:S(2)}) collective-permute-start(f32[56,128]{1,0:T(8,128)S(1)} %shard_map.59.own), channel_id=1, source_target_pairs={{0,40},{4,44},{8,32},{12,36},{16,56},{20,60},{24,48},{28,52},{32,8... | collective-permute-start | bytes 86024 | tf_op jit(solution)/shard_map/ppermute | solution.py:268
  45.1 3.0 %collective-permute-start.17 = (f32[56,128]{1,0:T(8,128)S(1)}, f32[56,128]{1,0:T(8,128)S(1)}, u32[]{:S(2)}, u32[]{:S(2)}) collective-permute-start(f32[56,128]{1,0:T(8,128)S(1)} %shard_map.59.own), channel_id=1, source_target_pairs={{0,32},{4,36},{8,40},{12,44},{16,48},{20,52},{24,56},{28,60},{32,0... | collective-permute-start | bytes 86024 | tf_op jit(solution)/shard_map/ppermute | solution.py:268
  45.2 3.2 %collective-permute-start.18 = (f32[56,128]{1,0:T(8,128)S(1)}, f32[56,128]{1,0:T(8,128)S(1)}, u32[]{:S(2)}, u32[]{:S(2)}) collective-permute-start(f32[56,128]{1,0:T(8,128)S(1)} %shard_map.59.own), channel_id=1, source_target_pairs={{0,8},{4,12},{8,0},{12,4},{16,24},{20,28},{24,16},{28,20},{32,40},... | collective-permute-start | bytes 86024 | tf_op jit(solution)/shard_map/ppermute | solution.py:268
  48.4 7.3 %collective-permute-start.19 = (f32[224,128]{1,0:T(8,128)S(1)}, f32[224,128]{1,0:T(8,128)S(1)}, u32[]{:S(2)}, u32[]{:S(2)}) collective-permute-start(f32[224,128]{1,0:T(8,128)S(1)} %shard_map.60.own), channel_id=1, source_target_pairs={{0,2},{2,0},{1,3},{3,1},{4,6},{6,4},{5,7},{7,5},{8,10},{10,8},{9,1... | collective-permute-start | bytes 344072 | tf_op jit(solution)/shard_map/ppermute | solution.py:19
